TPU v7x, 32 devices: a whole 2x2x4 slice. The times are simulated.
32 devices in a mesh: seq: 4 (over y, x), exp: 4 (over z), fsdp: 2 (over core).
Axes of the slice: x: 2, y: 2, z: 4, core: 2. Of those that a mesh axis runs over, the one named last changes fastest.
Arguments:
- tokens: bfloat16 [8, 1024, 2048], P(('exp', 'fsdp'), 'seq')
- cotangent: bfloat16 [8, 1024, 2048], P(('exp', 'fsdp'), 'seq'), may hold values from -6 to 6
- expert_ids: int32 [8, 1024, 8], P(('exp', 'fsdp'), 'seq'), may hold values from 0 to 15, all different within a row; in each aligned block of 256 rows (0 to 255, 256 to 511, ..., all dimensions but the last counted through in order) at most 144 rows name the same one
- segment_ids: int32 [8, 1024], P(('exp', 'fsdp')), may hold values from 0 to 6, as said below
- norm_gains: bfloat16 [2048, 4], P(('seq', 'exp', 'fsdp')), may hold values from 0.099609375 to 1.8984375
- w_qkv: bfloat16 [2048, 6144], P(('seq', 'exp', 'fsdp')), may hold values from -0.125 to 0.125
- w_out: bfloat16 [2048, 2048], P(('seq', 'exp', 'fsdp')), may hold values from -1 to 1
- router: bfloat16 [2048, 16], P(('seq', 'exp', 'fsdp')), may hold values from -0.0625 to 0.0625
- expert_in: bfloat16 [2048, 16, 2048], P(('seq', 'fsdp'), 'exp'), may hold values from -0.125 to 0.125
- expert_out: bfloat16 [2048, 16, 1024], P(('seq', 'fsdp'), 'exp'), may hold values from -1.5 to 1.5
Outputs:
- output: bfloat16 [8, 1024, 2048], P(('exp', 'fsdp'), 'seq')
- grad_tokens: float32 [8, 1024, 2048], P(('exp', 'fsdp'), 'seq')
- grad_norm_gains: float32 [2048, 4], P(('seq', 'exp', 'fsdp'))
- grad_w_qkv: float32 [2048, 6144], P(('seq', 'exp', 'fsdp'))
- grad_w_out: float32 [2048, 2048], P(('seq', 'exp', 'fsdp'))
- grad_router: float32 [2048, 16], P(('seq', 'exp', 'fsdp'))
- grad_expert_in: float32 [2048, 16, 2048], P(('seq', 'fsdp'), 'exp')
- grad_expert_out: float32 [2048, 16, 1024], P(('seq', 'fsdp'), 'exp')
Inputs may be any that keep to these rules, and one draw needn't show every extreme that they name: `expert_ids`: each token's 8 ids differ. Among the tokens of one device (aligned blocks of 256 positions) no id appears more than 144 times, and in some blocks one appears exactly 144 times. `segment_ids`: Non-decreasing along each sequence, starting at 0; every sequence holds exactly seven documents.
All inputs are finite; a program needn't handle non-finite values.
Results may differ from a plain program's by a relative error of at most 0.018.
Values may be sent and summed in bfloat16 or wider, within the bound.
No kernel may reach another device: no remote copies, remote signals or barrier semaphores. Data moves between devices by JAX's collectives and lax.ppermute only.
A program may use at most 448 MiB of HBM per device.

v0:
```python
import jax
import jax.numpy as jnp
from jax import lax
from jax.sharding import PartitionSpec as P

HEADS = 16
HEAD_DIM = 128
FF = 1024
TOP = 8
ATT_BLOCK = 256


epsilon = 1e-05
rotary_base = 10000.0
highest = lax.Precision.HIGHEST


def rms_parts(values, gain_vector):
    inverse = lax.rsqrt(jnp.mean(values * values, axis=-1, keepdims=True) + epsilon)
    return (values * inverse * gain_vector, inverse)


def rms_back(gradient, values, inverse, gain_vector):
    scaled = gradient * gain_vector
    gain_grad = jnp.sum(gradient * values * inverse, axis=0)
    value_grad = inverse * scaled - values * inverse**3 * jnp.mean(
        scaled * values, axis=-1, keepdims=True
    )
    return (value_grad, gain_grad)


def rotary_tables(position, head_dim):
    half_dim = head_dim // 2
    exponent = jnp.arange(half_dim, dtype=jnp.float32) * (2.0 / head_dim)
    angles = position.astype(jnp.float32)[:, None] * (rotary_base ** (-exponent))[None, :]
    return (jnp.cos(angles)[:, None, :], jnp.sin(angles)[:, None, :])


def rotate(values, cosine, sine_part):
    half_dim = values.shape[-1] // 2
    first_half = values[..., :half_dim]
    second_half = values[..., half_dim:]
    return jnp.concatenate(
        [
            first_half * cosine - second_half * sine_part,
            second_half * cosine + first_half * sine_part,
        ],
        axis=-1,
    )


def rotate_back(gradient, cosine, sine_part):
    half_dim = gradient.shape[-1] // 2
    first_half = gradient[..., :half_dim]
    second_half = gradient[..., half_dim:]
    return jnp.concatenate(
        [
            first_half * cosine + second_half * sine_part,
            second_half * cosine - first_half * sine_part,
        ],
        axis=-1,
    )


def allowed_mask(segment, offset, block_rows):
    length = segment.shape[0]
    key_block = jnp.arange(length, dtype=jnp.int32) // ATT_BLOCK
    query_pos = offset + jnp.arange(block_rows, dtype=jnp.int32)
    query_seg = lax.dynamic_slice_in_dim(segment, offset, block_rows, 0)
    return (query_seg[:, None] == segment[None, :]) & (
        key_block[None, :] <= (query_pos // ATT_BLOCK)[:, None]
    )


def attend_heads(segment, head_group):
    head_block = head_group[:, 0]
    head_dim = head_block.shape[2] // 3
    length = head_block.shape[0]
    heads_here = head_block.shape[1]
    block_rows = min(512, length)
    queries = head_block[:, :, :head_dim]
    keys_all = head_block[:, :, head_dim : 2 * head_dim]
    values_all = head_block[:, :, 2 * head_dim :]
    scale_factor = head_dim ** (-0.5)

    def one_block(offset):
        query_rows = lax.dynamic_slice_in_dim(queries, offset, block_rows, 0)
        scores = (
            jnp.einsum("qhd,khd->hqk", query_rows, keys_all, preferred_element_type=jnp.float32)
            * scale_factor
        )
        scores = jnp.where(allowed_mask(segment, offset, block_rows)[None], scores, -jnp.inf)
        highest_score = jnp.max(scores, axis=-1, keepdims=True)
        exponent_terms = jnp.exp(scores - highest_score)
        totals = jnp.sum(exponent_terms, axis=-1, keepdims=True)
        weights = (exponent_terms / totals).astype(jnp.bfloat16)
        output = jnp.einsum("hqk,khd->qhd", weights, values_all, preferred_element_type=jnp.float32)
        log_total = (highest_score + jnp.log(totals))[..., 0]
        return (output.astype(jnp.bfloat16), jnp.transpose(log_total))

    starts = jnp.arange(length // block_rows, dtype=jnp.int32) * block_rows
    outputs, log_totals = lax.map(one_block, starts)
    return (
        outputs.reshape(length, 1, heads_here, head_dim),
        log_totals.reshape(length, 1, heads_here),
        head_group,
    )


def attend_back(head_group, total_group, grad_group, segment):
    head_block = head_group[:, 0]
    log_totals = total_group[:, 0]
    grad_heads = grad_group[:, 0]
    head_dim = head_block.shape[2] // 3
    length = head_block.shape[0]
    heads_here = head_block.shape[1]
    block_rows = min(512, length)
    queries = head_block[:, :, :head_dim]
    keys_all = head_block[:, :, head_dim : 2 * head_dim]
    values_all = head_block[:, :, 2 * head_dim :]
    scale_factor = head_dim ** (-0.5)

    def one_block(carried, offset):
        key_grad, value_grad = carried
        query_rows = lax.dynamic_slice_in_dim(queries, offset, block_rows, 0)
        grad_rows = lax.dynamic_slice_in_dim(grad_heads, offset, block_rows, 0)
        total_rows = lax.dynamic_slice_in_dim(log_totals, offset, block_rows, 0)
        scores = (
            jnp.einsum("qhd,khd->hqk", query_rows, keys_all, preferred_element_type=jnp.float32)
            * scale_factor
        )
        scores = jnp.where(allowed_mask(segment, offset, block_rows)[None], scores, -jnp.inf)
        prob_rows = jnp.exp(scores - jnp.transpose(total_rows)[:, :, None])
        value_grad = value_grad + jnp.einsum(
            "hqk,qhd->khd",
            prob_rows.astype(jnp.bfloat16),
            grad_rows,
            preferred_element_type=jnp.float32,
        )
        prob_grad = jnp.einsum(
            "qhd,khd->hqk", grad_rows, values_all, preferred_element_type=jnp.float32
        )
        inner_sum = jnp.sum(prob_rows * prob_grad, axis=-1, keepdims=True)
        score_grad = (prob_rows * (prob_grad - inner_sum)).astype(jnp.bfloat16)
        query_grad = (
            jnp.einsum("hqk,khd->qhd", score_grad, keys_all, preferred_element_type=jnp.float32)
            * scale_factor
        )
        key_grad = (
            key_grad
            + jnp.einsum("hqk,qhd->khd", score_grad, query_rows, preferred_element_type=jnp.float32)
            * scale_factor
        )
        return ((key_grad, value_grad), query_grad)

    zeros_grad = jnp.zeros((length, heads_here, head_dim), jnp.float32)
    starts = jnp.arange(length // block_rows, dtype=jnp.int32) * block_rows
    (key_grad, value_grad), query_grads = lax.scan(one_block, (zeros_grad, zeros_grad), starts)
    query_grad = query_grads.reshape(length, heads_here, head_dim)
    return jnp.concatenate([query_grad, key_grad, value_grad], axis=2).astype(jnp.bfloat16)[:, None]


def on_device(
    tokens,
    cotangent,
    expert_ids,
    segment_ids,
    norm_gains,
    w_qkv,
    w_out,
    router,
    expert_in,
    expert_out,
):
    inputs = tokens[0].astype(jnp.float32)
    tok_count, model_width = inputs.shape
    segment = segment_ids[0]
    qkv_weight, out_weight, router_weight, gains_low = (
        lax.all_gather(w_qkv, ("seq", "exp", "fsdp"), axis=0, tiled=True),
        lax.all_gather(w_out, ("seq", "exp", "fsdp"), axis=0, tiled=True),
        lax.all_gather(router, ("seq", "exp", "fsdp"), axis=0, tiled=True),
        lax.all_gather(norm_gains, ("seq", "exp", "fsdp"), axis=0, tiled=True),
    )
    gains = gains_low.astype(jnp.float32)
    attn_norm, first_inverse = rms_parts(inputs, gains[:, 0])
    attn_low = attn_norm.astype(jnp.bfloat16)
    projected = jnp.dot(attn_low, qkv_weight, preferred_element_type=jnp.float32)
    query_norm, query_inverse = rms_parts(projected[:, :model_width], gains[:, 1])
    key_norm, key_inverse = rms_parts(projected[:, model_width : 2 * model_width], gains[:, 2])
    position = lax.axis_index("seq") * tok_count + jnp.arange(tok_count, dtype=jnp.int32)
    cosine, sine_part = rotary_tables(position, HEAD_DIM)
    head_shape = (tok_count, HEADS, HEAD_DIM)
    seq_count = lax.axis_size("seq")
    heads_dev = HEADS // seq_count
    packed = jnp.concatenate(
        [
            rotate(query_norm.reshape(head_shape), cosine, sine_part),
            rotate(key_norm.reshape(head_shape), cosine, sine_part),
            projected[:, 2 * model_width :].reshape(head_shape),
        ],
        axis=2,
    ).astype(jnp.bfloat16)
    packed = packed.reshape(tok_count, seq_count, heads_dev, 3 * HEAD_DIM)
    attended, log_totals, head_packed = attend_heads(
        segment, lax.all_to_all(packed, "seq", split_axis=1, concat_axis=0, tiled=True)
    )
    merged = lax.all_to_all(attended, "seq", split_axis=0, concat_axis=1, tiled=True)
    merged_flat = merged.reshape(tok_count, model_width)
    branch = jnp.einsum("tc,dc->td", merged_flat, out_weight, preferred_element_type=jnp.float32)
    residual = inputs + branch
    mlp_norm, mlp_inverse = rms_parts(residual, gains[:, 3])
    mlp_low = mlp_norm.astype(jnp.bfloat16)
    logits = jnp.dot(mlp_low, router_weight, preferred_element_type=jnp.float32)
    router_probs = jax.nn.softmax(logits, axis=-1)
    experts_total = router_weight.shape[1]
    routed_ids = expert_ids[0]
    pick_table = (
        routed_ids[:, :, None] == jnp.arange(experts_total, dtype=jnp.int32)[None, None, :]
    ).astype(jnp.float32)
    gate_values = jnp.einsum("tje,te->tj", pick_table, router_probs, precision=highest)
    exp_dev = expert_in.shape[1]
    exp_count = lax.axis_size("exp")
    capacity = tok_count * TOP // experts_total * 9 // 8
    flat_ids = routed_ids.reshape(-1)
    flat_table = pick_table.reshape(-1, experts_total).astype(jnp.int32)
    slot_rank = jnp.sum((jnp.cumsum(flat_table, axis=0) - 1) * flat_table, axis=1)
    slot_index = (flat_ids % exp_dev * exp_count + flat_ids // exp_dev) * capacity + slot_rank
    token_index = jnp.arange(tok_count * TOP, dtype=jnp.int32) // TOP
    buffer_shape = (exp_dev, exp_count, capacity, model_width)
    empty_buffer = jnp.zeros((exp_dev * exp_count * capacity, model_width), jnp.bfloat16)
    outgoing = empty_buffer.at[slot_index].set(mlp_low[token_index])
    arrived = lax.all_to_all(
        outgoing.reshape(buffer_shape), "exp", split_axis=1, concat_axis=1, tiled=True
    )
    expert_rows = arrived.reshape(exp_dev, exp_count * capacity, model_width)
    in_weight, down_weight = (
        lax.all_gather(expert_in, ("seq", "fsdp"), axis=0, tiled=True),
        lax.all_gather(expert_out, ("seq", "fsdp"), axis=0, tiled=True),
    )
    gate_up = jnp.einsum("erd,def->erf", expert_rows, in_weight, preferred_element_type=jnp.float32)
    gate_part = gate_up[..., :FF]
    up_part = gate_up[..., FF:]
    activated = (jax.nn.silu(gate_part) * up_part).astype(jnp.bfloat16)
    expert_result = jnp.einsum(
        "erf,def->erd", activated, down_weight, preferred_element_type=jnp.float32
    ).astype(jnp.bfloat16)
    returned = lax.all_to_all(
        expert_result.reshape(buffer_shape), "exp", split_axis=1, concat_axis=1, tiled=True
    )
    routed_out = returned.reshape(-1, model_width)[slot_index].reshape(tok_count, TOP, model_width)
    expert_mix = jnp.sum(routed_out.astype(jnp.float32) * gate_values[:, :, None], axis=1)
    output = (residual + expert_mix).astype(jnp.bfloat16)
    out_grad = cotangent[0].astype(jnp.float32)
    gate_grad = jnp.sum(routed_out.astype(jnp.float32) * out_grad[:, None, :], axis=2)
    send_grad = (
        (gate_values[:, :, None] * out_grad[:, None, :])
        .astype(jnp.bfloat16)
        .reshape(-1, model_width)
    )
    outgoing_grad = empty_buffer.at[slot_index].set(send_grad)
    arrived_grad = lax.all_to_all(
        outgoing_grad.reshape(buffer_shape), "exp", split_axis=1, concat_axis=1, tiled=True
    )
    arrived_grad = arrived_grad.reshape(exp_dev, exp_count * capacity, model_width)
    in_weight, down_weight = (
        lax.all_gather(expert_in, ("seq", "fsdp"), axis=0, tiled=True),
        lax.all_gather(expert_out, ("seq", "fsdp"), axis=0, tiled=True),
    )
    act_grad = jnp.einsum(
        "erd,def->erf", arrived_grad, down_weight, preferred_element_type=jnp.float32
    )
    sigmoid_gate = jax.nn.sigmoid(gate_part)
    gate_up_grad = jnp.concatenate(
        [
            act_grad * up_part * sigmoid_gate * (1.0 + gate_part * (1.0 - sigmoid_gate)),
            act_grad * gate_part * sigmoid_gate,
        ],
        axis=-1,
    ).astype(jnp.bfloat16)
    row_grad = jnp.einsum(
        "erf,def->erd", gate_up_grad, in_weight, preferred_element_type=jnp.float32
    ).astype(jnp.bfloat16)
    in_grad_full = jnp.einsum(
        "erd,erf->def", expert_rows, gate_up_grad, preferred_element_type=jnp.float32
    )
    down_grad_full = jnp.einsum(
        "erd,erf->def", arrived_grad, activated, preferred_element_type=jnp.float32
    )
    grad_expert_in, grad_expert_out = (
        lax.psum_scatter(
            in_grad_full.astype(jnp.bfloat16), ("seq", "fsdp"), scatter_dimension=0, tiled=True
        ).astype(jnp.float32),
        lax.psum_scatter(
            down_grad_full.astype(jnp.bfloat16), ("seq", "fsdp"), scatter_dimension=0, tiled=True
        ).astype(jnp.float32),
    )
    back_rows = lax.all_to_all(
        row_grad.reshape(buffer_shape), "exp", split_axis=1, concat_axis=1, tiled=True
    )
    copy_grads = back_rows.reshape(-1, model_width)[slot_index].reshape(tok_count, TOP, model_width)
    mlp_grad_experts = jnp.sum(copy_grads.astype(jnp.float32), axis=1)
    prob_grad = jnp.einsum("tje,tj->te", pick_table, gate_grad, precision=highest)
    logit_grad = router_probs * (
        prob_grad - jnp.sum(router_probs * prob_grad, axis=-1, keepdims=True)
    )
    router_grad_full = jnp.dot(mlp_low.astype(jnp.float32).T, logit_grad, precision=highest)
    mlp_grad = mlp_grad_experts + jnp.dot(
        logit_grad, router_weight.astype(jnp.float32).T, precision=highest
    )
    residual_norm_grad, mlp_gain_grad = rms_back(mlp_grad, residual, mlp_inverse, gains[:, 3])
    residual_grad = out_grad + residual_norm_grad
    branch_grad = residual_grad.astype(jnp.bfloat16)
    qkv_weight, out_weight = (
        lax.all_gather(w_qkv, ("seq", "exp", "fsdp"), axis=0, tiled=True),
        lax.all_gather(w_out, ("seq", "exp", "fsdp"), axis=0, tiled=True),
    )
    out_weight_grad = jnp.einsum(
        "td,tc->dc", branch_grad, merged_flat, preferred_element_type=jnp.float32
    )
    merged_grad = jnp.einsum(
        "td,dc->tc", branch_grad, out_weight, preferred_element_type=jnp.float32
    )
    merged_grad = merged_grad.astype(jnp.bfloat16).reshape(
        tok_count, seq_count, heads_dev, HEAD_DIM
    )
    heads_grad = lax.all_to_all(merged_grad, "seq", split_axis=1, concat_axis=0, tiled=True)
    packed_grad = attend_back(head_packed, log_totals, heads_grad, segment)
    token_grad = lax.all_to_all(packed_grad, "seq", split_axis=0, concat_axis=1, tiled=True)
    token_grad = token_grad.reshape(tok_count, HEADS, 3 * HEAD_DIM).astype(jnp.float32)
    query_grad = rotate_back(token_grad[:, :, :HEAD_DIM], cosine, sine_part).reshape(
        tok_count, model_width
    )
    key_grad = rotate_back(token_grad[:, :, HEAD_DIM : 2 * HEAD_DIM], cosine, sine_part).reshape(
        tok_count, model_width
    )
    value_grad = token_grad[:, :, 2 * HEAD_DIM :].reshape(tok_count, model_width)
    query_pre, query_gain_grad = rms_back(
        query_grad, projected[:, :model_width], query_inverse, gains[:, 1]
    )
    key_pre, key_gain_grad = rms_back(
        key_grad, projected[:, model_width : 2 * model_width], key_inverse, gains[:, 2]
    )
    qkv_grad = jnp.concatenate([query_pre, key_pre, value_grad], axis=1).astype(jnp.bfloat16)
    qkv_weight_grad = jnp.einsum(
        "td,tc->dc", attn_low, qkv_grad, preferred_element_type=jnp.float32
    )
    attn_in_grad = jnp.einsum("tc,dc->td", qkv_grad, qkv_weight, preferred_element_type=jnp.float32)
    input_norm_grad, first_gain_grad = rms_back(attn_in_grad, inputs, first_inverse, gains[:, 0])
    input_grad = residual_grad + input_norm_grad
    gain_grads = jnp.stack([first_gain_grad, query_gain_grad, key_gain_grad, mlp_gain_grad], axis=1)
    grad_norm_gains, grad_w_qkv, grad_w_out, grad_router = (
        lax.psum_scatter(gain_grads, ("seq", "exp", "fsdp"), scatter_dimension=0, tiled=True),
        lax.psum_scatter(qkv_weight_grad, ("seq", "exp", "fsdp"), scatter_dimension=0, tiled=True),
        lax.psum_scatter(out_weight_grad, ("seq", "exp", "fsdp"), scatter_dimension=0, tiled=True),
        lax.psum_scatter(router_grad_full, ("seq", "exp", "fsdp"), scatter_dimension=0, tiled=True),
    )
    return (
        output[None],
        input_grad[None],
        grad_norm_gains,
        grad_w_qkv,
        grad_w_out,
        grad_router,
        grad_expert_in,
        grad_expert_out,
    )


def solution(mesh):
    in_specs = (
        P(("exp", "fsdp"), "seq", None),
        P(("exp", "fsdp"), "seq", None),
        P(("exp", "fsdp"), "seq", None),
        P(("exp", "fsdp"), None),
        P(("seq", "exp", "fsdp"), None),
        P(("seq", "exp", "fsdp"), None),
        P(("seq", "exp", "fsdp"), None),
        P(("seq", "exp", "fsdp"), None),
        P(("seq", "fsdp"), "exp", None),
        P(("seq", "fsdp"), "exp", None),
    )
    out_specs = (
        P(("exp", "fsdp"), "seq", None),
        P(("exp", "fsdp"), "seq", None),
        P(("seq", "exp", "fsdp"), None),
        P(("seq", "exp", "fsdp"), None),
        P(("seq", "exp", "fsdp"), None),
        P(("seq", "exp", "fsdp"), None),
        P(("seq", "fsdp"), "exp", None),
        P(("seq", "fsdp"), "exp", None),
    )
    return jax.shard_map(
        on_device, mesh=mesh, in_specs=in_specs, out_specs=out_specs, check_vma=False
    )
```

profile of v0, /device:TPU:10, one launch (start us, length us, event | category | flops | bytes accessed | tf_op | source)
XLA Modules:
  0.0 2781.1 jit_solution(2796475139871000835)
XLA Ops:
  15.3 33.4 %all-gather = bf16[32,64,4]{1,2,0:T(4,128)(2,1)S(1)} all-gather(bf16[1,64,4]{1,2,0:T(4,128)(2,1)S(1)} %bitcast.295), channel_id=1, replica_groups=mesh['seq'=4,'exp'=4,'fsdp'=2] {'seq','exp','fsdp'}, dimensions={0}, use_global_device_ids=true | all-gather | bytes 16896 | tf_op jit(solution)/shard_map/all_gather | solution.py:182
  50.2 115.0 %all-gather.7.cloned.1.call-done = bf16[2048,6144]{1,0:T(8,128)(2,1)} async-done(((bf16[64,6144]{1,0:T(8,128)(2,1)}), bf16[2048,6144]{1,0:T(8,128)(2,1)}) %all-gather.7.cloned.1.call-update) | async-done | bytes 25165840 | tf_op jit(solution)/shard_map/all_gather | solution.py:179
  165.2 11.7 fusion.78
  197.9 11.9 concatenate.51
  220.2 45.3 %all-to-all-done = bf16[256,4,4,384]{3,2,0,1:T(4,128)(2,1)S(1)} async-done(((bf16[256,4,4,384]{3,2,0,1:T(4,128)(2,1)}), bf16[256,4,4,384]{3,2,0,1:T(4,128)(2,1)S(1)}, u32[]{:S(2)}, u32[]{:S(2)}) %all-to-all-start) | async-done | bytes 3145760 | tf_op jit(solution)/shard_map/all_to_all | solution.py:205
  267.3 24.4 while.33
  300.6 25.1 all-to-all-done.1
  338.3 54.5 %scatter_custom_fusion = bf16[2304,2048]{1,0:T(8,128)(2,1)} fusion(s32[2048]{0:T(1024)S(1)} %bitcast.286, bf16[256,2048]{1,0:T(8,128)(2,1)S(1)} %multiply_convert_fusion.4, s32[2048]{0:T(1024)S(1)} %broadcast_clamp_fusion.1, bf16[]{:T(256)} %constant.242.clone.1), kind=kCustom, calls=%fused_computation.95 | custom fusion | bytes 9437186 | tf_op jit(solution)/shard_map/scatter | solution.py:231
  411.7 226.6 %all-gather.1 = bf16[32,64,16]{1,2,0:T(8,128)(2,1)S(1)} all-gather(bf16[1,64,16]{1,2,0:T(8,128)(2,1)S(1)} %bitcast.294), channel_id=1, replica_groups=mesh['seq'=4,'exp'=4,'fsdp'=2] {'seq','exp','fsdp'}, dimensions={0}, use_global_device_ids=true | all-gather | bytes 67584 | tf_op jit(solution)/shard_map/all_gather | solution.py:181
  643.4 18.4 scatter_custom_fusion.1
  689.3 193.9 %all-to-all-done.4 = bf16[4,4,144,2048]{3,2,0,1:T(8,128)(2,1)} async-done(((bf16[4,4,144,2048]{3,2,0,1:T(8,128)(2,1)}), bf16[4,4,144,2048]{3,2,0,1:T(8,128)(2,1)}, u32[]{:S(2)}, u32[]{:S(2)}) %all-to-all-start.4) | async-done | bytes 9437216 | tf_op jit(solution)/shard_map/all_to_all | solution.py:261
  892.5 28.4 %fusion.101 = f32[4,576,2048]{2,1,0:T(8,128)} fusion(bf16[4,576,2048]{2,1,0:T(8,128)(2,1)} %bitcast.228, bf16[2048,4,2048]{2,0,1:T(8,128)(2,1)} %all-gather.11.cloned.1.call-done), kind=kOutput, calls=%fused_computation.225 | convolution fusion | flops 19327352832 | bytes 61865984 | tf_op jit(solution)/shard_map/erd,def->erf/dot_general | solution.py:240
  920.9 25.7 multiply_convert_fusion.2
  946.6 27.6 fusion.54
  992.6 16.5 convolution_convert_fusion
  1018.3 176.5 %all-to-all-done.5 = bf16[4,4,144,2048]{3,2,0,1:T(8,128)(2,1)} async-done(((bf16[4,4,144,2048]{3,2,0,1:T(8,128)(2,1)}), bf16[4,4,144,2048]{3,2,0,1:T(8,128)(2,1)}, u32[]{:S(2)}, u32[]{:S(2)}) %all-to-all-start.5) | async-done | bytes 9437216 | tf_op jit(solution)/shard_map/all_to_all | solution.py:297
  1213.3 21.2 gather_fusion.1
  1234.5 11.3 convert_reduce_fusion
  1245.8 160.0 %all-to-all-done.3 = bf16[4,4,144,2048]{3,2,0,1:T(8,128)(2,1)} async-done(((bf16[4,4,144,2048]{3,2,0,1:T(8,128)(2,1)}), bf16[4,4,144,2048]{3,2,0,1:T(8,128)(2,1)}, u32[]{:S(2)}, u32[]{:S(2)}) %all-to-all-start.3) | async-done | bytes 9437216 | tf_op jit(solution)/shard_map/all_to_all | solution.py:247
  1415.1 21.4 gather_fusion
  1471.0 11.7 all-to-all-done.6
  1482.7 51.8 %while.34 = (s32[]{:T(128)}, f32[1024,4,128]{0,2,1:T(8,128)S(1)}, f32[1024,4,128]{0,2,1:T(8,128)}, bf16[2,512,4,128]{3,1,0,2:T(8,128)(2,1)}, s32[2]{0:T(128)S(1)...) while((s32[]{:T(128)}, f32[1024,4,128]{0,2,1:T(8,128)S(1)}, ...), condition=%wide.region_22.23_spmd.clone, body=%wide.region_20.22_spmd.clone.sunk | while | flops 2720282624 | bytes 202455664 | solution.py:158
  1551.7 31.5 %all-to-all-done.7 = bf16[1024,1,4,384]{3,2,1,0:T(4,128)(2,1)S(1)} async-done(((bf16[1024,1,4,384]{3,2,1,0:T(4,128)(2,1)}), bf16[1024,1,4,384]{3,2,1,0:T(4,128)(2,1)S(1)}, u32[]{:S(2)}, u32[]{:S(2)}) %all-to-all-start.7) | async-done | bytes 3145760 | tf_op jit(solution)/shard_map/all_to_all | solution.py:328
  1616.0 14.2 fusion.66
  1631.6 21.4 convert_bitcast_fusion.1
  1653.1 33.7 %convert_bitcast_fusion = bf16[2048,4,2048]{0,2,1:T(8,128)(2,1)} fusion(bf16[4,576,2048]{2,1,0:T(8,128)(2,1)} %bitcast.229, bf16[4,576,1024]{2,1,0:T(8,128)(2,1)} %get-tuple-element.514, bf16[4,576,1024]{2,1,0:T(8,128)(2,1)} %get-tuple-element.513), kind=kOutput, calls=%fused_computation.80 | convolution fusion | flops 19363004416 | bytes 52428800 | tf_op jit(solution)/shard_map/erd,erf->def/dot_general | solution.py:283
  1697.9 21.8 fusion.67
  1724.6 84.6 %reduce-scatter.19.cloned.1.call-done = f32[64,4]{1,0:T(8,128)} async-done(((f32[2048,4]{1,0:T(8,128)}), f32[64,4]{1,0:T(8,128)}) %reduce-scatter.19.cloned.1.call-update) | async-done | bytes 1040
  1810.6 128.6 %reduce-scatter.17.cloned.1.call-done = bf16[256,4,1024]{0,2,1:T(8,128)(2,1)} async-done(((bf16[2048,4,1024]{0,2,1:T(8,128)(2,1)}), bf16[256,4,1024]{0,2,1:T(8,128)(2,1)}) %reduce-scatter.17.cloned.1.call-update) | async-done | bytes 2097168 | tf_op jit(solution)/shard_map/reduce_scatter | solution.py:293
  1944.0 204.1 %reduce-scatter.15.cloned.1.call-done = bf16[256,4,2048]{0,2,1:T(8,128)(2,1)} async-done(((bf16[2048,4,2048]{0,2,1:T(8,128)(2,1)}), bf16[256,4,2048]{0,2,1:T(8,128)(2,1)}) %reduce-scatter.15.cloned.1.call-update) | async-done | bytes 4194320 | tf_op jit(solution)/shard_map/reduce_scatter | solution.py:290
  2156.4 176.2 %reduce-scatter.13.cloned.1.call-done = f32[64,2048]{1,0:T(8,128)} async-done(((f32[2048,2048]{1,0:T(8,128)}), f32[64,2048]{1,0:T(8,128)}) %reduce-scatter.13.cloned.1.call-update) | async-done | bytes 524304 | tf_op jit(solution)/shard_map/reduce_scatter | solution.py:354
  2332.6 441.1 %reduce-scatter.11.cloned.1.call-done = f32[64,6144]{1,0:T(8,128)} async-done(((f32[2048,6144]{1,0:T(8,128)}), f32[64,6144]{1,0:T(8,128)}) %reduce-scatter.11.cloned.1.call-update) | async-done | bytes 1572880 | tf_op jit(solution)/shard_map/reduce_scatter | solution.py:353
  (384 shorter events, 364.1 us)
Async XLA Ops:
  7.2 158.0 %all-gather.7.cloned.1.call-start = ((), (), s32[]{:S(2)}) async-start(), calls=%async_computation.14 | async-start | bytes 25952256 | tf_op jit(solution)/shard_map/all_gather | solution.py:179
  7.9 322.4 %all-gather.9.cloned.1.call-start = ((), (), s32[]{:S(2)}) async-start(), calls=%async_computation.15 | async-start | bytes 8650752 | tf_op jit(solution)/shard_map/all_gather | solution.py:180
  8.7 883.8 %all-gather.11.cloned.1.call-start = ((), (), s32[]{:S(2)}) async-start(), calls=%async_computation.16 | async-start | bytes 37748736 | tf_op jit(solution)/shard_map/all_gather | solution.py:237
  49.8 127.1 %copy-start.59 = (f32[256]{0:T(256)}, f32[256]{0:T(256)S(1)}, u32[]{:S(2)}) copy-start(f32[256]{0:T(256)S(1)} %get-tuple-element.542) | copy-start | bytes 3076
  50.1 135.7 %copy-start.37 = (f32[256,64]{0,1:T(8,128)}, f32[256,64]{0,1:T(8,128)S(1)}, u32[]{:S(2)}) copy-start(f32[256,64]{0,1:T(8,128)S(1)} %get-tuple-element.539) | copy-start | bytes 196612
  50.1 135.7 %copy-start.39 = (f32[256,64]{0,1:T(8,128)}, f32[256,64]{0,1:T(8,128)S(1)}, u32[]{:S(2)}) copy-start(f32[256,64]{0,1:T(8,128)S(1)} %get-tuple-element.540) | copy-start | bytes 196612
  50.1 126.8 %copy-start.45 = (f32[2048,1]{0,1:T(1,128)}, f32[2048,1]{0,1:T(1,128)S(1)}, u32[]{:S(2)}) copy-start(f32[2048,1]{0,1:T(1,128)S(1)} %get-tuple-element.538) | copy-start | bytes 24580
  50.1 128.3 %copy-start.53 = (f32[2048,1]{0,1:T(1,128)}, f32[2048,1]{0,1:T(1,128)S(1)}, u32[]{:S(2)}) copy-start(f32[2048,1]{0,1:T(1,128)S(1)} %get-tuple-element.536) | copy-start | bytes 24580
  50.1 128.2 %copy-start.55 = (f32[2048,1]{0,1:T(1,128)}, f32[2048,1]{0,1:T(1,128)S(1)}, u32[]{:S(2)}) copy-start(f32[2048,1]{0,1:T(1,128)S(1)} %get-tuple-element.537) | copy-start | bytes 24580
  50.2 287.3 %copy-start.51 = (f32[2048,1]{0,1:T(1,128)}, f32[2048,1]{0,1:T(1,128)S(1)}, u32[]{:S(2)}) copy-start(f32[2048,1]{0,1:T(1,128)S(1)} %get-tuple-element.535) | copy-start | bytes 24580
  209.7 55.8 %all-to-all-start = ((bf16[256,4,4,384]{3,2,0,1:T(4,128)(2,1)}), bf16[256,4,4,384]{3,2,0,1:T(4,128)(2,1)S(1)}, u32[]{:S(2)}, u32[]{:S(2)}) async-start(bf16[256,4,4,384]{3,2,0,1:T(4,128)(2,1)} %concatenate.51), calls=%async_computation | async-start | bytes 6291456 | tf_op jit(solution)/shard_map/all_to_all | solution.py:205
  291.7 45.0 %copy-start.11 = (bf16[1024,4,128]{2,0,1:T(8,128)(2,1)}, bf16[1024,4,128]{2,0,1:T(8,128)(2,1)S(1)}, u32[]{:S(2)}) copy-start(bf16[1024,4,128]{2,0,1:T(8,128)(2,1)S(1)} %get-tuple-element.798) | copy-start | bytes 3145732
  291.7 45.0 %copy-start.57 = (f32[2,512,4]{1,2,0:T(4,128)}, f32[2,512,4]{1,2,0:T(4,128)S(1)}, u32[]{:S(2)}) copy-start(f32[2,512,4]{1,2,0:T(4,128)S(1)} %get-tuple-element.334) | copy-start | bytes 49156
  291.7 45.0 %copy-start.81 = (s32[2]{0:T(128)}, s32[2]{0:T(128)S(1)}, u32[]{:S(2)}) copy-start(s32[2]{0:T(128)S(1)} %get-tuple-element.834) | copy-start | bytes 28
  295.6 30.0 %all-to-all-start.1 = ((bf16[1024,1,4,128]{3,2,1,0:T(4,128)(2,1)}), bf16[1024,1,4,128]{3,2,1,0:T(4,128)(2,1)}, u32[]{:S(2)}, u32[]{:S(2)}) async-start(bf16[1024,1,4,128]{3,2,1,0:T(4,128)(2,1)} %copy.141), calls=%async_computation.1 | async-start | bytes 2097152 | tf_op jit(solution)/shard_map/all_to_all | solution.py:207
  300.6 342.8 %copy-start.65 = (s32[2048,1]{0,1:T(1,128)}, s32[2048,1]{0,1:T(1,128)S(1)}, u32[]{:S(2)}) copy-start(s32[2048,1]{0,1:T(1,128)S(1)} %compare_select_fusion.1) | copy-start | bytes 24580
  337.4 55.4 %copy-start.69 = (f32[256]{0:T(256)}, f32[256]{0:T(256)S(1)}, u32[]{:S(2)}) copy-start(f32[256]{0:T(256)S(1)} %get-tuple-element.548) | copy-start | bytes 3076
  338.3 301.8 %copy-start.24 = (bf16[256,2048]{1,0:T(8,128)(2,1)}, bf16[256,2048]{1,0:T(8,128)(2,1)S(1)}, u32[]{:S(2)}) copy-start(bf16[256,2048]{1,0:T(8,128)(2,1)S(1)} %multiply_convert_fusion.4) | copy-start | bytes 3145732
  402.0 269.1 %all-to-all-start.2 = ((bf16[4,4,144,2048]{3,2,0,1:T(8,128)(2,1)}), bf16[4,4,144,2048]{3,2,0,1:T(8,128)(2,1)}, u32[]{:S(2)}, u32[]{:S(2)}) async-start(bf16[4,4,144,2048]{3,2,0,1:T(8,128)(2,1)} %copy.147), calls=%async_computation.2 | async-start | bytes 18874368 | tf_op jit(solution)/shard_map/all_to_all | solution.py:232
  409.7 511.2 %all-gather.13.cloned.1.call-start = ((), (), s32[]{:S(2)}) async-start(), calls=%async_computation.17 | async-start | bytes 18874368 | tf_op jit(solution)/shard_map/all_gather | solution.py:238
  671.1 212.1 %all-to-all-start.4 = ((bf16[4,4,144,2048]{3,2,0,1:T(8,128)(2,1)}), bf16[4,4,144,2048]{3,2,0,1:T(8,128)(2,1)}, u32[]{:S(2)}, u32[]{:S(2)}) async-start(bf16[4,4,144,2048]{3,2,0,1:T(8,128)(2,1)} %copy.155), calls=%async_computation.4 | async-start | bytes 18874368 | tf_op jit(solution)/shard_map/all_to_all | solution.py:261
  983.3 211.5 %all-to-all-start.5 = ((bf16[4,4,144,2048]{3,2,0,1:T(8,128)(2,1)}), bf16[4,4,144,2048]{3,2,0,1:T(8,128)(2,1)}, u32[]{:S(2)}, u32[]{:S(2)}) async-start(bf16[4,4,144,2048]{3,2,0,1:T(8,128)(2,1)} %copy.157), calls=%async_computation.5 | async-start | bytes 18874368 | tf_op jit(solution)/shard_map/all_to_all | solution.py:297
  1018.3 185.9 %copy-start.66 = (s32[2048,1]{0,1:T(1,128)S(1)}, s32[2048,1]{0,1:T(1,128)}, u32[]{:S(2)}) copy-start(s32[2048,1]{0,1:T(1,128)} %copy-done.65) | copy-start | bytes 24580
  1194.8 211.0 %all-to-all-start.3 = ((bf16[4,4,144,2048]{3,2,0,1:T(8,128)(2,1)}), bf16[4,4,144,2048]{3,2,0,1:T(8,128)(2,1)}, u32[]{:S(2)}, u32[]{:S(2)}) async-start(bf16[4,4,144,2048]{3,2,0,1:T(8,128)(2,1)} %copy.151), calls=%async_computation.3 | async-start | bytes 18874368 | tf_op jit(solution)/shard_map/all_to_all | solution.py:247
  1463.1 19.6 all-to-all-start.6
  1544.0 39.3 %all-to-all-start.7 = ((bf16[1024,1,4,384]{3,2,1,0:T(4,128)(2,1)}), bf16[1024,1,4,384]{3,2,1,0:T(4,128)(2,1)S(1)}, u32[]{:S(2)}, u32[]{:S(2)}) async-start(bf16[1024,1,4,384]{3,2,1,0:T(4,128)(2,1)} %copy.164), calls=%async_computation.7 | async-start | bytes 6291456 | tf_op jit(solution)/shard_map/all_to_all | solution.py:328
  1548.2 171.5 %reduce-scatter.21.cloned.1.call-start = ((), (), s32[]{:S(2)}) async-start(), calls=%async_computation.23 | async-start | bytes 1081344
  1551.7 257.6 %reduce-scatter.19.cloned.1.call-start = ((), (), s32[]{:S(2)}) async-start(), calls=%async_computation.22 | async-start | bytes 1081344
  1631.6 307.6 %reduce-scatter.17.cloned.1.call-start = ((), (), s32[]{:S(2)}) async-start(), calls=%async_computation.21 | async-start | bytes 18874368 | tf_op jit(solution)/shard_map/reduce_scatter | solution.py:293
  1653.0 495.0 %reduce-scatter.15.cloned.1.call-start = ((), (), s32[]{:S(2)}) async-start(), calls=%async_computation.20 | async-start | bytes 37748736 | tf_op jit(solution)/shard_map/reduce_scatter | solution.py:290
  1686.8 645.8 %reduce-scatter.13.cloned.1.call-start = ((), (), s32[]{:S(2)}) async-start(), calls=%async_computation.19 | async-start | bytes 17301504 | tf_op jit(solution)/shard_map/reduce_scatter | solution.py:354
  1697.8 1076.0 %reduce-scatter.11.cloned.1.call-start = ((), (), s32[]{:S(2)}) async-start(), calls=%async_computation.18 | async-start | bytes 51904512 | tf_op jit(solution)/shard_map/reduce_scatter | solution.py:353
  (85 other events, 696.2 us)
Sparse Core Ops, SparseCore 0:
  11.0 154.1 all-gather.6
  168.1 92.5 all-gather.8
  263.2 186.6 all-gather.10
  452.3 89.8 all-gather.12
  1551.8 123.5 reduce-scatter.20
  1677.6 131.6 reduce-scatter.18
  1812.8 126.3 reduce-scatter.16
  1942.8 205.2 reduce-scatter.14
  2151.0 181.5 reduce-scatter.12
  2340.6 433.1 reduce-scatter.10
where the time goes:
time: 2800 us; the launch traced here: 2780 us
  waiting for transfers between devices  1800 us (64%)
  local copies, waits for them, and re-layouts  277 us (10%)
  matrix products  271 us (10%)
  blocking collectives  260 us (9%)
  other arithmetic  97 us (3%)
  starting transfers between devices  57.3 us (2%)
    reduce_scatter x1, waiting for transfers between devices, on_device(): lax.psum_scatter(qkv_weight_grad, ('seq', 'exp', 'fsdp'), scatter_dimensi...  441 us
    all_gather x1, blocking collectives, on_device(): lax.all_gather(router, ('seq', 'exp', 'fsdp'), axis=0, tiled=True)  227 us
    reduce_scatter x1, waiting for transfers between devices, on_device(): lax.psum_scatter(in_grad_full.astype(jnp.bfloat16), ('seq', 'fsdp'), scat...  204 us
    all_to_all x1, waiting for transfers between devices, on_device(): lax.all_to_all(outgoing_grad.reshape(buffer_shape), 'exp', split_axis=1,...  194 us
    all_to_all x1, waiting for transfers between devices, on_device(): lax.all_to_all(row_grad.reshape(buffer_shape), 'exp', split_axis=1, conca...  177 us
    reduce_scatter x1, waiting for transfers between devices, on_device(): lax.psum_scatter(out_weight_grad, ('seq', 'exp', 'fsdp'), scatter_dimensi...  176 us
    all_to_all x1, waiting for transfers between devices, on_device(): lax.all_to_all(expert_result.reshape(buffer_shape), 'exp', split_axis=1,...  160 us
    reduce_scatter x1, waiting for transfers between devices, on_device(): lax.psum_scatter(down_grad_full.astype(jnp.bfloat16), ('seq', 'fsdp'), sc...  129 us
  transfers between devices with their start and end apart: 18, of which 13 were waited for; matrix products, arithmetic and copies ran while one was open for 17% of the time, Pallas kernels for 0%

commit v1 on v0

v1 whole, which is shorter than its diff:
```python
import jax
import jax.numpy as jnp
from jax import lax
from jax.sharding import PartitionSpec as P

HEADS = 16
HEAD_DIM = 128
FF = 1024
TOP = 8
ATT_BLOCK = 256


epsilon = 1e-05
rotary_base = 10000.0
highest = lax.Precision.HIGHEST
f32 = jnp.float32
bf16 = jnp.bfloat16


def swap_pairs(count, mask):
    return [(i, i ^ mask) for i in range(count)]


def put_block(buffer, block, index, axis):
    return lax.dynamic_update_index_in_dim(buffer, block, index, axis)


def is_square(axis):
    return lax.axis_size(axis) == 4


def gather_square(block, axis, out_axis):
    if not is_square(axis):
        return lax.all_gather(block, axis, axis=out_axis)
    own = lax.axis_index(axis)
    half = block.shape[0] // 2
    first, second = block[:half], block[half:]
    first_near = lax.ppermute(first, axis, swap_pairs(4, 1))
    second_near = lax.ppermute(second, axis, swap_pairs(4, 2))
    first_pair = lax.ppermute(jnp.stack([first, first_near]), axis, swap_pairs(4, 2))
    second_pair = lax.ppermute(jnp.stack([second, second_near]), axis, swap_pairs(4, 1))
    parts = [
        (block[:half], block[half:]),
        (first_near, second_pair[0]),
        (first_pair[0], second_near),
        (first_pair[1], second_pair[1]),
    ]
    shape = block.shape[:out_axis] + (4,) + block.shape[out_axis:]
    out = jnp.zeros(shape, block.dtype)
    for mask, (low_part, high_part) in enumerate(parts):
        whole = jnp.concatenate([low_part, high_part], axis=0)
        out = put_block(out, whole, own ^ mask, out_axis)
    return out


def scatter_square(blocks, axis):
    if not is_square(axis):
        return lax.psum_scatter(blocks, axis, scatter_dimension=0, tiled=False)
    own = lax.axis_index(axis)
    kind = blocks.dtype
    half = blocks.shape[1] // 2
    rel = [lax.dynamic_index_in_dim(blocks, own ^ mask, 0, keepdims=False) for mask in range(4)]

    def add(one, other):
        return (one.astype(f32) + other.astype(f32)).astype(kind)

    first = [block[:half] for block in rel]
    second = [block[half:] for block in rel]
    first_in = lax.ppermute(jnp.stack([first[2], first[3]]), axis, swap_pairs(4, 2))
    second_in = lax.ppermute(jnp.stack([second[1], second[3]]), axis, swap_pairs(4, 1))
    first_far = lax.ppermute(add(first[1], first_in[1]), axis, swap_pairs(4, 1))
    second_far = lax.ppermute(add(second[2], second_in[1]), axis, swap_pairs(4, 2))
    first_sum = first[0].astype(f32) + first_in[0].astype(f32) + first_far.astype(f32)
    second_sum = second[0].astype(f32) + second_in[0].astype(f32) + second_far.astype(f32)
    return jnp.concatenate([first_sum, second_sum], axis=0)


def sum_square(value, axis):
    count = lax.axis_size(axis)
    if count & (count - 1):
        return lax.psum(value, axis)
    mask = 1
    while mask < count:
        value = value + lax.ppermute(value, axis, swap_pairs(count, mask))
        mask *= 2
    return value


def gather_line(block, axis):
    count = lax.axis_size(axis)
    own = lax.axis_index(axis)
    up, down = block, block
    ups, downs = [block], [block]
    for step in range(1, count):
        up = lax.ppermute(up, axis, [(j, j + 1) for j in range(step - 1, count - 1)])
        down = lax.ppermute(down, axis, [(j, j - 1) for j in range(1, count - step + 1)])
        ups.append(up)
        downs.append(down)
    return [block] + [
        jnp.where(own >= k, ups[k], downs[count - k]) for k in range(1, count)
    ]


def scatter_line(blocks, axis):
    count = lax.axis_size(axis)
    kind = blocks[0].dtype
    up = down = None

    def add(one, other):
        return one if other is None else (one.astype(f32) + other.astype(f32)).astype(kind)

    for step in range(1, count):
        up = lax.ppermute(
            add(blocks[step], up), axis, [(j, j + 1) for j in range(min(step, count - 1))]
        )
        down = lax.ppermute(
            add(blocks[count - step], down),
            axis,
            [(j, j - 1) for j in range(max(count - step, 1), count)],
        )
    return blocks[0].astype(f32) + up.astype(f32) + down.astype(f32)


def order_line(blocks, axis, out_axis):
    count = lax.axis_size(axis)
    own = lax.axis_index(axis)
    shape = blocks[0].shape[:out_axis] + (count,) + blocks[0].shape[out_axis:]
    out = jnp.zeros(shape, blocks[0].dtype)
    for k, block in enumerate(blocks):
        out = put_block(out, block, lax.rem(own - k + count, count), out_axis)
    return out


def split_line(stacked, axis, in_axis):
    count = lax.axis_size(axis)
    own = lax.axis_index(axis)
    return [
        lax.dynamic_index_in_dim(
            stacked, lax.rem(own - k + count, count), in_axis, keepdims=False
        )
        for k in range(count)
    ]


def gather_core(block, axis, out_axis):
    if lax.axis_size(axis) != 2:
        return lax.all_gather(block, axis, axis=out_axis)
    other = lax.ppermute(block, axis, swap_pairs(2, 1))
    is_first = lax.axis_index(axis) == 0
    return jnp.stack(
        [jnp.where(is_first, block, other), jnp.where(is_first, other, block)], axis=out_axis
    )


def scatter_core(stacked, axis, in_axis):
    if lax.axis_size(axis) != 2:
        return lax.psum_scatter(stacked, axis, scatter_dimension=in_axis, tiled=False)
    own = lax.axis_index(axis)
    kept = lax.dynamic_index_in_dim(stacked, own, in_axis, keepdims=False)
    given = lax.dynamic_index_in_dim(stacked, 1 - own, in_axis, keepdims=False)
    received = lax.ppermute(given, axis, swap_pairs(2, 1))
    return (kept.astype(f32) + received.astype(f32)).astype(stacked.dtype)


def rms_inverse(values):
    return lax.rsqrt(jnp.mean(values * values, axis=-1, keepdims=True) + epsilon)


def rms_back(gradient, values, inverse, gain_vector):
    scaled = gradient * gain_vector
    gain_grad = jnp.sum(gradient * values * inverse, axis=0)
    value_grad = inverse * scaled - values * inverse**3 * jnp.mean(
        scaled * values, axis=-1, keepdims=True
    )
    return (value_grad, gain_grad)


def rotary_tables(position, head_dim):
    half_dim = head_dim // 2
    exponent = jnp.arange(half_dim, dtype=f32) * (2.0 / head_dim)
    angles = position.astype(f32)[:, None] * (rotary_base ** (-exponent))[None, :]
    return (jnp.cos(angles)[:, None, :], jnp.sin(angles)[:, None, :])


def rotate(values, cosine, sine_part):
    half_dim = values.shape[-1] // 2
    first_half = values[..., :half_dim]
    second_half = values[..., half_dim:]
    return jnp.concatenate(
        [
            first_half * cosine - second_half * sine_part,
            second_half * cosine + first_half * sine_part,
        ],
        axis=-1,
    )


def rotate_back(gradient, cosine, sine_part):
    return rotate(gradient, cosine, -sine_part)


def block_scores(query_rows, keys, query_segment, key_segment, block_index):
    scores = jnp.einsum("qhd,khd->hqk", query_rows, keys, preferred_element_type=f32)
    scores = scores * (query_rows.shape[-1] ** (-0.5))
    allowed = query_segment[:, None] == key_segment[None, :]
    return jnp.where(allowed[None], scores, -jnp.inf)


def attend(queries, keys, values, segment):
    length = queries.shape[0]
    outputs, log_totals = [], []
    for start in range(0, length, ATT_BLOCK):
        stop = start + ATT_BLOCK
        scores = block_scores(
            queries[start:stop], keys[:stop], segment[start:stop], segment[:stop], start
        )
        highest_score = jnp.max(scores, axis=-1, keepdims=True)
        exponent_terms = jnp.exp(scores - highest_score)
        totals = jnp.sum(exponent_terms, axis=-1, keepdims=True)
        weights = (exponent_terms / totals).astype(bf16)
        output = jnp.einsum("hqk,khd->qhd", weights, values[:stop], preferred_element_type=f32)
        outputs.append(output.astype(bf16))
        log_totals.append(highest_score + jnp.log(totals))
    return jnp.concatenate(outputs, axis=0), log_totals


def attend_back(queries, keys, values, log_totals, grads, segment):
    length = queries.shape[0]
    scale_factor = queries.shape[-1] ** (-0.5)
    query_grads = []
    key_grads = [[] for _ in range(0, length, ATT_BLOCK)]
    value_grads = [[] for _ in range(0, length, ATT_BLOCK)]
    for number, start in enumerate(range(0, length, ATT_BLOCK)):
        stop = start + ATT_BLOCK
        query_rows, grad_rows = queries[start:stop], grads[start:stop]
        scores = block_scores(query_rows, keys[:stop], segment[start:stop], segment[:stop], start)
        prob_rows = jnp.exp(scores - log_totals[number])
        value_grad = jnp.einsum(
            "hqk,qhd->khd", prob_rows.astype(bf16), grad_rows, preferred_element_type=f32
        )
        prob_grad = jnp.einsum(
            "qhd,khd->hqk", grad_rows, values[:stop], preferred_element_type=f32
        )
        inner_sum = jnp.sum(prob_rows * prob_grad, axis=-1, keepdims=True)
        score_grad = (prob_rows * (prob_grad - inner_sum)).astype(bf16)
        query_grad = jnp.einsum("hqk,khd->qhd", score_grad, keys[:stop], preferred_element_type=f32)
        key_grad = jnp.einsum("hqk,qhd->khd", score_grad, query_rows, preferred_element_type=f32)
        query_grads.append((query_grad * scale_factor).astype(bf16))
        for earlier in range(number + 1):
            rows = slice(earlier * ATT_BLOCK, (earlier + 1) * ATT_BLOCK)
            key_grads[earlier].append(key_grad[rows])
            value_grads[earlier].append(value_grad[rows])
    key_grad = jnp.concatenate([sum(parts) for parts in key_grads], axis=0) * scale_factor
    value_grad = jnp.concatenate([sum(parts) for parts in value_grads], axis=0)
    return jnp.concatenate(query_grads, axis=0), key_grad.astype(bf16), value_grad.astype(bf16)


def on_device(
    tokens,
    cotangent,
    expert_ids,
    segment_ids,
    norm_gains,
    w_qkv,
    w_out,
    router,
    expert_in,
    expert_out,
):
    own_low = tokens[0]
    inputs = own_low.astype(f32)
    tok_count, model_width = inputs.shape
    segment = segment_ids[0]
    length = segment.shape[0]
    seq_count = lax.axis_size("seq")
    exp_count = lax.axis_size("exp")
    core_count = lax.axis_size("fsdp")
    own_seq = lax.axis_index("seq")
    own_exp = lax.axis_index("exp")
    rows_dev = w_qkv.shape[0]
    heads_dev = HEADS // seq_count
    head_cols = heads_dev * HEAD_DIM
    experts_total = router.shape[1]
    exp_dev = expert_in.shape[1]

    small = jnp.concatenate([norm_gains, router], axis=1).T
    small = gather_square(small, "seq", 1)
    small = order_line(gather_line(small, "exp"), "exp", 2)
    small = gather_core(small, "fsdp", 3).reshape(-1, model_width)
    gains = small[:4].astype(f32)
    router_rows = small[4:]

    all_tokens = gather_square(own_low, "seq", 0).reshape(length, model_width)
    heads_weight = lax.all_to_all(
        w_qkv.reshape(rows_dev, 3, seq_count, head_cols), "seq", split_axis=2, concat_axis=0, tiled=True
    ).reshape(seq_count, rows_dev, 3 * head_cols)
    heads_weight = order_line(gather_line(heads_weight, "exp"), "exp", 1)
    heads_weight = gather_core(heads_weight, "fsdp", 2).reshape(model_width, 3 * head_cols)

    out_weight = gather_square(w_out, "seq", 0)
    out_weight = order_line(gather_line(out_weight, "exp"), "exp", 1)
    out_weight = gather_core(out_weight, "fsdp", 2).reshape(model_width, model_width)

    in_weight = lax.all_gather(
        jnp.transpose(expert_in, (1, 0, 2)), ("seq", "fsdp"), axis=1, tiled=True
    )
    down_weight = lax.all_gather(
        jnp.transpose(expert_out, (1, 0, 2)), ("seq", "fsdp"), axis=1, tiled=True
    )
    cot_group = jnp.stack(gather_line(cotangent[0], "exp"))

    capacity = tok_count * TOP // experts_total * 9 // 8
    chosen = jnp.any(
        expert_ids[0][:, :, None] == jnp.arange(experts_total, dtype=jnp.int32)[None, None, :], axis=1
    )
    earlier = (
        jnp.arange(tok_count)[:, None] > jnp.arange(tok_count)[None, :]
    ).astype(bf16)
    rank = jnp.dot(earlier, chosen.astype(bf16), preferred_element_type=f32)
    rank = jnp.where(chosen, rank, -1.0).T
    rank_group = jnp.stack(gather_line(rank, "exp"))
    rank_group = lax.dynamic_slice_in_dim(rank_group, own_exp * exp_dev, exp_dev, 1)
    rank_group = jnp.transpose(rank_group, (1, 0, 2))
    pick = rank_group[:, :, None, :] == jnp.arange(capacity, dtype=f32)[None, None, :, None]
    pick_low = pick.astype(bf16)

    all_inputs = all_tokens.astype(f32)
    first_inverse = rms_inverse(all_inputs)
    attn_low = (all_inputs * first_inverse * gains[0]).astype(bf16)
    projected = jnp.dot(attn_low, heads_weight, preferred_element_type=f32)
    own_gains = lax.dynamic_slice_in_dim(gains, own_seq * head_cols, head_cols, 1)
    query_pre, key_pre = projected[:, :head_cols], projected[:, head_cols : 2 * head_cols]
    squares = jnp.stack([jnp.sum(query_pre * query_pre, axis=-1), jnp.sum(key_pre * key_pre, axis=-1)])
    squares = sum_square(squares, "seq")
    inverses = lax.rsqrt(squares / model_width + epsilon)
    query_inverse, key_inverse = inverses[0][:, None], inverses[1][:, None]
    cosine, sine_part = rotary_tables(jnp.arange(length, dtype=jnp.int32), HEAD_DIM)
    head_shape = (length, heads_dev, HEAD_DIM)
    queries = rotate(
        (query_pre * query_inverse * own_gains[1]).reshape(head_shape), cosine, sine_part
    ).astype(bf16)
    keys = rotate(
        (key_pre * key_inverse * own_gains[2]).reshape(head_shape), cosine, sine_part
    ).astype(bf16)
    values = projected[:, 2 * head_cols :].astype(bf16).reshape(head_shape)
    attended, log_totals = attend(queries, keys, values, segment)
    merged = lax.all_to_all(
        attended.reshape(length, head_cols), "seq", split_axis=0, concat_axis=1, tiled=True
    )
    branch = jnp.einsum("tc,dc->td", merged, out_weight, preferred_element_type=f32)
    residual = inputs + branch
    mlp_inverse = rms_inverse(residual)
    mlp_low = (residual * mlp_inverse * gains[3]).astype(bf16)

    mlp_group = jnp.stack(gather_line(mlp_low, "exp"))
    logits = jnp.einsum("std,ed->ste", mlp_group, router_rows, preferred_element_type=f32)
    group_probs = jax.nn.softmax(logits, axis=-1)
    router_probs = group_probs[0]
    near_probs = lax.dynamic_slice_in_dim(group_probs, own_exp * exp_dev, exp_dev, 2)
    near_probs = jnp.transpose(near_probs, (2, 0, 1))
    gate_rows = jnp.sum(jnp.where(pick, near_probs[:, :, None, :], 0.0), axis=-1)
    rows_shape = (exp_dev, exp_count * capacity)
    gate_rows = gate_rows.reshape(rows_shape + (1,))
    expert_rows = jnp.einsum("esrt,std->esrd", pick_low, mlp_group, preferred_element_type=f32)
    expert_rows = expert_rows.astype(bf16).reshape(rows_shape + (model_width,))
    cot_rows = jnp.einsum("esrt,std->esrd", pick_low, cot_group, preferred_element_type=f32)
    cot_rows = cot_rows.astype(bf16).reshape(rows_shape + (model_width,))
    gate_up = jnp.einsum("erd,edf->erf", expert_rows, in_weight, preferred_element_type=f32)
    gate_part, up_part = gate_up[..., :FF], gate_up[..., FF:]
    sigmoid_gate = jax.nn.sigmoid(gate_part)
    silu_gate = gate_part * sigmoid_gate
    activated = silu_gate * up_part
    gated = (activated * gate_rows).astype(bf16)
    expert_result = jnp.einsum("erf,edf->erd", gated, down_weight, preferred_element_type=f32)
    expert_result = expert_result.astype(bf16).reshape(exp_dev, exp_count, capacity, model_width)
    mix_parts = jnp.einsum(
        "esrt,esrd->std", pick_low, expert_result, preferred_element_type=f32
    ).astype(bf16)

    result_grad = jnp.einsum("erd,edf->erf", cot_rows, down_weight, preferred_element_type=f32)
    gate_grad = jnp.sum(result_grad * activated, axis=-1)
    act_grad = result_grad * gate_rows
    gate_up_grad = jnp.concatenate(
        [
            act_grad * up_part * sigmoid_gate * (1.0 + gate_part * (1.0 - sigmoid_gate)),
            act_grad * silu_gate,
        ],
        axis=-1,
    ).astype(bf16)
    down_grad = jnp.einsum("erd,erf->edf", cot_rows, gated, preferred_element_type=f32)
    grad_expert_out = lax.psum_scatter(
        down_grad.astype(bf16), ("seq", "fsdp"), scatter_dimension=1, tiled=True
    )
    row_grad = jnp.einsum("erf,edf->erd", gate_up_grad, in_weight, preferred_element_type=f32)
    row_grad = row_grad.astype(bf16).reshape(exp_dev, exp_count, capacity, model_width)
    copy_parts = jnp.einsum(
        "esrt,esrd->std", pick_low, row_grad, preferred_element_type=f32
    ).astype(bf16)
    in_grad = jnp.einsum("erd,erf->edf", expert_rows, gate_up_grad, preferred_element_type=f32)
    grad_expert_in = lax.psum_scatter(
        in_grad.astype(bf16), ("seq", "fsdp"), scatter_dimension=1, tiled=True
    )
    gate_grad = gate_grad.reshape(exp_dev, exp_count, capacity)
    prob_parts = jnp.sum(jnp.where(pick, gate_grad[..., None], 0.0), axis=2)
    prob_parts = jnp.transpose(prob_parts, (1, 0, 2))
    prob_parts = lax.dynamic_update_slice_in_dim(
        jnp.zeros((exp_count, experts_total, tok_count), f32), prob_parts, own_exp * exp_dev, 1
    )
    prob_grad = scatter_line([prob_parts[k] for k in range(exp_count)], "exp").T
    mlp_grad_experts = scatter_line([copy_parts[k] for k in range(exp_count)], "exp")
    expert_mix = scatter_line([mix_parts[k] for k in range(exp_count)], "exp")
    output = (residual + expert_mix).astype(bf16)

    logit_grad = router_probs * (
        prob_grad - jnp.sum(router_probs * prob_grad, axis=-1, keepdims=True)
    )
    router_grad = jnp.dot(logit_grad.T, mlp_low.astype(f32), precision=highest)
    mlp_grad = mlp_grad_experts + jnp.dot(
        logit_grad, router_rows.astype(f32), precision=highest
    )
    residual_norm_grad, mlp_gain_grad = rms_back(mlp_grad, residual, mlp_inverse, gains[3])
    residual_grad = cotangent[0].astype(f32) + residual_norm_grad
    branch_grad = residual_grad.astype(bf16)

    merged_grad = jnp.einsum("td,dc->tc", branch_grad, out_weight, preferred_element_type=f32)
    heads_grad = lax.all_to_all(
        merged_grad.astype(bf16), "seq", split_axis=1, concat_axis=0, tiled=True
    ).reshape(head_shape)
    out_weight_grad = jnp.einsum("td,tc->dc", branch_grad, merged, preferred_element_type=f32)
    query_grad, key_grad, value_grad = attend_back(
        queries, keys, values, log_totals, heads_grad, segment
    )
    query_grad = rotate_back(query_grad.astype(f32), cosine, sine_part).reshape(length, head_cols)
    key_grad = rotate_back(key_grad.astype(f32), cosine, sine_part).reshape(length, head_cols)
    query_scaled, key_scaled = query_grad * own_gains[1], key_grad * own_gains[2]
    means = jnp.stack(
        [jnp.sum(query_scaled * query_pre, axis=-1), jnp.sum(key_scaled * key_pre, axis=-1)]
    )
    means = sum_square(means, "seq") / model_width
    query_gain_grad = jnp.sum(query_grad * query_pre * query_inverse, axis=0)
    key_gain_grad = jnp.sum(key_grad * key_pre * key_inverse, axis=0)
    query_pre_grad = query_inverse * query_scaled - query_pre * query_inverse**3 * means[0][:, None]
    key_pre_grad = key_inverse * key_scaled - key_pre * key_inverse**3 * means[1][:, None]
    qkv_grad = jnp.concatenate(
        [query_pre_grad.astype(bf16), key_pre_grad.astype(bf16), value_grad.reshape(length, head_cols)],
        axis=1,
    )
    attn_in_part = jnp.einsum("tc,dc->td", qkv_grad, heads_weight, preferred_element_type=f32)
    first_gain_grad = jnp.sum(attn_in_part * all_inputs * first_inverse, axis=0)
    attn_in_grad = scatter_square(
        attn_in_part.astype(bf16).reshape(seq_count, tok_count, model_width), "seq"
    )
    heads_weight_grad = jnp.einsum("td,tc->dc", attn_low, qkv_grad, preferred_element_type=f32)

    own_inverse = lax.dynamic_slice_in_dim(first_inverse, own_seq * tok_count, tok_count, 0)
    input_norm_grad, _ = rms_back(attn_in_grad, inputs, own_inverse, gains[0])
    input_grad = residual_grad + input_norm_grad

    rows_split = (seq_count, exp_count, core_count, rows_dev)
    heads_terms = heads_weight_grad.astype(bf16).reshape(rows_split + (3 * head_cols,))
    heads_terms = scatter_core(heads_terms, "fsdp", 2)
    heads_terms = scatter_line(split_line(heads_terms, "exp", 1), "exp").astype(bf16)
    grad_w_qkv = lax.all_to_all(
        heads_terms.reshape(seq_count, rows_dev, 3, 1, head_cols), "seq", split_axis=0, concat_axis=3, tiled=True
    ).reshape(rows_dev, 3 * model_width).astype(f32)

    out_terms = out_weight_grad.astype(bf16).reshape(rows_split + (model_width,))
    out_terms = scatter_core(out_terms, "fsdp", 2)
    out_terms = scatter_line(split_line(out_terms, "exp", 1), "exp").astype(bf16)
    grad_w_out = scatter_square(out_terms, "seq")

    zero_row = jnp.zeros((model_width,), f32)
    small_terms = jnp.concatenate(
        [
            jnp.stack(
                [
                    first_gain_grad,
                    lax.dynamic_update_slice_in_dim(zero_row, query_gain_grad, own_seq * head_cols, 0),
                    lax.dynamic_update_slice_in_dim(zero_row, key_gain_grad, own_seq * head_cols, 0),
                    mlp_gain_grad,
                ]
            ),
            router_grad,
        ],
        axis=0,
    ).reshape((-1,) + rows_split)
    small_terms = jnp.transpose(small_terms, (1, 0, 2, 3, 4))
    small_terms = scatter_core(small_terms, "fsdp", 3)
    small_terms = scatter_line(split_line(small_terms, "exp", 2), "exp")
    small_grad = scatter_square(small_terms, "seq").T
    return (
        output[None],
        input_grad[None],
        small_grad[:, :4],
        grad_w_qkv,
        grad_w_out,
        small_grad[:, 4:],
        jnp.transpose(grad_expert_in, (1, 0, 2)).astype(f32),
        jnp.transpose(grad_expert_out, (1, 0, 2)).astype(f32),
    )


def solution(mesh):
    in_specs = (
        P(("exp", "fsdp"), "seq", None),
        P(("exp", "fsdp"), "seq", None),
        P(("exp", "fsdp"), "seq", None),
        P(("exp", "fsdp"), None),
        P(("seq", "exp", "fsdp"), None),
        P(("seq", "exp", "fsdp"), None),
        P(("seq", "exp", "fsdp"), None),
        P(("seq", "exp", "fsdp"), None),
        P(("seq", "fsdp"), "exp", None),
        P(("seq", "fsdp"), "exp", None),
    )
    out_specs = (
        P(("exp", "fsdp"), "seq", None),
        P(("exp", "fsdp"), "seq", None),
        P(("seq", "exp", "fsdp"), None),
        P(("seq", "exp", "fsdp"), None),
        P(("seq", "exp", "fsdp"), None),
        P(("seq", "exp", "fsdp"), None),
        P(("seq", "fsdp"), "exp", None),
        P(("seq", "fsdp"), "exp", None),
    )
    return jax.shard_map(
        on_device, mesh=mesh, in_specs=in_specs, out_specs=out_specs, check_vma=False
    )
```

time: 2800 us -> 1180 us (0.42)
  waiting for transfers between devices: 1800 us -> 372 us
  blocking collectives: 260 us -> 0 us
  starting transfers between devices: 57.3 us -> 228 us
  local copies, waits for them, and re-layouts: 277 us -> 134 us
  other arithmetic: 97 us -> 154 us
    reduce_scatter x4 -> x2, waiting for transfers between devices: 950 us -> 0.01 us  [the longest x1 0.01 us: on_device(): lax.psum_scatter(down_grad.astype(bf16), ('seq', 'fsdp'), scatter_dimensi...]
    all_to_all x8 -> x4, waiting for transfers between devices: 644 us -> 11.6 us  [the longest x1 9.84 us: on_device(): lax.all_to_all(merged_grad.astype(bf16), 'seq', split_axis=1, concat_axis...]
    ppermute x0 -> x106, waiting for transfers between devices: none -> 361 us  [the longest x18 120 us: scatter_line(): lax.ppermute(add(blocks[step], up), axis, [(j, j + 1) for j in range(min(...]
    all_gather x2 -> x0, blocking collectives: 260 us -> none  [the longest x1 227 us: on_device(): lax.all_gather(router, ('seq', 'exp', 'fsdp'), axis=0, tiled=True)]
    ppermute x0 -> x106, starting transfers between devices: none -> 207 us  [the longest x18 60 us: gather_line(): lax.ppermute(up, axis, [(j, j + 1) for j in range(step - 1, count - 1)])]
    all_gather x4 -> x2, waiting for transfers between devices: 115 us -> 0.01 us  [the longest x1 0.01 us: on_device(): lax.all_gather(jnp.transpose(expert_in, (1, 0, 2)), ('seq', 'fsdp'), axis...]
    unnamed x12 -> x4, waiting for transfers between devices: 86.1 us -> 0.07 us
    scatter x1 -> x0, local copies, waits for them, and re-layouts: 54.5 us -> none  [on_device(): outgoing = empty_buffer.at[slot_index].set(mlp_low[token_index])]
  transfers between devices with their start and end apart: 18 -> 114, of which waited for: 13 -> 45; matrix products, arithmetic and copies ran while one was open for 17% -> 38% of each run, Pallas kernels for 0% -> 0%
where the time goes in v1:
time: 1180 us; the launch traced here: 1170 us
  waiting for transfers between devices  372 us (32%)
  matrix products  260 us (22%)
  starting transfers between devices  228 us (19%)
  other arithmetic  154 us (13%)
  local copies, waits for them, and re-layouts  134 us (11%)
  between operations  17.3 us (1%)
    ppermute x18, waiting for transfers between devices, scatter_line(): lax.ppermute(add(blocks[step], up), axis, [(j, j + 1) for j in range(min(...  120 us
    ppermute x18, waiting for transfers between devices, gather_line(): lax.ppermute(down, axis, [(j, j - 1) for j in range(1, count - step + 1)])  107 us
    ppermute x18, waiting for transfers between devices, scatter_line(): lax.ppermute(add(blocks[count - step], down), axis, [(j, j - 1) for j in...  62.9 us
    ppermute x18, starting transfers between devices, gather_line(): lax.ppermute(up, axis, [(j, j + 1) for j in range(step - 1, count - 1)])  60 us
    ppermute x18, starting transfers between devices, gather_line(): lax.ppermute(down, axis, [(j, j - 1) for j in range(1, count - step + 1)])  49.9 us
    unnamed x264, local copies, waits for them, and re-layouts  45.2 us
    ppermute x18, starting transfers between devices, scatter_line(): lax.ppermute(add(blocks[step], up), axis, [(j, j + 1) for j in range(min(...  42.9 us
    dot_general x1, matrix products, on_device(): jnp.einsum('erd,erf->edf', expert_rows, gate_up_grad, preferred_element_t...  34 us
  transfers between devices with their start and end apart: 114, of which 45 were waited for; matrix products, arithmetic and copies ran while one was open for 38% of the time, Pallas kernels for 0%

profile of v1, /device:TPU:10, one launch (start us, length us, event | category | flops | bytes accessed | tf_op | source)
XLA Modules:
  0.0 1166.0 jit_solution(9164097553902039975)
XLA Ops:
  135.6 10.1 collective-permute-done.16
  182.1 23.0 %collective-permute-done.18 = bf16[4,64,1536]{2,1,0:T(8,128)(2,1)} collective-permute-done((bf16[4,64,1536]{2,1,0:T(8,128)(2,1)}, bf16[4,64,1536]{2,1,0:T(8,128)(2,1)}, u32[]{:S(2)}, u32[]{:S(2)}) %collective-permute-start.18) | collective-permute-done | bytes 786464 | tf_op jit(solution)/shard_map/ppermute | solution.py:96
  210.9 9.5 collective-permute-done.2
  244.4 9.3 collective-permute-done.30
  266.7 9.5 collective-permute-done.55
  283.6 14.9 %collective-permute-done.31 = bf16[4,64,2048]{2,1,0:T(8,128)(2,1)S(1)} collective-permute-done((bf16[4,64,2048]{2,1,0:T(8,128)(2,1)S(1)}, bf16[4,64,2048]{2,1,0:T(8,128)(2,1)S(1)}, u32[]{:S(2)}, u32[]{:S(2)}) %collective-permute-start.31) | collective-permute-done | bytes 1048608 | tf_op jit(solution)/shard_map/ppermute | solution.py:96
  371.0 9.6 collective-permute-start.41
  385.4 17.6 %collective-permute-done.41 = bf16[256,2048]{1,0:T(8,128)(2,1)S(1)} collective-permute-done((bf16[256,2048]{1,0:T(8,128)(2,1)S(1)}, bf16[256,2048]{1,0:T(8,128)(2,1)S(1)}, u32[]{:S(2)}, u32[]{:S(2)}) %collective-permute-start.41) | collective-permute-done | bytes 1048608 | tf_op jit(solution)/shard_map/ppermute | solution.py:95
  440.6 18.0 %collective-permute-done.44 = bf16[256,2048]{1,0:T(8,128)(2,1)S(1)} collective-permute-done((bf16[256,2048]{1,0:T(8,128)(2,1)}, bf16[256,2048]{1,0:T(8,128)(2,1)S(1)}, u32[]{:S(2)}, u32[]{:S(2)}) %collective-permute-start.44) | collective-permute-done | bytes 1048608 | tf_op jit(solution)/shard_map/ppermute | solution.py:96
  465.1 9.3 copy.633
  477.5 28.4 %fusion.221 = f32[4,576,2048]{2,1,0:T(8,128)} fusion(bf16[4,576,2048]{2,1,0:T(8,128)(2,1)} %bitcast.630, bf16[4,2048,2048]{2,1,0:T(8,128)(2,1)} %all-gather.3.cloned.1.call-done), kind=kOutput, calls=%fused_computation.525 | convolution fusion | flops 19327352832 | bytes 61865984 | tf_op jit(solution)/shard_map/erd,edf->erf/dot_general | solution.py:368
  506.0 21.5 %multiply_reduce_fusion = (f32[4,576]{1,0:T(4,128)S(1)}, f32[4,576,1024]{2,1,0:T(8,128)}) fusion(f32[4,576,2048]{2,1,0:T(8,128)} %fusion.221, bf16[4,576,2048]{2,1,0:T(8,128)(2,1)} %bitcast.636, bf16[4,2048,1024]{2,1,0:T(8,128)(2,1)} %all-gather.5.cloned.1.call-done), kind=kOutput, calls=%fused_computation.8 | convolution fusion | flops 9680189440 | bytes 54535168 | tf_op jit(solution)/shard_map/erd,edf->erf/dot_general | solution.py:380
  529.2 18.1 %multiply_convert_fusion.1 = (bf16[4,576,1024]{2,1,0:T(8,128)(2,1)}, bf16[4,576,1024]{2,1,0:T(8,128)(2,1)}, bf16[4,576,1024]{2,1,0:T(8,128)(2,1)}) fusion(f32[4,576,2048]{2,1,0:T(8,128)} %fusion.221, f32[4,576,1024]{2,1,0:T(8,128)} %get-tuple-element.247, f32[4,576]{1,0:T(4,128)S(1)} %mul.722), kind=kLoop, calls=%fused_computation.10 | loop fusion | flops 40108032 | bytes 42476544 | tf_op jit(solution)/shard_map/convert.26
  547.3 20.4 %convolution_convert_fusion.1 = bf16[4,2048,1024]{2,1,0:T(8,128)(2,1)} fusion(bf16[4,576,2048]{2,1,0:T(8,128)(2,1)} %bitcast.637, bf16[4,576,1024]{2,1,0:T(8,128)(2,1)} %get-tuple-element.94), kind=kOutput, calls=%fused_computation.2 | convolution fusion | flops 9672065024 | bytes 30932992 | tf_op jit(solution)/shard_map/erd,erf->edf/dot_general | solution.py:390
  569.4 34.0 %convolution_convert_fusion = bf16[4,2048,2048]{2,1,0:T(8,128)(2,1)} fusion(bf16[4,576,2048]{2,1,0:T(8,128)(2,1)} %bitcast.631, bf16[4,576,1024]{2,1,0:T(8,128)(2,1)} %get-tuple-element.93, bf16[4,576,1024]{2,1,0:T(8,128)(2,1)} %get-tuple-element.92), kind=kOutput, calls=%fused_computation.1 | convolution fusion | flops 19363004416 | bytes 52428800 | tf_op jit(solution)/shard_map/erd,erf->edf/dot_general | solution.py:399
  604.7 27.5 %fusion.16 = bf16[4,576,2048]{2,1,0:T(8,128)(2,1)} fusion(bf16[4,2048,2048]{2,1,0:T(8,128)(2,1)} %all-gather.3.cloned.1.call-done, bf16[4,576,1024]{2,1,0:T(8,128)(2,1)} %get-tuple-element.93, bf16[4,576,1024]{2,1,0:T(8,128)(2,1)} %get-tuple-element.92), kind=kOutput, calls=%fused_computation.41 | convolution fusion | flops 19350945792 | bytes 52428800 | tf_op jit(solution)/shard_map/erf,edf->erd/dot_general | solution.py:394
  645.5 16.6 %convolution_convert_fusion.4 = bf16[4,576,2048]{2,1,0:T(8,128)(2,1)} fusion(bf16[4,576,1024]{2,1,0:T(8,128)(2,1)} %get-tuple-element.94, bf16[4,2048,1024]{2,1,0:T(8,128)(2,1)} %all-gather.5.cloned.1.call-done), kind=kOutput, calls=%fused_computation.40 | convolution fusion | flops 9668395008 | bytes 30932992 | tf_op jit(solution)/shard_map/erf,edf->erd/dot_general | solution.py:374
  678.2 21.0 %collective-permute-done.47 = bf16[256,2048]{1,0:T(8,128)(2,1)S(1)} collective-permute-done((bf16[256,2048]{1,0:T(8,128)(2,1)S(1)}, bf16[256,2048]{1,0:T(8,128)(2,1)S(1)}, u32[]{:S(2)}, u32[]{:S(2)}) %collective-permute-start.47) | collective-permute-done | bytes 1048608 | tf_op jit(solution)/shard_map/ppermute | solution.py:113
  702.4 19.6 %collective-permute-done.65 = f32[16,256]{1,0:T(8,128)S(1)} collective-permute-done((f32[16,256]{1,0:T(8,128)S(1)}, f32[16,256]{1,0:T(8,128)S(1)}, u32[]{:S(2)}, u32[]{:S(2)}) %collective-permute-start.65) | collective-permute-done | bytes 16416 | tf_op jit(solution)/shard_map/ppermute | solution.py:113
  759.2 13.9 %collective-permute-done.70 = f32[16,256]{1,0:T(8,128)S(1)} collective-permute-done((f32[16,256]{1,0:T(8,128)S(1)}, f32[16,256]{1,0:T(8,128)S(1)}, u32[]{:S(2)}, u32[]{:S(2)}) %collective-permute-start.70) | collective-permute-done | bytes 16416 | tf_op jit(solution)/shard_map/ppermute | solution.py:116
  777.1 9.4 collective-permute-done.52
  815.7 9.8 all-to-all-done.2
  876.8 24.1 %fusion.11 = (f32[2048]{0:T(1024)S(1)}, bf16[1024,2048]{1,0:T(8,128)(2,1)}, bf16[1024,2048]{1,0:T(8,128)(2,1)}) fusion(bf16[4,256,2048]{2,1,0:T(8,128)(2,1)} %fusion.112, f32[1024]{0:T(1024)S(1)} %bitcast.713, f32[2048]{0:T(1024)S(1)} %copy-done.79, bf16[2048,1536]{1,0:T(8,128)(2,1)} %bitcast.644, bf16[256,512]{1,0:T(8,128)(2,1)S(1)} %copy.721, ...), kind=kOutput, calls=%fused_computation.28 | convolution fusion | flops 6478100480 | bytes 22040576 | tf_op jit(solution)/shard_map/tc,dc->td/dot_general | solution.py:448
  900.8 13.0 %convolution_convert_fusion.3 = bf16[2048,1536]{1,0:T(8,128)(2,1)S(1)} fusion(bf16[1024,2048]{1,0:T(8,128)(2,1)} %get-tuple-element.113, bf16[256,512]{1,0:T(8,128)(2,1)S(1)} %copy.721, bf16[256,512]{1,0:T(8,128)(2,1)S(1)} %copy.720, bf16[256,512]{1,0:T(8,128)(2,1)S(1)} %copy.719, bf16[256,512]{1,0:T(8,128)(2,1)S(1)} %copy.718, ...), kind=kOutput, calls=%fused_computation.35 | convolution fusion | flops 6464471040 | bytes 13631488 | tf_op jit(solution)/shard_map/td,tc->dc/dot_general | solution.py:453
  955.6 13.7 %collective-permute-done.89 = bf16[4,64,1536]{2,1,0:T(8,128)(2,1)S(1)} collective-permute-done((bf16[4,64,1536]{2,1,0:T(8,128)(2,1)S(1)}, bf16[4,64,1536]{2,1,0:T(8,128)(2,1)S(1)}, u32[]{:S(2)}, u32[]{:S(2)}) %collective-permute-start.89) | collective-permute-done | bytes 786464 | tf_op jit(solution)/shard_map/ppermute | solution.py:113
  971.5 20.3 %collective-permute-done.96 = bf16[4,64,2048]{2,1,0:T(8,128)(2,1)S(1)} collective-permute-done((bf16[4,64,2048]{2,1,0:T(8,128)(2,1)S(1)}, bf16[4,64,2048]{2,1,0:T(8,128)(2,1)S(1)}, u32[]{:S(2)}, u32[]{:S(2)}) %collective-permute-start.96) | collective-permute-done | bytes 1048608 | tf_op jit(solution)/shard_map/ppermute | solution.py:113
  997.7 11.0 collective-permute-done.90
  1009.8 18.4 %collective-permute-done.97 = bf16[4,64,2048]{2,1,0:T(8,128)(2,1)S(1)} collective-permute-done((bf16[4,64,2048]{2,1,0:T(8,128)(2,1)S(1)}, bf16[4,64,2048]{2,1,0:T(8,128)(2,1)S(1)}, u32[]{:S(2)}, u32[]{:S(2)}) %collective-permute-start.97) | collective-permute-done | bytes 1048608 | tf_op jit(solution)/shard_map/ppermute | solution.py:113
  1038.6 16.1 %collective-permute-done.75 = bf16[2,128,2048]{2,1,0:T(8,128)(2,1)S(1)} collective-permute-done((bf16[2,128,2048]{2,1,0:T(8,128)(2,1)S(1)}, bf16[2,128,2048]{2,1,0:T(8,128)(2,1)S(1)}, u32[]{:S(2)}, u32[]{:S(2)}) %collective-permute-start.75) | collective-permute-done | bytes 1048608 | tf_op jit(solution)/shard_map/ppermute | solution.py:70
  1062.1 12.5 %collective-permute-done.100 = bf16[4,64,2048]{2,1,0:T(8,128)(2,1)S(1)} collective-permute-done((bf16[4,64,2048]{2,1,0:T(8,128)(2,1)S(1)}, bf16[4,64,2048]{2,1,0:T(8,128)(2,1)S(1)}, u32[]{:S(2)}, u32[]{:S(2)}) %collective-permute-start.100) | collective-permute-done | bytes 1048608 | tf_op jit(solution)/shard_map/ppermute | solution.py:116
  1081.8 15.1 %collective-permute-done.94 = bf16[4,64,1536]{2,1,0:T(8,128)(2,1)S(1)} collective-permute-done((bf16[4,64,1536]{2,1,0:T(8,128)(2,1)S(1)}, bf16[4,64,1536]{2,1,0:T(8,128)(2,1)S(1)}, u32[]{:S(2)}, u32[]{:S(2)}) %collective-permute-start.94) | collective-permute-done | bytes 786464 | tf_op jit(solution)/shard_map/ppermute | solution.py:116
  1147.1 12.2 %copy.687 = f32[256,4,2048]{2,1,0:T(4,128)} copy(f32[256,4,2048]{2,0,1:T(8,128)} %convert_bitcast_fusion.2) | data formatting | bytes 16777216
  (761 shorter events, 621.1 us)
Async XLA Ops:
  7.2 470.4 %all-gather.3.cloned.1.call-start = ((), (), s32[]{:S(2)}) async-start(), calls=%async_computation.6 | async-start | bytes 37748736 | tf_op jit(solution)/shard_map/all_gather | solution.py:304
  14.6 59.6 %collective-permute-start.35 = (f32[16,256]{1,0:T(8,128)S(1)}, f32[16,256]{1,0:T(8,128)}, u32[]{:S(2)}, u32[]{:S(2)}) collective-permute-start(f32[16,256]{1,0:T(8,128)S(1)} %convolution_select_fusion), channel_id=1, source_target_pairs={{0,2},{2,4},{4,6},{1,3},{3,5},{5,7},{8,10},{10,12},{12,14},{9,11},... | collective-permute-start | bytes 49160 | tf_op jit(solution)/shard_map/ppermute | solution.py:95
  18.1 56.6 %collective-permute-start.36 = (f32[16,256]{1,0:T(8,128)S(1)}, f32[16,256]{1,0:T(8,128)}, u32[]{:S(2)}, u32[]{:S(2)}) collective-permute-start(f32[16,256]{1,0:T(8,128)S(1)} %convolution_select_fusion), channel_id=1, source_target_pairs={{2,0},{4,2},{6,4},{3,1},{5,3},{7,5},{10,8},{12,10},{14,12},{11,9},... | collective-permute-start | bytes 49160 | tf_op jit(solution)/shard_map/ppermute | solution.py:96
  22.5 129.8 %collective-permute-start.1 = (bf16[128,2048]{1,0:T(8,128)(2,1)}, bf16[128,2048]{1,0:T(8,128)(2,1)}, u32[]{:S(2)}, u32[]{:S(2)}) collective-permute-start(bf16[128,2048]{1,0:T(8,128)(2,1)} %get-tuple-element.171), channel_id=1, source_target_pairs={{0,16},{8,24},{16,0},{24,8},{1,17},{9,25},{17,1},{25,9},{2,18},{10... | collective-permute-start | bytes 1572872 | tf_op jit(solution)/shard_map/ppermute | solution.py:39
  26.7 89.1 %all-to-all-start = ((bf16[64,3,4,512]{3,0,1,2:T(8,128)(2,1)}), bf16[64,3,4,512]{3,0,1,2:T(8,128)(2,1)S(1)}, u32[]{:S(2)}, u32[]{:S(2)}) async-start(bf16[64,3,4,512]{3,0,1,2:T(8,128)(2,1)} %copy.609), calls=%async_computation | async-start | bytes 1572864 | tf_op jit(solution)/shard_map/all_to_all | solution.py:294
  31.8 474.2 %all-gather.5.cloned.1.call-start = ((), (), s32[]{:S(2)}) async-start(), calls=%async_computation.7 | async-start | bytes 18874368 | tf_op jit(solution)/shard_map/all_gather | solution.py:307
  74.2 99.1 %collective-permute-start = (bf16[128,2048]{1,0:T(8,128)(2,1)}, bf16[128,2048]{1,0:T(8,128)(2,1)}, u32[]{:S(2)}, u32[]{:S(2)}) collective-permute-start(bf16[128,2048]{1,0:T(8,128)(2,1)} %get-tuple-element.170), channel_id=1, source_target_pairs={{0,8},{8,0},{16,24},{24,16},{1,9},{9,1},{17,25},{25,17},{2,10},{10... | collective-permute-start | bytes 1572872 | tf_op jit(solution)/shard_map/ppermute | solution.py:38
  101.2 107.4 %collective-permute-start.53 = (bf16[256,2048]{1,0:T(8,128)(2,1)}, bf16[256,2048]{1,0:T(8,128)(2,1)}, u32[]{:S(2)}, u32[]{:S(2)}) collective-permute-start(bf16[256,2048]{1,0:T(8,128)(2,1)} %bitcast.115), channel_id=1, source_target_pairs={{0,2},{2,4},{4,6},{1,3},{3,5},{5,7},{8,10},{10,12},{12,14},{9,11},... | collective-permute-start | bytes 3145736 | tf_op jit(solution)/shard_map/ppermute | solution.py:95
  152.3 79.7 %collective-permute-start.54 = (bf16[256,2048]{1,0:T(8,128)(2,1)}, bf16[256,2048]{1,0:T(8,128)(2,1)}, u32[]{:S(2)}, u32[]{:S(2)}) collective-permute-start(bf16[256,2048]{1,0:T(8,128)(2,1)} %bitcast.115), channel_id=1, source_target_pairs={{2,0},{4,2},{6,4},{3,1},{5,3},{7,5},{10,8},{12,10},{14,12},{11,9},... | collective-permute-start | bytes 3145736 | tf_op jit(solution)/shard_map/ppermute | solution.py:96
  168.1 37.0 %collective-permute-start.18 = (bf16[4,64,1536]{2,1,0:T(8,128)(2,1)}, bf16[4,64,1536]{2,1,0:T(8,128)(2,1)}, u32[]{:S(2)}, u32[]{:S(2)}) collective-permute-start(bf16[4,64,1536]{2,1,0:T(8,128)(2,1)} %collective-permute-done.17), channel_id=1, source_target_pairs={{2,0},{3,1},{10,8},{11,9},{18,16},{19,17},{26,24},{27,25}} | collective-permute-start | bytes 2359304 | tf_op jit(solution)/shard_map/ppermute | solution.py:96
  173.3 52.0 %collective-permute-start.29 = (bf16[4,64,2048]{2,1,0:T(8,128)(2,1)S(1)}, bf16[4,64,2048]{2,1,0:T(8,128)(2,1)}, u32[]{:S(2)}, u32[]{:S(2)}) collective-permute-start(bf16[4,64,2048]{2,1,0:T(8,128)(2,1)S(1)} %fusion.147), channel_id=1, source_target_pairs={{2,0},{4,2},{6,4},{3,1},{5,3},{7,5},{10,8},{12,10},{14,12},{11,9},... | collective-permute-start | bytes 3145736 | tf_op jit(solution)/shard_map/ppermute | solution.py:96
  180.6 39.8 %collective-permute-start.2 = (bf16[2,128,2048]{2,1,0:T(8,128)(2,1)S(1)}, bf16[2,128,2048]{2,1,0:T(8,128)(2,1)S(1)}, u32[]{:S(2)}, u32[]{:S(2)}) collective-permute-start(bf16[2,128,2048]{2,1,0:T(8,128)(2,1)S(1)} %copy-done.61), channel_id=1, source_target_pairs={{0,8},{8,0},{16,24},{24,16},{1,9},{9,1},{17,25},{25,17},{2,10},{10... | collective-permute-start | bytes 3145736 | tf_op jit(solution)/shard_map/ppermute | solution.py:41
  220.4 79.6 %collective-permute-start.21 = (bf16[4,4,64,1536]{3,2,1,0:T(8,128)(2,1)S(1)}, bf16[4,4,64,1536]{3,2,1,0:T(8,128)(2,1)S(1)}, u32[]{:S(2)}, u32[]{:S(2)}) collective-permute-start(bf16[4,4,64,1536]{3,2,1,0:T(8,128)(2,1)S(1)} %bitcast_dynamic-update-slice_fusion.4), channel_id=1, source_target_pairs={{0,1},{1,0},{2,3},{3,2},{4,5},{5,4},{6,7},{7,6},{8,9},{9,8},{10,11... | collective-permute-start | bytes 9437192 | tf_op jit(solution)/shard_map/ppermute | solution.py:148
  234.3 41.9 %collective-permute-start.55 = (bf16[256,2048]{1,0:T(8,128)(2,1)}, bf16[256,2048]{1,0:T(8,128)(2,1)}, u32[]{:S(2)}, u32[]{:S(2)}) collective-permute-start(bf16[256,2048]{1,0:T(8,128)(2,1)} %collective-permute-done.54), channel_id=1, source_target_pairs={{2,0},{4,2},{3,1},{5,3},{10,8},{12,10},{11,9},{13,11},{18,16},{20,... | collective-permute-start | bytes 3145736 | tf_op jit(solution)/shard_map/ppermute | solution.py:96
  236.2 45.4 %collective-permute-start.32 = (bf16[4,64,2048]{2,1,0:T(8,128)(2,1)S(1)}, bf16[4,64,2048]{2,1,0:T(8,128)(2,1)S(1)}, u32[]{:S(2)}, u32[]{:S(2)}) collective-permute-start(bf16[4,64,2048]{2,1,0:T(8,128)(2,1)S(1)} %collective-permute-done.28), channel_id=1, source_target_pairs={{2,4},{4,6},{3,5},{5,7},{10,12},{12,14},{11,13},{13,15},{18,20},{2... | collective-permute-start | bytes 3145736 | tf_op jit(solution)/shard_map/ppermute | solution.py:95
  253.7 44.8 %collective-permute-start.31 = (bf16[4,64,2048]{2,1,0:T(8,128)(2,1)S(1)}, bf16[4,64,2048]{2,1,0:T(8,128)(2,1)S(1)}, u32[]{:S(2)}, u32[]{:S(2)}) collective-permute-start(bf16[4,64,2048]{2,1,0:T(8,128)(2,1)S(1)} %collective-permute-done.30), channel_id=1, source_target_pairs={{2,0},{3,1},{10,8},{11,9},{18,16},{19,17},{26,24},{27,25}} | collective-permute-start | bytes 3145736 | tf_op jit(solution)/shard_map/ppermute | solution.py:96
  265.0 119.0 %collective-permute-start.58 = (bf16[256,2048]{1,0:T(8,128)(2,1)}, bf16[256,2048]{1,0:T(8,128)(2,1)}, u32[]{:S(2)}, u32[]{:S(2)}) collective-permute-start(bf16[256,2048]{1,0:T(8,128)(2,1)} %collective-permute-done.57), channel_id=1, source_target_pairs={{4,6},{5,7},{12,14},{13,15},{20,22},{21,23},{28,30},{29,31}} | collective-permute-start | bytes 3145736 | tf_op jit(solution)/shard_map/ppermute | solution.py:95
  276.2 132.3 %collective-permute-start.56 = (bf16[256,2048]{1,0:T(8,128)(2,1)}, bf16[256,2048]{1,0:T(8,128)(2,1)}, u32[]{:S(2)}, u32[]{:S(2)}) collective-permute-start(bf16[256,2048]{1,0:T(8,128)(2,1)} %collective-permute-done.55), channel_id=1, source_target_pairs={{2,0},{3,1},{10,8},{11,9},{18,16},{19,17},{26,24},{27,25}} | collective-permute-start | bytes 3145736 | tf_op jit(solution)/shard_map/ppermute | solution.py:96
  349.7 784.1 %reduce-scatter.5.cloned.1.call-start = ((), (), s32[]{:S(2)}) async-start(), calls=%async_computation.9 | async-start | bytes 18874368 | tf_op jit(solution)/shard_map/reduce_scatter | solution.py:391
  567.7 572.8 %reduce-scatter.3.cloned.1.call-start = ((), (), s32[]{:S(2)}) async-start(), calls=%async_computation.8 | async-start | bytes 37748736 | tf_op jit(solution)/shard_map/reduce_scatter | solution.py:400
  673.0 54.9 %collective-permute-start.60 = (bf16[256,2048]{1,0:T(8,128)(2,1)S(1)}, bf16[256,2048]{1,0:T(8,128)(2,1)S(1)}, u32[]{:S(2)}, u32[]{:S(2)}) collective-permute-start(bf16[256,2048]{1,0:T(8,128)(2,1)S(1)} %get-tuple-element.124), channel_id=1, source_target_pairs={{0,2},{2,4},{1,3},{3,5},{8,10},{10,12},{9,11},{11,13},{16,18},{18,... | collective-permute-start | bytes 3145736 | tf_op jit(solution)/shard_map/ppermute | solution.py:113
  675.6 53.8 %collective-permute-start.63 = (bf16[256,2048]{1,0:T(8,128)(2,1)S(1)}, bf16[256,2048]{1,0:T(8,128)(2,1)S(1)}, u32[]{:S(2)}, u32[]{:S(2)}) collective-permute-start(bf16[256,2048]{1,0:T(8,128)(2,1)S(1)} %get-tuple-element.125), channel_id=1, source_target_pairs={{4,2},{6,4},{5,3},{7,5},{12,10},{14,12},{13,11},{15,13},{20,18},{2... | collective-permute-start | bytes 3145736 | tf_op jit(solution)/shard_map/ppermute | solution.py:116
  676.9 45.1 %collective-permute-start.65 = (f32[16,256]{1,0:T(8,128)S(1)}, f32[16,256]{1,0:T(8,128)S(1)}, u32[]{:S(2)}, u32[]{:S(2)}) collective-permute-start(f32[16,256]{1,0:T(8,128)S(1)} %get-tuple-element.193), channel_id=1, source_target_pairs={{0,2},{1,3},{8,10},{9,11},{16,18},{17,19},{24,26},{25,27}} | collective-permute-start | bytes 49160 | tf_op jit(solution)/shard_map/ppermute | solution.py:113
  700.5 51.8 %collective-permute-start.48 = (bf16[256,2048]{1,0:T(8,128)(2,1)S(1)}, bf16[256,2048]{1,0:T(8,128)(2,1)S(1)}, u32[]{:S(2)}, u32[]{:S(2)}) collective-permute-start(bf16[256,2048]{1,0:T(8,128)(2,1)S(1)} %get-tuple-element.130), channel_id=1, source_target_pairs={{0,2},{2,4},{1,3},{3,5},{8,10},{10,12},{9,11},{11,13},{16,18},{18,... | collective-permute-start | bytes 3145736 | tf_op jit(solution)/shard_map/ppermute | solution.py:113
  730.2 44.9 %collective-permute-start.64 = (bf16[256,2048]{1,0:T(8,128)(2,1)S(1)}, bf16[256,2048]{1,0:T(8,128)(2,1)S(1)}, u32[]{:S(2)}, u32[]{:S(2)}) collective-permute-start(bf16[256,2048]{1,0:T(8,128)(2,1)S(1)} %get-tuple-element.123), channel_id=1, source_target_pairs={{2,0},{4,2},{6,4},{3,1},{5,3},{7,5},{10,8},{12,10},{14,12},{11,9},... | collective-permute-start | bytes 3145736 | tf_op jit(solution)/shard_map/ppermute | solution.py:116
  815.7 132.6 %collective-permute-start.95 = (bf16[4,4,64,2048]{3,2,0,1:T(8,128)(2,1)}, bf16[4,4,64,2048]{3,2,0,1:T(8,128)(2,1)}, u32[]{:S(2)}, u32[]{:S(2)}) collective-permute-start(bf16[4,4,64,2048]{3,2,0,1:T(8,128)(2,1)} %bitcast.624), channel_id=1, source_target_pairs={{0,1},{1,0},{2,3},{3,2},{4,5},{5,4},{6,7},{7,6},{8,9},{9,8},{10,11... | collective-permute-start | bytes 12582920 | tf_op jit(solution)/shard_map/ppermute | solution.py:161
  952.7 39.1 %collective-permute-start.96 = (bf16[4,64,2048]{2,1,0:T(8,128)(2,1)S(1)}, bf16[4,64,2048]{2,1,0:T(8,128)(2,1)S(1)}, u32[]{:S(2)}, u32[]{:S(2)}) collective-permute-start(bf16[4,64,2048]{2,1,0:T(8,128)(2,1)S(1)} %dynamic-slice_bitcast_fusion), channel_id=1, source_target_pairs={{0,2},{1,3},{8,10},{9,11},{16,18},{17,19},{24,26},{25,27}} | collective-permute-start | bytes 3145736 | tf_op jit(solution)/shard_map/ppermute | solution.py:113
  954.4 41.2 %collective-permute-start.84 = (f32[2,10,64]{2,1,0:T(8,128)S(1)}, f32[2,10,64]{2,1,0:T(8,128)S(1)}, u32[]{:S(2)}, u32[]{:S(2)}) collective-permute-start(f32[2,10,64]{2,1,0:T(8,128)S(1)} %pad_maximum_fusion.26), channel_id=1, source_target_pairs={{0,16},{8,24},{16,0},{24,8},{1,17},{9,25},{17,1},{25,9},{2,18},{10... | collective-permute-start | bytes 15368 | tf_op jit(solution)/shard_map/ppermute | solution.py:69
  969.6 39.1 %collective-permute-start.90 = (bf16[4,64,1536]{2,1,0:T(8,128)(2,1)S(1)}, bf16[4,64,1536]{2,1,0:T(8,128)(2,1)S(1)}, u32[]{:S(2)}, u32[]{:S(2)}) collective-permute-start(bf16[4,64,1536]{2,1,0:T(8,128)(2,1)S(1)} %fusion.64), channel_id=1, source_target_pairs={{0,2},{2,4},{1,3},{3,5},{8,10},{10,12},{9,11},{11,13},{16,18},{18,... | collective-permute-start | bytes 2359304 | tf_op jit(solution)/shard_map/ppermute | solution.py:113
  994.3 44.3 %collective-permute-start.73 = (bf16[2,128,2048]{2,1,0:T(8,128)(2,1)S(1)}, bf16[2,128,2048]{2,1,0:T(8,128)(2,1)S(1)}, u32[]{:S(2)}, u32[]{:S(2)}) collective-permute-start(bf16[2,128,2048]{2,1,0:T(8,128)(2,1)S(1)} %pad_maximum_fusion.11), channel_id=1, source_target_pairs={{0,16},{8,24},{16,0},{24,8},{1,17},{9,25},{17,1},{25,9},{2,18},{10... | collective-permute-start | bytes 3145736 | tf_op jit(solution)/shard_map/ppermute | solution.py:69
  1036.1 38.5 %collective-permute-start.100 = (bf16[4,64,2048]{2,1,0:T(8,128)(2,1)S(1)}, bf16[4,64,2048]{2,1,0:T(8,128)(2,1)S(1)}, u32[]{:S(2)}, u32[]{:S(2)}) collective-permute-start(bf16[4,64,2048]{2,1,0:T(8,128)(2,1)S(1)} %fusion.37), channel_id=1, source_target_pairs={{4,2},{6,4},{5,3},{7,5},{12,10},{14,12},{13,11},{15,13},{20,18},{2... | collective-permute-start | bytes 3145736 | tf_op jit(solution)/shard_map/ppermute | solution.py:116
  1059.2 50.2 %collective-permute-start.98 = (bf16[4,64,2048]{2,1,0:T(8,128)(2,1)}, bf16[4,64,2048]{2,1,0:T(8,128)(2,1)}, u32[]{:S(2)}, u32[]{:S(2)}) collective-permute-start(bf16[4,64,2048]{2,1,0:T(8,128)(2,1)} %get-tuple-element.84), channel_id=1, source_target_pairs={{0,2},{2,4},{4,6},{1,3},{3,5},{5,7},{8,10},{10,12},{12,14},{9,11},... | collective-permute-start | bytes 3145736 | tf_op jit(solution)/shard_map/ppermute | solution.py:113
  (209 other events, 3226.9 us)
Sparse Core Ops, SparseCore 0:
  13.9 203.8 all-gather.2
  219.7 94.0 all-gather.4
  567.9 114.9 reduce-scatter.4
  686.3 216.6 reduce-scatter.2

commit v2 on v1

v2 whole, which is shorter than its diff:
```python
import functools

import jax
import jax.numpy as jnp
from jax import lax
from jax.experimental import pallas as pl
from jax.experimental.pallas import tpu as pltpu
from jax.sharding import PartitionSpec as P

HEADS = 16
HEAD_DIM = 128
FF = 1024
TOP = 8
ATT_BLOCK = 256


epsilon = 1e-05
rotary_base = 10000.0
highest = lax.Precision.HIGHEST
f32 = jnp.float32
bf16 = jnp.bfloat16
VMEM_BYTES = 63 * 1024 * 1024
KERNEL_PARAMS = pltpu.CompilerParams(vmem_limit_bytes=VMEM_BYTES)
SMALL_COST = pl.CostEstimate(flops=1, bytes_accessed=1, transcendentals=0)
DOWN_GRAD_COST = pl.CostEstimate(flops=10**11, bytes_accessed=1, transcendentals=0)
ATTEND_BACK_COST = pl.CostEstimate(flops=345 * 10**9, bytes_accessed=1, transcendentals=0)


def after(value, other):
    first = lax.slice(other, (0,) * other.ndim, (1,) * other.ndim).reshape(())
    return value + (0.0 * first.astype(f32)).astype(value.dtype)


def swap_pairs(count, mask):
    return [(i, i ^ mask) for i in range(count)]


def shift_pairs(count, step):
    return [(i, (i + step) % count) for i in range(count)]


def ring_place(index, count):
    return index & (count - 1) if count & (count - 1) == 0 else lax.rem(index + count, count)


def exchange(stacked, axis, split_axis=0):
    return lax.all_to_all(stacked, axis, split_axis=split_axis, concat_axis=split_axis, tiled=True)


def gather_near(block, axis):
    count = lax.axis_size(axis)
    return [block] + [
        lax.ppermute(block, axis, shift_pairs(count, k)) for k in range(1, count)
    ]


def send_near(blocks, axis):
    count = lax.axis_size(axis)
    return [blocks[0]] + [
        lax.ppermute(blocks[k], axis, shift_pairs(count, -k)) for k in range(1, count)
    ]


def add_up(blocks):
    return sum(block.astype(f32) for block in blocks)


def order(blocks, axis, out_axis=0, sign=-1):
    count = lax.axis_size(axis)
    own = lax.axis_index(axis)
    shape = blocks[0].shape[:out_axis] + (count,) + blocks[0].shape[out_axis:]
    out = jnp.zeros(shape, blocks[0].dtype)
    for k, block in enumerate(blocks):
        place = ring_place(own + sign * k, count)
        out = lax.dynamic_update_index_in_dim(out, block, place, out_axis)
    return out


def split(stacked, axis, in_axis=0, sign=-1):
    count = lax.axis_size(axis)
    own = lax.axis_index(axis)
    return [
        lax.dynamic_index_in_dim(
            stacked, ring_place(own + sign * k, count), in_axis, keepdims=False
        )
        for k in range(count)
    ]


def gather(block, axis, out_axis=0):
    return order(gather_near(block, axis), axis, out_axis)


def scatter(stacked, axis, split_axis=0):
    return add_up(send_near(split(stacked, axis, split_axis), axis))


def sum_all(value, axis):
    return add_up(gather_near(value, axis))


def assemble_kernel(groups, parts, place_ref, *refs):
    sources, out_ref, sems = refs[: len(refs) - 2], refs[-2], refs[-1]
    rows = sources[0].shape[0] // groups
    copies = []
    for k, source in enumerate(sources):
        for group in range(groups):
            target = pl.multiple_of((group * parts + place_ref[k]) * rows, rows)
            copies.append(
                pltpu.make_async_copy(
                    source.at[pl.ds(group * rows, rows)],
                    out_ref.at[pl.ds(target, rows)],
                    sems.at[k, group],
                )
            )
    for copy in copies:
        copy.start()
    for copy in copies:
        copy.wait()


def assemble(blocks, places, groups):
    parts = len(blocks)
    return pl.pallas_call(
        functools.partial(assemble_kernel, groups, parts),
        in_specs=[pl.BlockSpec(memory_space=pltpu.SMEM)]
        + [pl.BlockSpec(memory_space=pltpu.VMEM)] * parts,
        out_specs=pl.BlockSpec(memory_space=pl.ANY),
        out_shape=jax.ShapeDtypeStruct(
            (parts * blocks[0].shape[0], blocks[0].shape[1]), blocks[0].dtype
        ),
        scratch_shapes=[pltpu.SemaphoreType.DMA((parts, groups))],
        compiler_params=KERNEL_PARAMS,
        cost_estimate=SMALL_COST,
        name="assemble",
    )(places, *blocks)


def order_cores(blocks, groups, axis, core_axis):
    count, cores = lax.axis_size(axis), lax.axis_size(core_axis)
    own, own_core = lax.axis_index(axis), lax.axis_index(core_axis)
    if cores == 2:
        blocks = blocks + [lax.ppermute(block, core_axis, swap_pairs(2, 1)) for block in blocks]
        core_places = [own_core, 1 - own_core]
    else:
        every = lax.all_gather(jnp.stack(blocks), core_axis, axis=0)
        blocks = [every[core, k] for core in range(cores) for k in range(count)]
        core_places = list(range(cores))
    places = [
        ring_place(own - k, count) * cores + core for core in core_places for k in range(count)
    ]
    places = jnp.stack([jnp.asarray(place, jnp.int32) for place in places])
    return assemble(blocks, places, groups)


def scatter_core(stacked, axis):
    if lax.axis_size(axis) != 2:
        return lax.psum_scatter(stacked, axis, scatter_dimension=0, tiled=False)
    own = lax.axis_index(axis)
    kept = lax.dynamic_index_in_dim(stacked, own, 0, keepdims=False)
    given = lax.dynamic_index_in_dim(stacked, 1 - own, 0, keepdims=False)
    received = lax.ppermute(given, axis, swap_pairs(2, 1))
    return (kept.astype(f32) + received.astype(f32)).astype(stacked.dtype)


def rms_inverse(values):
    return lax.rsqrt(jnp.mean(values * values, axis=-1, keepdims=True) + epsilon)


def rms_back(gradient, values, inverse, gain_vector):
    scaled = gradient * gain_vector
    gain_grad = jnp.sum(gradient * values * inverse, axis=0)
    value_grad = inverse * scaled - values * inverse**3 * jnp.mean(
        scaled * values, axis=-1, keepdims=True
    )
    return (value_grad, gain_grad)


def rotary_tables(position, head_dim):
    half_dim = head_dim // 2
    exponent = jnp.arange(half_dim, dtype=f32) * (2.0 / head_dim)
    angles = position.astype(f32)[:, None] * (rotary_base ** (-exponent))[None, :]
    cosine, sine_part = jnp.cos(angles), jnp.sin(angles)
    return jnp.stack(
        [
            jnp.concatenate([cosine, cosine], axis=1),
            jnp.concatenate([-sine_part, sine_part], axis=1),
        ]
    )


def dot(one, other, one_axis, other_axis):
    return lax.dot_general(
        one, other, (((one_axis,), (other_axis,)), ((), ())), preferred_element_type=f32
    )


def turn(values, cosines, sines):
    return values * cosines + pltpu.roll(values, HEAD_DIM // 2, 1) * sines


def block_probs(query_rows, keys, query_segment, key_segment, scale):
    scores = dot(query_rows, keys, 1, 1) * scale
    scores = jnp.where(query_segment == key_segment, scores, -jnp.inf)
    terms = jnp.exp(scores - jnp.max(scores, axis=1, keepdims=True))
    return terms / jnp.sum(terms, axis=1, keepdims=True)


def attend_kernel(
    query_ref, key_ref, value_ref, scale_ref, gain_ref, turn_ref, row_seg_ref, col_seg_ref,
    out_ref, query_low_ref, key_low_ref, value_low_ref,
):
    length = query_ref.shape[0]
    cosines, sines = turn_ref[0], turn_ref[1]
    query = query_ref[...] * scale_ref[:, 0:1] * gain_ref[0:1, :]
    key = key_ref[...] * scale_ref[:, 1:2] * gain_ref[1:2, :]
    query_low_ref[...] = turn(query, cosines, sines).astype(bf16)
    key_low_ref[...] = turn(key, cosines, sines).astype(bf16)
    value_low_ref[...] = value_ref[...].astype(bf16)
    for start in range(0, length, ATT_BLOCK):
        stop = start + ATT_BLOCK
        probs = block_probs(
            query_low_ref[start:stop],
            key_low_ref[:stop],
            row_seg_ref[start:stop, 0:1],
            col_seg_ref[0:1, :stop],
            HEAD_DIM ** (-0.5),
        )
        out = dot(probs.astype(bf16), value_low_ref[:stop], 1, 0)
        out_ref[start:stop] = out.astype(bf16)


def attend(projected, scales, gains, turns, row_segment, col_segment, heads):
    length = projected.shape[0]
    column = lambda part: pl.BlockSpec((length, HEAD_DIM), lambda h: (0, part * heads + h))
    whole = lambda shape: pl.BlockSpec(shape, lambda h: (0,) * len(shape))
    out = pl.BlockSpec((length, HEAD_DIM), lambda h: (0, h))
    return pl.pallas_call(
        attend_kernel,
        grid=(heads,),
        in_specs=[
            column(0), column(1), column(2), whole(scales.shape),
            pl.BlockSpec((2, HEAD_DIM), lambda h: (0, h)),
            whole(turns.shape), whole(row_segment.shape), whole(col_segment.shape),
        ],
        out_specs=[out] * 4,
        out_shape=[jax.ShapeDtypeStruct((length, heads * HEAD_DIM), bf16)] * 4,
        compiler_params=KERNEL_PARAMS,
        cost_estimate=SMALL_COST,
        name="attend",
    )(projected, projected, projected, scales, gains, turns, row_segment, col_segment)


def attend_back_kernel(
    query_ref, key_ref, value_ref, grad_ref, turn_ref, row_seg_ref, col_seg_ref,
    query_out_ref, key_out_ref, value_out_ref, key_sum_ref, value_sum_ref,
):
    length = query_ref.shape[0]
    scale = HEAD_DIM ** (-0.5)
    cosines, sines = turn_ref[0], -turn_ref[1]
    for start in reversed(range(0, length, ATT_BLOCK)):
        stop = start + ATT_BLOCK
        query_rows, grad_rows, keys = query_ref[start:stop], grad_ref[start:stop], key_ref[:stop]
        probs = block_probs(
            query_rows, keys, row_seg_ref[start:stop, 0:1], col_seg_ref[0:1, :stop], scale
        )
        value_terms = dot(probs.astype(bf16), grad_rows, 0, 0)
        prob_grad = dot(grad_rows, value_ref[:stop], 1, 1)
        inner = jnp.sum(probs * prob_grad, axis=1, keepdims=True)
        score_grad = (probs * (prob_grad - inner)).astype(bf16)
        query_grad = (dot(score_grad, keys, 1, 0) * scale).astype(bf16).astype(f32)
        query_out_ref[start:stop] = turn(query_grad, cosines[start:stop], sines[start:stop])
        key_terms = dot(score_grad, query_rows, 0, 0)
        if stop == length:
            key_sum_ref[...] = key_terms
            value_sum_ref[...] = value_terms
        else:
            key_sum_ref[:stop] += key_terms
            value_sum_ref[:stop] += value_terms
    key_grad = (key_sum_ref[...] * scale).astype(bf16).astype(f32)
    key_out_ref[...] = turn(key_grad, cosines, sines)
    value_out_ref[...] = value_sum_ref[...].astype(bf16)


def attend_back(queries, keys, values, grads, turns, row_segment, col_segment, heads):
    length = queries.shape[0]
    column = pl.BlockSpec((length, HEAD_DIM), lambda h: (0, h))
    whole = lambda shape: pl.BlockSpec(shape, lambda h: (0,) * len(shape))
    shape = (length, heads * HEAD_DIM)
    return pl.pallas_call(
        attend_back_kernel,
        grid=(heads,),
        in_specs=[column] * 4 + [whole(turns.shape), whole(row_segment.shape), whole(col_segment.shape)],
        out_specs=[column] * 3,
        out_shape=[
            jax.ShapeDtypeStruct(shape, f32),
            jax.ShapeDtypeStruct(shape, f32),
            jax.ShapeDtypeStruct(shape, bf16),
        ],
        scratch_shapes=[pltpu.VMEM((length, HEAD_DIM), f32)] * 2,
        compiler_params=KERNEL_PARAMS,
        cost_estimate=ATTEND_BACK_COST,
        name="attend_back",
    )(queries, keys, values, grads, turns, row_segment, col_segment)


def chunk_of(width, most):
    return most if width % most == 0 else width


def forward_kernel(count, kept, pick_ref, gate_ref, in_ref, down_ref, *refs):
    near_refs, refs = refs[:count], refs[count:]
    earlier_refs, refs = refs[4:kept], refs[kept:]
    rows_ref, gate_out_ref, up_out_ref, gated_ref = refs[:4]
    mix_refs = refs[4 : count + 4]
    result_ref, sums_ref = refs[count + 4 :]
    step_number, steps = pl.program_id(0), pl.num_programs(0)
    capacity, width = pick_ref.shape[2], rows_ref.shape[2]
    hidden = gated_ref.shape[2]
    for k in range(count):
        rows_ref[0, k * capacity : (k + 1) * capacity] = dot(
            pick_ref[0, k], near_refs[k][...], 1, 0
        ).astype(bf16)
    step = chunk_of(hidden, 512)

    @pl.loop(0, hidden // step)
    def _(j):
        low = pl.ds(pl.multiple_of(j * step, step), step)
        high = pl.ds(pl.multiple_of(hidden + j * step, step), step)
        gate = dot(rows_ref[0], in_ref[0, :, low], 1, 0)
        up = dot(rows_ref[0], in_ref[0, :, high], 1, 0)
        gate_out_ref[0, :, low] = gate.astype(bf16)
        up_out_ref[0, :, low] = up.astype(bf16)
        gated_ref[0, :, low] = (gate * jax.nn.sigmoid(gate) * up * gate_ref[0]).astype(bf16)

    wide = chunk_of(width, 1024)

    @pl.loop(0, width // wide)
    def _(j):
        cols = pl.ds(pl.multiple_of(j * wide, wide), wide)
        result_ref[...] = dot(gated_ref[0], down_ref[0, cols, :], 1, 1).astype(bf16)
        for k in range(count):
            part = dot(pick_ref[0, k], result_ref[k * capacity : (k + 1) * capacity], 0, 0)

            @pl.when(step_number == 0)
            def _():
                sums_ref[k, :, cols] = part

            @pl.when(step_number > 0)
            def _():
                sums_ref[k, :, cols] += part

    @pl.when(step_number == steps - 1)
    def _():
        for k in range(count):
            mix = sums_ref[k]
            if earlier_refs:
                mix = mix + earlier_refs[k][...].astype(f32)
            mix_refs[k][...] = mix.astype(bf16)


def experts_forward(first, kept, pick, gates, in_weight, down_weight, near):
    experts, count, capacity, tokens = pick.shape
    here, width, hidden = in_weight.shape[0], in_weight.shape[1], down_weight.shape[2]
    rows = count * capacity
    each = lambda shape: pl.BlockSpec((1,) + shape, lambda e: (first + e,) + (0,) * len(shape))
    near_each = lambda shape: pl.BlockSpec((1,) + shape, lambda e: (e,) + (0,) * len(shape))
    whole = pl.BlockSpec((tokens, width), lambda e: (0, 0), pipeline_mode=pl.Buffered(1))
    return pl.pallas_call(
        functools.partial(forward_kernel, count, len(kept)),
        grid=(here,),
        in_specs=[
            each((count, capacity, tokens)), each((rows, 1)),
            near_each((width, 2 * hidden)), near_each((width, hidden)),
        ] + [whole] * count + [pl.BlockSpec(memory_space=pl.ANY)] * len(kept[:4]) + [whole] * len(kept[4:]),
        out_specs=[each((rows, width))] + [each((rows, hidden))] * 3 + [whole] * count,
        out_shape=[jax.ShapeDtypeStruct((experts, rows, width), bf16)]
        + [jax.ShapeDtypeStruct((experts, rows, hidden), bf16)] * 3
        + [jax.ShapeDtypeStruct((tokens, width), bf16)] * count,
        scratch_shapes=[
            pltpu.VMEM((rows, chunk_of(width, 1024)), bf16),
            pltpu.VMEM((count, tokens, width), f32),
        ],
        input_output_aliases={4 + count + i: i for i in range(len(kept[:4]))},
        compiler_params=KERNEL_PARAMS,
        cost_estimate=SMALL_COST,
        name="experts_forward",
    )(pick, gates, in_weight, down_weight, *near, *kept)


def down_grad_kernel(count, pick_ref, gated_ref, *refs):
    near_refs = refs[:count]
    rows_ref, grad_ref = refs[count:]
    capacity, width = pick_ref.shape[2], rows_ref.shape[2]
    for k in range(count):
        rows_ref[0, k * capacity : (k + 1) * capacity] = dot(
            pick_ref[0, k], near_refs[k][...], 1, 0
        ).astype(bf16)
    step = chunk_of(width, 2048)

    @pl.loop(0, width // step)
    def _(j):
        cols = pl.ds(pl.multiple_of(j * step, step), step)
        grad_ref[0, cols, :] = dot(rows_ref[0, :, cols], gated_ref[0], 0, 0).astype(bf16)


def experts_down_grad(pick, gated, near):
    experts, count, capacity, tokens = pick.shape
    width, hidden = near[0].shape[1], gated.shape[2]
    rows = count * capacity
    each = lambda shape: pl.BlockSpec((1,) + shape, lambda e: (e,) + (0,) * len(shape))
    whole = pl.BlockSpec((tokens, width), lambda e: (0, 0), pipeline_mode=pl.Buffered(1))
    return pl.pallas_call(
        functools.partial(down_grad_kernel, count),
        grid=(experts,),
        in_specs=[each((count, capacity, tokens)), each((rows, hidden))] + [whole] * count,
        out_specs=[each((rows, width)), each((width, hidden))],
        out_shape=[
            jax.ShapeDtypeStruct((experts, rows, width), bf16),
            jax.ShapeDtypeStruct((experts, width, hidden), bf16),
        ],
        compiler_params=KERNEL_PARAMS,
        cost_estimate=DOWN_GRAD_COST,
        name="experts_down_grad",
    )(pick, gated, *near)


def backward_kernel(
    first, count, kept, pick_ref, gate_rows_ref, cot_ref, gate_ref, up_ref, in_ref, down_ref, *refs
):
    earlier_refs, refs = refs[1:kept], refs[kept:]
    both_ref = refs[0]
    copy_refs = refs[1 : 1 + count]
    result_ref, inner_ref, sums_ref, inner_sums_ref = refs[1 + count :]
    step_number, steps = pl.program_id(0), pl.num_programs(0)
    capacity, width = pick_ref.shape[2], cot_ref.shape[2]
    hidden = gate_ref.shape[2]
    lanes = inner_sums_ref.shape[2]
    step = chunk_of(hidden, 512)
    inner_ref[...] = jnp.zeros_like(inner_ref)

    @pl.when(step_number == 0)
    def _():
        inner_sums_ref[...] = jnp.zeros_like(inner_sums_ref)

    @pl.loop(0, hidden // step)
    def _(j):
        low = pl.ds(pl.multiple_of(j * step, step), step)
        high = pl.ds(pl.multiple_of(hidden + j * step, step), step)
        result_grad = dot(cot_ref[0], down_ref[0, :, low], 1, 0)
        gate, up = gate_ref[0, :, low].astype(f32), up_ref[0, :, low].astype(f32)
        sigmoid = jax.nn.sigmoid(gate)
        silu = gate * sigmoid
        inner_ref[...] += jnp.sum(result_grad * silu * up, axis=1, keepdims=True)
        act_grad = result_grad * gate_rows_ref[0]
        both_ref[0, :, low] = (act_grad * up * (sigmoid + silu * (1.0 - sigmoid))).astype(bf16)
        both_ref[0, :, high] = (act_grad * silu).astype(bf16)

    inner_high = inner_ref[...].astype(bf16).astype(f32)
    lane = lax.broadcasted_iota(jnp.int32, (count * capacity, lanes), 1)
    place = 2 * (first + step_number)
    inner_wide = jnp.where(lane == place, inner_high, 0.0)
    inner_wide = jnp.where(lane == place + 1, inner_ref[...] - inner_high, inner_wide)
    inner_wide = inner_wide.astype(bf16)
    for k in range(count):
        inner_sums_ref[k] += dot(pick_ref[0, k], inner_wide[k * capacity : (k + 1) * capacity], 0, 0)
    wide = chunk_of(width, 1024)

    @pl.loop(0, width // wide)
    def _(j):
        cols = pl.ds(pl.multiple_of(j * wide, wide), wide)
        result_ref[...] = dot(both_ref[0], in_ref[0, cols, :], 1, 1).astype(bf16)
        for k in range(count):
            part = dot(pick_ref[0, k], result_ref[k * capacity : (k + 1) * capacity], 0, 0)

            @pl.when(step_number == 0)
            def _():
                sums_ref[k, :, cols] = part

            @pl.when(step_number > 0)
            def _():
                sums_ref[k, :, cols] += part

    @pl.when(step_number == steps - 1)
    def _():
        for k in range(count):
            copies, inner = sums_ref[k], inner_sums_ref[k]
            if earlier_refs:
                copies = copies + earlier_refs[k][:, :width].astype(f32)
                inner = inner + earlier_refs[k][:, width:].astype(f32)
            copy_refs[k][:, :width] = copies.astype(bf16)
            copy_refs[k][:, width:] = inner.astype(bf16)


def experts_backward(first, kept, pick, gate_rows, cot_rows, gate, up, in_weight, down_weight):
    experts, count, capacity, tokens = pick.shape
    here, width, hidden = in_weight.shape[0], in_weight.shape[1], down_weight.shape[2]
    rows = count * capacity
    lanes = 128 * -(-2 * experts // 128)
    each = lambda shape: pl.BlockSpec((1,) + shape, lambda e: (first + e,) + (0,) * len(shape))
    near_each = lambda shape: pl.BlockSpec((1,) + shape, lambda e: (e,) + (0,) * len(shape))
    whole = pl.BlockSpec((tokens, width + lanes), lambda e: (0, 0), pipeline_mode=pl.Buffered(1))
    return pl.pallas_call(
        functools.partial(backward_kernel, first, count, len(kept)),
        grid=(here,),
        in_specs=[
            each((count, capacity, tokens)), each((rows, 1)), each((rows, width)),
            each((rows, hidden)), each((rows, hidden)),
            near_each((width, 2 * hidden)), near_each((width, hidden)),
        ] + [pl.BlockSpec(memory_space=pl.ANY)] * len(kept[:1]) + [whole] * len(kept[1:]),
        out_specs=[each((rows, 2 * hidden))] + [whole] * count,
        out_shape=[jax.ShapeDtypeStruct((experts, rows, 2 * hidden), bf16)]
        + [jax.ShapeDtypeStruct((tokens, width + lanes), bf16)] * count,
        scratch_shapes=[
            pltpu.VMEM((rows, chunk_of(width, 1024)), bf16),
            pltpu.VMEM((rows, 1), f32),
            pltpu.VMEM((count, tokens, width), f32),
            pltpu.VMEM((count, tokens, lanes), f32),
        ],
        input_output_aliases={7 + i: i for i in range(len(kept[:1]))},
        compiler_params=KERNEL_PARAMS,
        cost_estimate=SMALL_COST,
        name="experts_backward",
    )(pick, gate_rows, cot_rows, gate, up, in_weight, down_weight, *kept)


def in_grad_kernel(rows_ref, both_ref, earlier_ref, grad_ref):
    width = rows_ref.shape[2]
    step = chunk_of(width, 512)

    @pl.loop(0, width // step)
    def _(j):
        cols = pl.ds(pl.multiple_of(j * step, step), step)
        grad_ref[0, cols, :] = dot(rows_ref[0, :, cols], both_ref[0], 0, 0).astype(bf16)


def experts_in_grad(rows, both, earlier):
    experts, count, width = rows.shape
    each = lambda shape: pl.BlockSpec((1,) + shape, lambda e: (e,) + (0,) * len(shape))
    return pl.pallas_call(
        in_grad_kernel,
        grid=(experts,),
        in_specs=[each(rows.shape[1:]), each(both.shape[1:]), pl.BlockSpec(memory_space=pl.ANY)],
        out_specs=each((width, both.shape[2])),
        out_shape=jax.ShapeDtypeStruct((experts, width, both.shape[2]), bf16),
        compiler_params=KERNEL_PARAMS,
        cost_estimate=SMALL_COST,
        name="experts_in_grad",
    )(rows, both, earlier)


def spread_kernel(split, left_ref, right_ref, *refs):
    groups, parts, cores = split
    out_ref = refs[-1]
    width = right_ref.shape[1]
    rows = out_ref.shape[2] // groups
    each = parts * cores * rows
    for group in range(groups):
        terms = dot(left_ref[:, group * each : (group + 1) * each], right_ref[...], 0, 0).astype(bf16)
        for part in range(parts):
            for core in range(cores):
                start = (part * cores + core) * rows
                place = pl.ds(group * rows, rows)
                out_ref[core, part, place, :width] = terms[start : start + rows]
                if len(refs) > 1:
                    begin = group * each + start
                    out_ref[core, part, place, width:] = refs[0][begin : begin + rows, :]


def spread_product(left, right, beside, split):
    groups, parts, cores = split
    rows = left.shape[1] // (groups * parts * cores)
    width = right.shape[1] + sum(array.shape[1] for array in beside)
    return pl.pallas_call(
        functools.partial(spread_kernel, split),
        out_shape=jax.ShapeDtypeStruct((cores, parts, groups * rows, width), bf16),
        compiler_params=KERNEL_PARAMS,
        cost_estimate=SMALL_COST,
        name="spread_product",
    )(left, right, *beside)


def on_device(
    tokens,
    cotangent,
    expert_ids,
    segment_ids,
    norm_gains,
    w_qkv,
    w_out,
    router,
    expert_in,
    expert_out,
):
    own_low = tokens[0]
    inputs = own_low.astype(f32)
    tok_count, model_width = inputs.shape
    segment = segment_ids[0]
    length = segment.shape[0]
    seq_count = lax.axis_size("seq")
    exp_count = lax.axis_size("exp")
    core_count = lax.axis_size("fsdp")
    own_seq = lax.axis_index("seq")
    own_exp = lax.axis_index("exp")
    rows_dev = w_qkv.shape[0]
    heads_dev = HEADS // seq_count
    head_cols = heads_dev * HEAD_DIM
    experts_total = router.shape[1]
    exp_dev = expert_in.shape[1]

    small = jnp.concatenate([norm_gains, router], axis=1)
    small_cols = small.shape[1]
    ids_room = TOP * tok_count // (seq_count * rows_dev)
    small = jnp.pad(small, ((0, 0), (0, ids_room + -(small_cols + ids_room) % 128)))
    heads_rows = w_qkv.reshape(rows_dev, 3, seq_count, head_cols).transpose(2, 0, 1, 3)
    heads_rows = heads_rows.reshape(seq_count, rows_dev, 3 * head_cols)
    small = jnp.broadcast_to(small[None], (seq_count,) + small.shape)
    heads_seq = exchange(jnp.concatenate([heads_rows, small], axis=2), "seq")
    ids_low = expert_ids[0].astype(bf16).reshape(seq_count, rows_dev, -1)
    first_id = 3 * head_cols + small_cols
    ids_cols = ids_low.shape[2]
    after_ids = heads_seq.shape[2] - first_id - ids_cols
    heads_rows = heads_seq + jnp.pad(ids_low, ((0, 0), (0, 0), (first_id, after_ids)))
    heads_near = gather_near(heads_rows.reshape(seq_count * rows_dev, -1), "exp")
    ids_group = jnp.stack(
        [near[:, first_id : first_id + ids_cols].reshape(tok_count, TOP) for near in heads_near]
    )
    heads_all = order_cores(heads_near, seq_count, "exp", "fsdp")
    heads_weight = heads_all[:, : 3 * head_cols]
    small = heads_all[:, 3 * head_cols : first_id].T
    gains = small[:4].astype(f32)
    router_rows = small[4:]
    all_tokens = jnp.broadcast_to(own_low[None], (seq_count, tok_count, model_width))
    all_tokens = exchange(all_tokens, "seq").reshape(length, model_width)

    out_rows = after(w_out, all_tokens)[None]
    out_rows = exchange(jnp.broadcast_to(out_rows, (seq_count,) + w_out.shape), "seq")
    out_rows = out_rows.reshape(seq_count * rows_dev, model_width)
    out_near = gather_near(after(out_rows, heads_near[-1]), "exp")

    parts = 2 if exp_dev % 2 == 0 else 1
    part_experts = exp_dev // parts
    in_blocks = jnp.transpose(after(expert_in, heads_seq), (1, 0, 2))
    down_blocks = jnp.transpose(after(expert_out, heads_seq), (1, 0, 2))
    in_weights, down_weights = [], []
    for part in range(parts):
        chosen_experts = slice(part * part_experts, (part + 1) * part_experts)
        for blocks, weights in ((in_blocks, in_weights), (down_blocks, down_weights)):
            weights.append(
                lax.all_gather(blocks[chosen_experts], ("seq", "fsdp"), axis=1, tiled=True)
            )

    all_inputs = all_tokens.astype(f32)
    first_inverse = rms_inverse(all_inputs)
    attn_low = (all_inputs * first_inverse * gains[0]).astype(bf16)
    projected = jnp.dot(attn_low, heads_weight, preferred_element_type=f32)
    own_gains = lax.dynamic_slice_in_dim(gains, own_seq * head_cols, head_cols, 1)
    query_pre, key_pre = projected[:, :head_cols], projected[:, head_cols : 2 * head_cols]
    squares = jnp.stack([jnp.sum(query_pre * query_pre, axis=-1), jnp.sum(key_pre * key_pre, axis=-1)])
    squares = sum_all(squares, "seq")
    scales = lax.rsqrt(squares / model_width + epsilon).T
    query_inverse, key_inverse = scales[:, 0:1], scales[:, 1:2]
    turns = rotary_tables(jnp.arange(length, dtype=jnp.int32), HEAD_DIM)
    row_segment, col_segment = segment[:, None], segment[None, :]
    attended, queries, keys, values = attend(
        projected, after(scales, out_near[-1]), own_gains[1:3], turns, row_segment, col_segment, heads_dev
    )
    out_weight = order_cores(out_near, seq_count, "exp", "fsdp")
    merged = lax.all_to_all(attended, "seq", split_axis=0, concat_axis=1, tiled=True)
    branch = jnp.einsum("tc,dc->td", merged, out_weight, preferred_element_type=f32)
    residual = inputs + branch
    mlp_inverse = rms_inverse(residual)
    mlp_low = (residual * mlp_inverse * gains[3]).astype(bf16)

    capacity = tok_count * TOP // experts_total * 9 // 8
    near_experts = own_exp * exp_dev + jnp.arange(exp_dev, dtype=jnp.int32)
    chosen = jnp.any(
        ids_group[:, :, :, None] == near_experts.astype(bf16)[None, None, None, :], axis=2
    )
    earlier = (
        jnp.arange(tok_count)[:, None] > jnp.arange(tok_count)[None, :]
    ).astype(bf16)
    rank = jnp.einsum("tu,sue->est", earlier, chosen.astype(bf16), preferred_element_type=f32)
    rank = jnp.where(jnp.transpose(chosen, (2, 0, 1)), rank, -1.0)
    pick = rank[:, :, None, :] == jnp.arange(capacity, dtype=f32)[None, None, :, None]
    pick_low = pick.astype(bf16)

    mlp_near = gather_near(mlp_low, "exp")
    cot_near = cotangent[0]
    for near in mlp_near[1:]:
        cot_near = after(cot_near, near)
    cot_near = gather_near(cot_near, "exp")
    logits = jnp.stack(
        [jnp.einsum("td,ed->te", near, router_rows, preferred_element_type=f32) for near in mlp_near]
    )
    group_probs = jax.nn.softmax(logits, axis=-1)
    router_probs = group_probs[0]
    near_probs = lax.dynamic_slice_in_dim(group_probs, own_exp * exp_dev, exp_dev, 2)
    near_probs = jnp.transpose(near_probs, (2, 0, 1))
    gate_rows = jnp.sum(jnp.where(pick, near_probs[:, :, None, :], 0.0), axis=-1)
    gate_rows = gate_rows.reshape(exp_dev, exp_count * capacity, 1)
    kept = []
    for part in range(parts):
        kept = experts_forward(
            part * part_experts, kept, pick_low, gate_rows, in_weights[part], down_weights[part], mlp_near
        )
    expert_rows, gate, up, gated = kept[:4]
    mix_near = send_near(kept[4:], "exp")
    output = (residual + add_up(mix_near)).astype(bf16)

    cot_rows, down_grad = experts_down_grad(pick_low, gated, cot_near)
    grad_expert_out = lax.psum_scatter(
        down_grad, ("seq", "fsdp"), scatter_dimension=1, tiled=True
    )
    kept = []
    for part in range(parts):
        kept = experts_backward(
            part * part_experts, kept, pick_low, gate_rows, cot_rows, gate, up,
            in_weights[part], down_weights[part],
        )
    copy_near = send_near(kept[1:], "exp")
    earlier = jnp.stack([block[:8, :128] for block in kept[1:]] + [output[:8, :128]])
    in_grad = experts_in_grad(expert_rows, kept[0], earlier)
    grad_expert_in = lax.psum_scatter(in_grad, ("seq", "fsdp"), scatter_dimension=1, tiled=True)
    copy_near[0] = after(copy_near[0], in_grad)
    mlp_grad_experts = add_up([near[:, :model_width] for near in copy_near])
    prob_pairs = [
        near[:, model_width : model_width + 2 * exp_dev].astype(f32).reshape(tok_count, exp_dev, 2)
        for near in copy_near
    ]
    prob_grad = order([jnp.sum(pair, axis=2) for pair in prob_pairs], "exp", 1, 1)
    prob_grad = prob_grad.reshape(tok_count, experts_total)
    grad_expert_in = jnp.transpose(grad_expert_in, (1, 0, 2)).astype(f32)
    grad_expert_out = jnp.transpose(grad_expert_out, (1, 0, 2)).astype(f32)

    logit_grad = router_probs * (
        prob_grad - jnp.sum(router_probs * prob_grad, axis=-1, keepdims=True)
    )
    router_grad = jnp.dot(logit_grad.T, mlp_low.astype(f32), precision=highest)
    mlp_grad = mlp_grad_experts + jnp.dot(
        logit_grad, router_rows.astype(f32), precision=highest
    )
    residual_norm_grad, mlp_gain_grad = rms_back(mlp_grad, residual, mlp_inverse, gains[3])
    residual_grad = cotangent[0].astype(f32) + residual_norm_grad
    branch_grad = residual_grad.astype(bf16)

    merged_grad = jnp.einsum("td,dc->tc", branch_grad, out_weight, preferred_element_type=f32)
    heads_grad = lax.all_to_all(
        merged_grad.astype(bf16), "seq", split_axis=1, concat_axis=0, tiled=True
    )
    split_sizes = (seq_count, exp_count, core_count)
    out_terms = spread_product(after(branch_grad, merged_grad), merged, [], split_sizes)
    out_terms = scatter_core(out_terms, "fsdp")
    out_terms = scatter(out_terms, "exp").astype(bf16)
    query_grad, key_grad, value_grad = attend_back(
        queries, keys, values, heads_grad, turns, row_segment, col_segment, heads_dev
    )
    query_scaled, key_scaled = query_grad * own_gains[1], key_grad * own_gains[2]
    means = jnp.stack(
        [jnp.sum(query_scaled * query_pre, axis=-1), jnp.sum(key_scaled * key_pre, axis=-1)]
    )
    means = after(sum_all(means, "seq") / model_width, out_terms)
    query_gain_grad = jnp.sum(query_grad * query_pre * query_inverse, axis=0)
    key_gain_grad = jnp.sum(key_grad * key_pre * key_inverse, axis=0)
    query_pre_grad = query_inverse * query_scaled - query_pre * query_inverse**3 * means[0][:, None]
    key_pre_grad = key_inverse * key_scaled - key_pre * key_inverse**3 * means[1][:, None]
    qkv_grad = jnp.concatenate(
        [query_pre_grad.astype(bf16), key_pre_grad.astype(bf16), value_grad],
        axis=1,
    )
    attn_in_part = jnp.einsum("tc,dc->td", qkv_grad, heads_weight, preferred_element_type=f32)
    first_gain_grad = jnp.sum(attn_in_part * all_inputs * first_inverse, axis=0)
    attn_in_grad = scatter(
        attn_in_part.astype(bf16).reshape(seq_count, tok_count, model_width), "seq"
    )
    zero_row = jnp.zeros((model_width,), f32)
    small_terms = jnp.concatenate(
        [
            jnp.stack(
                [
                    first_gain_grad,
                    lax.dynamic_update_slice_in_dim(zero_row, query_gain_grad, own_seq * head_cols, 0),
                    lax.dynamic_update_slice_in_dim(zero_row, key_gain_grad, own_seq * head_cols, 0),
                    mlp_gain_grad,
                ]
            ),
            router_grad,
        ],
        axis=0,
    ).T
    small_terms = jnp.pad(small_terms, ((0, 0), (0, -small_cols % 128)))
    heads_terms = spread_product(attn_low, qkv_grad, [small_terms.astype(bf16)], split_sizes)
    heads_terms = scatter_core(heads_terms, "fsdp")
    heads_terms = scatter(heads_terms, "exp").astype(bf16)
    grad_w_out = scatter(
        after(out_terms, heads_terms).reshape(seq_count, rows_dev, model_width), "seq"
    )
    heads_terms = heads_terms.reshape(seq_count, rows_dev, -1)
    heads_terms = after(after(heads_terms, grad_expert_in), grad_expert_out)
    heads_given, heads_terms = heads_terms, exchange(heads_terms, "seq")
    grad_w_qkv = jnp.concatenate(
        [
            heads_terms[source, :, part * head_cols : (part + 1) * head_cols]
            for part in range(3)
            for source in range(seq_count)
        ],
        axis=1,
    ).astype(f32)
    own_inverse = lax.dynamic_slice_in_dim(first_inverse, own_seq * tok_count, tok_count, 0)
    input_norm_grad, _ = rms_back(after(attn_in_grad, heads_given), inputs, own_inverse, gains[0])
    input_grad = residual_grad + input_norm_grad

    small_grad = jnp.sum(
        heads_terms[:, :, 3 * head_cols : 3 * head_cols + small_cols].astype(f32), axis=0
    )
    return (
        output[None],
        input_grad[None],
        small_grad[:, :4],
        grad_w_qkv,
        grad_w_out,
        small_grad[:, 4:],
        grad_expert_in,
        grad_expert_out,
    )


def solution(mesh):
    in_specs = (
        P(("exp", "fsdp"), "seq", None),
        P(("exp", "fsdp"), "seq", None),
        P(("exp", "fsdp"), "seq", None),
        P(("exp", "fsdp"), None),
        P(("seq", "exp", "fsdp"), None),
        P(("seq", "exp", "fsdp"), None),
        P(("seq", "exp", "fsdp"), None),
        P(("seq", "exp", "fsdp"), None),
        P(("seq", "fsdp"), "exp", None),
        P(("seq", "fsdp"), "exp", None),
    )
    out_specs = (
        P(("exp", "fsdp"), "seq", None),
        P(("exp", "fsdp"), "seq", None),
        P(("seq", "exp", "fsdp"), None),
        P(("seq", "exp", "fsdp"), None),
        P(("seq", "exp", "fsdp"), None),
        P(("seq", "exp", "fsdp"), None),
        P(("seq", "fsdp"), "exp", None),
        P(("seq", "fsdp"), "exp", None),
    )
    return jax.shard_map(
        on_device, mesh=mesh, in_specs=in_specs, out_specs=out_specs, check_vma=False
    )
```

time: 1180 us -> 1060 us (0.90)
  Pallas kernels: 0 us -> 273 us
  matrix products: 260 us -> 44.7 us
  starting transfers between devices: 228 us -> 86.1 us
  other arithmetic: 154 us -> 79 us
  waiting for transfers between devices: 372 us -> 436 us
  local copies, waits for them, and re-layouts: 134 us -> 92.2 us
  blocking collectives: 0 us -> 15.1 us
    pallas_call x0 -> x12, Pallas kernels: none -> 273 us  [the longest x2 77.7 us: experts_backward(): pl.pallas_call(functools.partial(backward_kernel, first, count, len(kept)...]
    dot_general x37 -> x5, matrix products: 213 us -> 2.9 us  [the longest x4 2.73 us: on_device(): jnp.einsum('td,ed->te', near, router_rows, preferred_element_type=f32)]
    ppermute x103 -> x44, starting transfers between devices: 207 us -> 51.7 us  [the longest x18 29.5 us: gather_near(): lax.ppermute(block, axis, shift_pairs(count, k))]
    another operation x31 -> x3, other arithmetic: 49.8 us -> 2.48 us  [the longest x2 2.4 us: rotary_tables(): jnp.stack([jnp.concatenate([cosine, cosine], axis=1), jnp.concatenate([-s...]
    reduce_scatter x2, waiting for transfers between devices: 0.01 us -> 40.3 us  [the longest x1 40.3 us: on_device(): lax.psum_scatter(in_grad, ('seq', 'fsdp'), scatter_dimension=1, tiled=True)]
    all_to_all x3 -> x4, waiting for transfers between devices: 1.79 us -> 35.9 us  [the longest x1 20.8 us: on_device(): lax.all_to_all(attended, 'seq', split_axis=0, concat_axis=1, tiled=True)]
    convert_element_type x6 -> x1, local copies, waits for them, and re-layouts: 22 us -> 0.13 us  [on_device(): ids_low = expert_ids[0].astype(bf16).reshape(seq_count, rows_dev, -1)]
    dynamic_update_slice x15 -> x0, other arithmetic: 19.1 us -> none  [the longest x13 17.8 us: put_block(): return lax.dynamic_update_index_in_dim(buffer, block, index, axis)]
  transfers between devices with their start and end apart: 114 -> 57, of which waited for: 45 -> 22; matrix products, arithmetic and copies ran while one was open for 38% -> 18% of each run, Pallas kernels for 0% -> 24%
where the time goes in v2:
time: 1060 us; the launch traced here: 1050 us
  waiting for transfers between devices  436 us (41%)
  Pallas kernels  273 us (26%)
  local copies, waits for them, and re-layouts  92.2 us (9%)
  starting transfers between devices  86.1 us (8%)
  other arithmetic  79 us (7%)
  matrix products  44.7 us (4%)
  between operations  25.8 us (2%)
  blocking collectives  15.1 us (1%)
    ppermute x18, waiting for transfers between devices, gather_near(): lax.ppermute(block, axis, shift_pairs(count, k))  228 us
    ppermute x18, waiting for transfers between devices, send_near(): lax.ppermute(blocks[k], axis, shift_pairs(count, -k))  125 us
    pallas_call x2, Pallas kernels, experts_backward(): pl.pallas_call(functools.partial(backward_kernel, first, count, len(kept)...  77.7 us
    pallas_call x2, Pallas kernels, experts_forward(): pl.pallas_call(functools.partial(forward_kernel, count, len(kept)), grid=...  70 us
    reduce_scatter x1, waiting for transfers between devices, on_device(): lax.psum_scatter(in_grad, ('seq', 'fsdp'), scatter_dimension=1, tiled=True)  40.3 us
    pallas_call x1, Pallas kernels, experts_in_grad(): pl.pallas_call(in_grad_kernel, grid=(experts,), in_specs=[each(rows.shape...  35.1 us
    unnamed x155, local copies, waits for them, and re-layouts  35 us
    ppermute x18, starting transfers between devices, gather_near(): lax.ppermute(block, axis, shift_pairs(count, k))  29.5 us
  transfers between devices with their start and end apart: 57, of which 22 were waited for; matrix products, arithmetic and copies ran while one was open for 18% of the time, Pallas kernels for 24%

profile of v2, /device:TPU:10, one launch (start us, length us, event | category | flops | bytes accessed | tf_op | source)
XLA Modules:
  0.0 1052.0 jit_solution(17749948758088848205)
XLA Ops:
  12.0 15.1 %all_to_all.58 = bf16[4,64,1664]{2,1,0:T(8,128)(2,1)S(1)} all-to-all(bf16[4,64,1664]{2,1,0:T(8,128)(2,1)S(1)} %pad_maximum_fusion.2), channel_id=1, replica_groups=mesh['seq'=4,'exp'=4,'fsdp'=2] {'seq'}, dimensions={0} | all-to-all | bytes 1703936 | tf_op jit(solution)/shard_map/all_to_all | solution.py:47
  55.5 52.7 %collective-permute-done.refs_1_ = bf16[256,1664]{1,0:T(8,128)(2,1)S(1)} collective-permute-done((bf16[256,1664]{1,0:T(8,128)(2,1)S(1)}, bf16[256,1664]{1,0:T(8,128)(2,1)S(1)}, u32[]{:S(2)}, u32[]{:S(2)}) %collective-permute-start) | collective-permute-done | bytes 852000 | tf_op jit(solution)/shard_map/ppermute | solution.py:53
  108.2 15.4 %collective-permute-done.1.refs_2_ = bf16[256,1664]{1,0:T(8,128)(2,1)S(1)} collective-permute-done((bf16[256,1664]{1,0:T(8,128)(2,1)S(1)}, bf16[256,1664]{1,0:T(8,128)(2,1)S(1)}, u32[]{:S(2)}, u32[]{:S(2)}) %collective-permute-start.1) | collective-permute-done | bytes 852000 | tf_op jit(solution)/shard_map/ppermute | solution.py:53
  130.6 7.3 assemble.2
  155.5 15.0 %all-to-all-done.2 = bf16[4,64,2048]{2,1,0:T(8,128)(2,1)S(1)} async-done(((bf16[4,64,2048]{2,1,0:T(8,128)(2,1)}), bf16[4,64,2048]{2,1,0:T(8,128)(2,1)S(1)}, u32[]{:S(2)}, u32[]{:S(2)}) %all-to-all-start.2) | async-done | bytes 1048608 | tf_op jit(solution)/shard_map/all_to_all | solution.py:47
  177.7 11.1 %fusion.9.query_ref.key_ref.value_ref = f32[1024,1536]{1,0:T(8,128)S(1)} fusion(bf16[1024,2048]{1,0:T(8,128)(2,1)} %fusion.2.left_ref, bf16[2048,1664]{1,0:T(8,128)(2,1)} %assemble.2), kind=kOutput, calls=%fused_computation.15 | convolution fusion | flops 6442450944 | bytes 16777216 | tf_op jit(solution)/shard_map/dot_general | solution.py:656
  199.0 43.8 %collective-permute-done.10.refs_3_ = bf16[256,2048]{1,0:T(8,128)(2,1)} collective-permute-done((bf16[256,2048]{1,0:T(8,128)(2,1)}, bf16[256,2048]{1,0:T(8,128)(2,1)}, u32[]{:S(2)}, u32[]{:S(2)}) %collective-permute-start.10) | collective-permute-done | bytes 1048608 | tf_op jit(solution)/shard_map/ppermute | solution.py:53
  245.4 18.0 %collective-permute-done.12.refs_2_ = bf16[256,2048]{1,0:T(8,128)(2,1)} collective-permute-done((bf16[256,2048]{1,0:T(8,128)(2,1)}, bf16[256,2048]{1,0:T(8,128)(2,1)}, u32[]{:S(2)}, u32[]{:S(2)}) %collective-permute-start.12) | collective-permute-done | bytes 1048608 | tf_op jit(solution)/shard_map/ppermute | solution.py:53
  264.5 16.4 %attend.1 = (bf16[1024,512]{1,0:T(8,128)(2,1)}, bf16[1024,512]{1,0:T(8,128)(2,1)}, bf16[1024,512]{1,0:T(8,128)(2,1)}, bf16[1024,512]{1,0:T(8,128)(2,1)}) custom-call(f32[1024,1536]{1,0:T(8,128)} %copy-done, f32[1024,1536]{1,0:T(8,128)} %copy-done, f32[1024,1536]{1,0:T(8,128)} %copy-done, f32[1024,2]{1,0:T(8,128)} %get-tuple-element.138.scale_ref, ...), custom_call_target="tpu_custom_call" | custom-call | flops 1 | bytes 1 | tf_op jit(solution)/shard_map/attend/pallas_call | solution.py:238
  289.7 20.8 %all-to-all-done.3 = bf16[4,256,512]{2,1,0:T(8,128)(2,1)S(1)} async-done(((bf16[4,256,512]{2,1,0:T(8,128)(2,1)}), bf16[4,256,512]{2,1,0:T(8,128)(2,1)S(1)}, u32[]{:S(2)}, u32[]{:S(2)}) %all-to-all-start.3) | async-done | bytes 1048608 | tf_op jit(solution)/shard_map/all_to_all | solution.py:669
  311.6 7.0 assemble.3
  335.8 17.3 %collective-permute-done.19.refs_3_ = bf16[256,2048]{1,0:T(8,128)(2,1)S(1)} collective-permute-done((bf16[256,2048]{1,0:T(8,128)(2,1)S(1)}, bf16[256,2048]{1,0:T(8,128)(2,1)S(1)}, u32[]{:S(2)}, u32[]{:S(2)}) %collective-permute-start.19) | collective-permute-done | bytes 1048608 | tf_op jit(solution)/shard_map/ppermute | solution.py:53
  354.3 43.8 %collective-permute-done.18.refs_2_ = bf16[256,2048]{1,0:T(8,128)(2,1)S(1)} collective-permute-done((bf16[256,2048]{1,0:T(8,128)(2,1)S(1)}, bf16[256,2048]{1,0:T(8,128)(2,1)S(1)}, u32[]{:S(2)}, u32[]{:S(2)}) %collective-permute-start.18) | collective-permute-done | bytes 1048608 | tf_op jit(solution)/shard_map/ppermute | solution.py:53
  399.2 20.4 %collective-permute-done.17.refs_1_ = bf16[256,2048]{1,0:T(8,128)(2,1)} collective-permute-done((bf16[256,2048]{1,0:T(8,128)(2,1)S(1)}, bf16[256,2048]{1,0:T(8,128)(2,1)}, u32[]{:S(2)}, u32[]{:S(2)}) %collective-permute-start.17) | collective-permute-done | bytes 1048608 | tf_op jit(solution)/shard_map/ppermute | solution.py:53
  432.5 34.0 %experts_forward.2 = (bf16[4,576,2048]{2,1,0:T(8,128)(2,1)}, bf16[4,576,1024]{2,1,0:T(8,128)(2,1)}, bf16[4,576,1024]{2,1,0:T(8,128)(2,1)}, bf16[4,576,1024]{2,1,...) custom-call(bf16[4,4,144,256]{3,2,1,0:T(8,128)(2,1)} %fusion.12.pick, ...), custom_call_target="tpu_custom_call" | custom-call | flops 1 | bytes 1 | tf_op jit(solution)/shard_map/experts_forward/pallas_call | solution.py:369
  466.5 36.0 %experts_forward.3 = (bf16[4,576,2048]{2,1,0:T(8,128)(2,1)}, bf16[4,576,1024]{2,1,0:T(8,128)(2,1)}, bf16[4,576,1024]{2,1,0:T(8,128)(2,1)}, bf16[4,576,1024]{2,1,...) custom-call(bf16[4,4,144,256]{3,2,1,0:T(8,128)(2,1)} %fusion.12.pick, ...), custom_call_target="tpu_custom_call", output_to_operand_aliasing={{0}: (8, {}), {1}: (9, {}), {2}: (10, {}), {3}: (11, {})} | custom-call | flops 1 | bytes 1 | tf_op jit(solution)/shard_map/experts_forward/pallas_call | solution.py:369
  502.5 11.9 %collective-permute-done.24.refs_2_ = bf16[256,2048]{1,0:T(8,128)(2,1)} collective-permute-done((bf16[256,2048]{1,0:T(8,128)(2,1)}, bf16[256,2048]{1,0:T(8,128)(2,1)}, u32[]{:S(2)}, u32[]{:S(2)}) %collective-permute-start.24) | collective-permute-done | bytes 1048608 | tf_op jit(solution)/shard_map/ppermute | solution.py:53
  515.6 21.2 %experts_down_grad.1 = (bf16[4,576,2048]{2,1,0:T(8,128)(2,1)}, bf16[4,2048,1024]{2,1,0:T(8,128)(2,1)}) custom-call(bf16[4,4,144,256]{3,2,1,0:T(8,128)(2,1)} %fusion.12.pick_ref, bf16[4,576,1024]{2,1,0:T(8,128)(2,1)} %get-tuple-element.56.gated_ref, bf16[256,2048]{1,0:T(8,128)(2,1)} %add_bitcast_fusion.refs_0_, ...), custom_call_target="tpu_custom_call" | custom-call | flops 99999997952 | bytes 1 | tf_op jit(solution)/shard_map/experts_down_grad/pallas_call | solution.py:413
  541.2 37.7 %experts_backward.2 = (bf16[4,576,2048]{2,1,0:T(8,128)(2,1)}, bf16[256,2176]{1,0:T(8,128)(2,1)}, bf16[256,2176]{1,0:T(8,128)(2,1)}, bf16[256,2176]{1,0:T(8,128)(2,1)}, bf16[256,2176]{1,0:T(8,128)(2,1)}) custom-call(bf16[4,4,144,256]{3,2,1,0:T(8,128)(2,1)} %fusion.12.pick_ref, f32[4,576,1]{2,1,0:T(8,128)} %reshape.281.gate_ref.gate_rows_ref, ...), custom_call_target="tpu_custom_call" | custom-call | flops 1 | bytes 1 | tf_op jit(solution)/shard_map/experts_backward/pallas_call | solution.py:503
  578.9 40.0 %experts_backward.3 = (bf16[4,576,2048]{2,1,0:T(8,128)(2,1)}, bf16[256,2176]{1,0:T(8,128)(2,1)}, bf16[256,2176]{1,0:T(8,128)(2,1)}, bf16[256,2176]{1,0:T(8,128)(2,1)}, bf16[256,2176]{1,0:T(8,128)(2,1)}) custom-call(bf16[4,4,144,256]{3,2,1,0:T(8,128)(2,1)} %fusion.12.pick_ref, ...), custom_call_target="tpu_custom_call", output_to_operand_aliasing={{0}: (7, {})} | custom-call | flops 1 | bytes 1 | tf_op jit(solution)/shard_map/experts_backward/pallas_call | solution.py:503
  624.4 51.6 %collective-permute-done.21 = bf16[256,2048]{1,0:T(8,128)(2,1)} collective-permute-done((bf16[256,2048]{1,0:T(8,128)(2,1)}, bf16[256,2048]{1,0:T(8,128)(2,1)}, u32[]{:S(2)}, u32[]{:S(2)}) %collective-permute-start.21) | collective-permute-done | bytes 1048608 | tf_op jit(solution)/shard_map/ppermute | solution.py:60
  681.2 35.1 %experts_in_grad.1 = bf16[4,2048,2048]{2,1,0:T(8,128)(2,1)} custom-call(bf16[4,576,2048]{2,1,0:T(8,128)(2,1)} %get-tuple-element.66.rows_ref, bf16[4,576,2048]{2,1,0:T(8,128)(2,1)} %get-tuple-element.67.both_ref, bf16[5,8,128]{2,1,0:T(8,128)(2,1)} %copy-done.61), custom_call_target="tpu_custom_call" | custom-call | flops 1 | bytes 1 | tf_op jit(solution)/shard_map/experts_in_grad/pallas_call | solution.py:540
  728.4 9.0 fusion.74
  739.7 8.9 spread_product.2
  765.2 6.9 fusion.5
  781.6 16.9 %attend_back.1 = (f32[1024,512]{1,0:T(8,128)}, f32[1024,512]{1,0:T(8,128)}, bf16[1024,512]{1,0:T(8,128)(2,1)}) custom-call(bf16[1024,512]{1,0:T(8,128)(2,1)} %get-tuple-element.71.query_ref, bf16[1024,512]{1,0:T(8,128)(2,1)} %get-tuple-element.72.key_ref, bf16[1024,512]{1,0:T(8,128)(2,1)} %get-tuple-element.73.value_ref, ...), custom_call_target="tpu_custom_call" | custom-call | flops 344999985152 | bytes 1 | tf_op jit(solution)/shard_map/attend_back/pallas_call | solution.py:290
  809.7 58.5 %collective-permute-done.34 = bf16[256,2048]{1,0:T(8,128)(2,1)} collective-permute-done((bf16[256,2048]{1,0:T(8,128)(2,1)}, bf16[256,2048]{1,0:T(8,128)(2,1)}, u32[]{:S(2)}, u32[]{:S(2)}) %collective-permute-start.34) | collective-permute-done | bytes 1048608 | tf_op jit(solution)/shard_map/ppermute | solution.py:60
  882.2 10.3 fusion.68
  896.9 12.9 %spread_product.3 = bf16[2,4,256,1664]{3,2,1,0:T(8,128)(2,1)} custom-call(bf16[1024,2048]{1,0:T(8,128)(2,1)} %fusion.2.left_ref, bf16[1024,1536]{1,0:T(8,128)(2,1)} %pad_maximum_fusion.right_ref, bf16[2048,128]{1,0:T(8,128)(2,1)} %pad.15.refs_0_), custom_call_target="tpu_custom_call" | custom-call | flops 1 | bytes 1 | tf_op jit(solution)/shard_map/spread_product/pallas_call | solution.py:574
  943.4 40.3 %reduce-scatter.3.cloned.1.call-done = bf16[4,256,2048]{2,1,0:T(8,128)(2,1)} async-done(((bf16[4,2048,2048]{2,1,0:T(8,128)(2,1)}), bf16[4,256,2048]{2,1,0:T(8,128)(2,1)}) %reduce-scatter.3.cloned.1.call-update) | async-done | bytes 4194320 | tf_op jit(solution)/shard_map/reduce_scatter | solution.py:724
  999.7 14.6 %all-to-all-start.5 = ((bf16[4,64,1664]{2,1,0:T(8,128)(2,1)}), bf16[4,64,1664]{2,1,0:T(8,128)(2,1)S(1)}, u32[]{:S(2)}, u32[]{:S(2)}) async-start(bf16[4,64,1664]{2,1,0:T(8,128)(2,1)} %bitcast.292), calls=%async_computation.7 | async-start | bytes 1703936 | tf_op jit(solution)/shard_map/all_to_all | solution.py:47
  1028.7 12.2 %copy.186 = f32[256,4,2048]{2,1,0:T(4,128)} copy(f32[256,4,2048]{2,0,1:T(8,128)} %copy-done.2) | data formatting | bytes 16777216
  (411 shorter events, 264.2 us)
Async XLA Ops:
  7.2 425.3 %all-gather.11.cloned.1.call-start = ((), (), s32[]{:S(2)}) async-start(), calls=%async_computation.11 | async-start | bytes 9437184 | tf_op jit(solution)/shard_map/all_gather | solution.py:650
  31.0 401.5 %all-gather.9.cloned.1.call-start = ((), (), s32[]{:S(2)}) async-start(), calls=%async_computation.10 | async-start | bytes 18874368 | tf_op jit(solution)/shard_map/all_gather | solution.py:650
  40.3 426.2 %all-gather.7.cloned.1.call-start = ((), (), s32[]{:S(2)}) async-start(), calls=%async_computation.9 | async-start | bytes 9437184 | tf_op jit(solution)/shard_map/all_gather | solution.py:650
  41.0 425.5 %all-gather.5.cloned.1.call-start = ((), (), s32[]{:S(2)}) async-start(), calls=%async_computation.8 | async-start | bytes 18874368 | tf_op jit(solution)/shard_map/all_gather | solution.py:650
  44.2 95.1 %all-to-all-start = ((bf16[4,256,2048]{2,1,0:T(8,128)(2,1)}), bf16[4,256,2048]{2,1,0:T(8,128)(2,1)}, u32[]{:S(2)}, u32[]{:S(2)}) async-start(bf16[4,256,2048]{2,1,0:T(8,128)(2,1)} %broadcast_in_dim.74), calls=%async_computation | async-start | bytes 8388608 | tf_op jit(solution)/shard_map/all_to_all | solution.py:47
  52.3 71.3 %collective-permute-start.1 = (bf16[256,1664]{1,0:T(8,128)(2,1)S(1)}, bf16[256,1664]{1,0:T(8,128)(2,1)S(1)}, u32[]{:S(2)}, u32[]{:S(2)}) collective-permute-start(bf16[256,1664]{1,0:T(8,128)(2,1)S(1)} %bitcast.286), channel_id=1, source_target_pairs={{0,4},{2,6},{4,0},{6,2},{1,5},{3,7},{5,1},{7,3},{8,12},{10,14},{12... | collective-permute-start | bytes 2555912 | tf_op jit(solution)/shard_map/ppermute | solution.py:53
  53.5 71.9 %collective-permute-start.2 = (bf16[256,1664]{1,0:T(8,128)(2,1)S(1)}, bf16[256,1664]{1,0:T(8,128)(2,1)S(1)}, u32[]{:S(2)}, u32[]{:S(2)}) collective-permute-start(bf16[256,1664]{1,0:T(8,128)(2,1)S(1)} %bitcast.287), channel_id=1, source_target_pairs={{0,6},{2,0},{4,2},{6,4},{1,7},{3,1},{5,3},{7,5},{8,14},{10,8},{12,... | collective-permute-start | bytes 2555912 | tf_op jit(solution)/shard_map/ppermute | solution.py:53
  55.5 75.1 %collective-permute-start.3 = (bf16[256,1664]{1,0:T(8,128)(2,1)S(1)}, bf16[256,1664]{1,0:T(8,128)(2,1)}, u32[]{:S(2)}, u32[]{:S(2)}) collective-permute-start(bf16[256,1664]{1,0:T(8,128)(2,1)S(1)} %bitcast.288), channel_id=1, source_target_pairs={{0,1},{1,0},{2,3},{3,2},{4,5},{5,4},{6,7},{7,6},{8,9},{9,8},{10,11... | collective-permute-start | bytes 2555912 | tf_op jit(solution)/shard_map/ppermute | solution.py:143
  171.6 71.3 %collective-permute-start.10 = (bf16[256,2048]{1,0:T(8,128)(2,1)}, bf16[256,2048]{1,0:T(8,128)(2,1)}, u32[]{:S(2)}, u32[]{:S(2)}) collective-permute-start(bf16[256,2048]{1,0:T(8,128)(2,1)} %bitcast.20.refs_0_), channel_id=1, source_target_pairs={{0,6},{2,0},{4,2},{6,4},{1,7},{3,1},{5,3},{7,5},{8,14},{10,8},{12,... | collective-permute-start | bytes 3145736 | tf_op jit(solution)/shard_map/ppermute | solution.py:53
  171.6 73.7 %collective-permute-start.11 = (bf16[256,2048]{1,0:T(8,128)(2,1)}, bf16[256,2048]{1,0:T(8,128)(2,1)}, u32[]{:S(2)}, u32[]{:S(2)}) collective-permute-start(bf16[256,2048]{1,0:T(8,128)(2,1)} %bitcast.20.refs_0_), channel_id=1, source_target_pairs={{0,2},{2,4},{4,6},{6,0},{1,3},{3,5},{5,7},{7,1},{8,10},{10,12},{12... | collective-permute-start | bytes 3145736 | tf_op jit(solution)/shard_map/ppermute | solution.py:53
  173.6 89.8 %collective-permute-start.12 = (bf16[256,2048]{1,0:T(8,128)(2,1)}, bf16[256,2048]{1,0:T(8,128)(2,1)}, u32[]{:S(2)}, u32[]{:S(2)}) collective-permute-start(bf16[256,2048]{1,0:T(8,128)(2,1)} %bitcast.20.refs_0_), channel_id=1, source_target_pairs={{0,4},{2,6},{4,0},{6,2},{1,5},{3,7},{5,1},{7,3},{8,12},{10,14},{12... | collective-permute-start | bytes 3145736 | tf_op jit(solution)/shard_map/ppermute | solution.py:53
  242.9 68.7 %collective-permute-start.13 = (bf16[256,2048]{1,0:T(8,128)(2,1)}, bf16[256,2048]{1,0:T(8,128)(2,1)}, u32[]{:S(2)}, u32[]{:S(2)}) collective-permute-start(bf16[256,2048]{1,0:T(8,128)(2,1)} %bitcast.20.refs_0_), channel_id=1, source_target_pairs={{0,1},{1,0},{2,3},{3,2},{4,5},{5,4},{6,7},{7,6},{8,9},{9,8},{10,11... | collective-permute-start | bytes 3145736 | tf_op jit(solution)/shard_map/ppermute | solution.py:143
  285.0 643.7 %reduce-scatter.5.cloned.1.call-start = ((), (), s32[]{:S(2)}) async-start(), calls=%async_computation.13 | async-start | bytes 18874368 | tf_op jit(solution)/shard_map/reduce_scatter | solution.py:712
  328.6 69.4 %collective-permute-start.18 = (bf16[256,2048]{1,0:T(8,128)(2,1)S(1)}, bf16[256,2048]{1,0:T(8,128)(2,1)S(1)}, u32[]{:S(2)}, u32[]{:S(2)}) collective-permute-start(bf16[256,2048]{1,0:T(8,128)(2,1)S(1)} %multiply_convert_fusion.refs_0_), channel_id=1, source_target_pairs={{0,4},{2,6},{4,0},{6,2},{1,5},{3,7},{5,1},{7,3},{8,12},{10,14},{12... | collective-permute-start | bytes 3145736 | tf_op jit(solution)/shard_map/ppermute | solution.py:53
  329.9 89.7 %collective-permute-start.17 = (bf16[256,2048]{1,0:T(8,128)(2,1)S(1)}, bf16[256,2048]{1,0:T(8,128)(2,1)}, u32[]{:S(2)}, u32[]{:S(2)}) collective-permute-start(bf16[256,2048]{1,0:T(8,128)(2,1)S(1)} %multiply_convert_fusion.refs_0_), channel_id=1, source_target_pairs={{0,2},{2,4},{4,6},{6,0},{1,3},{3,5},{5,7},{7,1},{8,10},{10,12},{12... | collective-permute-start | bytes 3145736 | tf_op jit(solution)/shard_map/ppermute | solution.py:53
  422.5 80.1 %collective-permute-start.23 = (bf16[256,2048]{1,0:T(8,128)(2,1)}, bf16[256,2048]{1,0:T(8,128)(2,1)}, u32[]{:S(2)}, u32[]{:S(2)}) collective-permute-start(bf16[256,2048]{1,0:T(8,128)(2,1)} %add_bitcast_fusion.refs_0_), channel_id=1, source_target_pairs={{0,2},{2,4},{4,6},{6,0},{1,3},{3,5},{5,7},{7,1},{8,10},{10,12},{12... | collective-permute-start | bytes 3145736 | tf_op jit(solution)/shard_map/ppermute | solution.py:53
  425.0 89.4 %collective-permute-start.24 = (bf16[256,2048]{1,0:T(8,128)(2,1)}, bf16[256,2048]{1,0:T(8,128)(2,1)}, u32[]{:S(2)}, u32[]{:S(2)}) collective-permute-start(bf16[256,2048]{1,0:T(8,128)(2,1)} %add_bitcast_fusion.refs_0_), channel_id=1, source_target_pairs={{0,4},{2,6},{4,0},{6,2},{1,5},{3,7},{5,1},{7,3},{8,12},{10,14},{12... | collective-permute-start | bytes 3145736 | tf_op jit(solution)/shard_map/ppermute | solution.py:53
  426.3 89.3 %collective-permute-start.25 = (bf16[256,2048]{1,0:T(8,128)(2,1)}, bf16[256,2048]{1,0:T(8,128)(2,1)}, u32[]{:S(2)}, u32[]{:S(2)}) collective-permute-start(bf16[256,2048]{1,0:T(8,128)(2,1)} %add_bitcast_fusion.refs_0_), channel_id=1, source_target_pairs={{0,6},{2,0},{4,2},{6,4},{1,7},{3,1},{5,3},{7,5},{8,14},{10,8},{12,... | collective-permute-start | bytes 3145736 | tf_op jit(solution)/shard_map/ppermute | solution.py:53
  536.8 446.9 %reduce-scatter.3.cloned.1.call-start = ((), (), s32[]{:S(2)}) async-start(), calls=%async_computation.12 | async-start | bytes 37748736 | tf_op jit(solution)/shard_map/reduce_scatter | solution.py:724
  536.9 85.3 %collective-permute-start.22 = (bf16[256,2048]{1,0:T(8,128)(2,1)}, bf16[256,2048]{1,0:T(8,128)(2,1)}, u32[]{:S(2)}, u32[]{:S(2)}) collective-permute-start(bf16[256,2048]{1,0:T(8,128)(2,1)} %get-tuple-element.55), channel_id=1, source_target_pairs={{0,2},{2,4},{4,6},{6,0},{1,3},{3,5},{5,7},{7,1},{8,10},{10,12},{12... | collective-permute-start | bytes 3145736 | tf_op jit(solution)/shard_map/ppermute | solution.py:60
  536.9 139.1 %collective-permute-start.21 = (bf16[256,2048]{1,0:T(8,128)(2,1)}, bf16[256,2048]{1,0:T(8,128)(2,1)}, u32[]{:S(2)}, u32[]{:S(2)}) collective-permute-start(bf16[256,2048]{1,0:T(8,128)(2,1)} %get-tuple-element.54), channel_id=1, source_target_pairs={{0,4},{2,6},{4,0},{6,2},{1,5},{3,7},{5,1},{7,3},{8,12},{10,14},{12... | collective-permute-start | bytes 3145736 | tf_op jit(solution)/shard_map/ppermute | solution.py:60
  539.3 136.7 %collective-permute-start.20 = (bf16[256,2048]{1,0:T(8,128)(2,1)}, bf16[256,2048]{1,0:T(8,128)(2,1)}, u32[]{:S(2)}, u32[]{:S(2)}) collective-permute-start(bf16[256,2048]{1,0:T(8,128)(2,1)} %get-tuple-element.53), channel_id=1, source_target_pairs={{0,6},{2,0},{4,2},{6,4},{1,7},{3,1},{5,3},{7,5},{8,14},{10,8},{12,... | collective-permute-start | bytes 3145736 | tf_op jit(solution)/shard_map/ppermute | solution.py:60
  618.9 100.8 %collective-permute-start.26 = (bf16[256,2176]{1,0:T(8,128)(2,1)}, bf16[256,2176]{1,0:T(8,128)(2,1)}, u32[]{:S(2)}, u32[]{:S(2)}) collective-permute-start(bf16[256,2176]{1,0:T(8,128)(2,1)} %get-tuple-element.68), channel_id=1, source_target_pairs={{0,6},{2,0},{4,2},{6,4},{1,7},{3,1},{5,3},{7,5},{8,14},{10,8},{12,... | collective-permute-start | bytes 3342344 | tf_op jit(solution)/shard_map/ppermute | solution.py:60
  619.0 101.8 %collective-permute-start.27 = (bf16[256,2176]{1,0:T(8,128)(2,1)}, bf16[256,2176]{1,0:T(8,128)(2,1)}, u32[]{:S(2)}, u32[]{:S(2)}) collective-permute-start(bf16[256,2176]{1,0:T(8,128)(2,1)} %get-tuple-element.69), channel_id=1, source_target_pairs={{0,4},{2,6},{4,0},{6,2},{1,5},{3,7},{5,1},{7,3},{8,12},{10,14},{12... | collective-permute-start | bytes 3342344 | tf_op jit(solution)/shard_map/ppermute | solution.py:60
  622.2 100.5 %collective-permute-start.28 = (bf16[256,2176]{1,0:T(8,128)(2,1)}, bf16[256,2176]{1,0:T(8,128)(2,1)}, u32[]{:S(2)}, u32[]{:S(2)}) collective-permute-start(bf16[256,2176]{1,0:T(8,128)(2,1)} %get-tuple-element.70), channel_id=1, source_target_pairs={{0,2},{2,4},{4,6},{6,0},{1,3},{3,5},{5,7},{7,1},{8,10},{10,12},{12... | collective-permute-start | bytes 3342344 | tf_op jit(solution)/shard_map/ppermute | solution.py:60
  777.8 90.4 %collective-permute-start.34 = (bf16[256,2048]{1,0:T(8,128)(2,1)}, bf16[256,2048]{1,0:T(8,128)(2,1)}, u32[]{:S(2)}, u32[]{:S(2)}) collective-permute-start(bf16[256,2048]{1,0:T(8,128)(2,1)} %get-tuple-element.149), channel_id=1, source_target_pairs={{0,4},{2,6},{4,0},{6,2},{1,5},{3,7},{5,1},{7,3},{8,12},{10,14},{12... | collective-permute-start | bytes 3145736 | tf_op jit(solution)/shard_map/ppermute | solution.py:60
  781.6 90.0 %collective-permute-start.33 = (bf16[256,2048]{1,0:T(8,128)(2,1)}, bf16[256,2048]{1,0:T(8,128)(2,1)}, u32[]{:S(2)}, u32[]{:S(2)}) collective-permute-start(bf16[256,2048]{1,0:T(8,128)(2,1)} %get-tuple-element.147), channel_id=1, source_target_pairs={{0,6},{2,0},{4,2},{6,4},{1,7},{3,1},{5,3},{7,5},{8,14},{10,8},{12,... | collective-permute-start | bytes 3145736 | tf_op jit(solution)/shard_map/ppermute | solution.py:60
  805.6 71.0 %collective-permute-start.31 = (f32[2,1024]{0,1:T(8,128)}, f32[2,1024]{0,1:T(8,128)S(1)}, u32[]{:S(2)}, u32[]{:S(2)}) collective-permute-start(f32[2,1024]{0,1:T(8,128)} %copy.179), channel_id=1, source_target_pairs={{0,24},{8,0},{16,8},{24,16},{1,25},{9,1},{17,9},{25,17},{2,26},{10... | collective-permute-start | bytes 24584 | tf_op jit(solution)/shard_map/ppermute | solution.py:53
  807.9 68.6 %collective-permute-start.30 = (f32[2,1024]{0,1:T(8,128)}, f32[2,1024]{0,1:T(8,128)}, u32[]{:S(2)}, u32[]{:S(2)}) collective-permute-start(f32[2,1024]{0,1:T(8,128)} %copy.179), channel_id=1, source_target_pairs={{0,16},{8,24},{16,0},{24,8},{1,17},{9,25},{17,1},{25,9},{2,18},{10... | collective-permute-start | bytes 24584 | tf_op jit(solution)/shard_map/ppermute | solution.py:53
  924.8 90.0 %collective-permute-start.38 = (bf16[256,2048]{1,0:T(8,128)(2,1)}, bf16[256,2048]{1,0:T(8,128)(2,1)}, u32[]{:S(2)}, u32[]{:S(2)}) collective-permute-start(bf16[256,2048]{1,0:T(8,128)(2,1)} %get-tuple-element.145), channel_id=1, source_target_pairs={{0,8},{8,16},{16,24},{24,0},{1,9},{9,17},{17,25},{25,1},{2,10},{10... | collective-permute-start | bytes 3145736 | tf_op jit(solution)/shard_map/ppermute | solution.py:60
  924.9 90.0 %collective-permute-start.37 = (bf16[256,2048]{1,0:T(8,128)(2,1)}, bf16[256,2048]{1,0:T(8,128)(2,1)}, u32[]{:S(2)}, u32[]{:S(2)}) collective-permute-start(bf16[256,2048]{1,0:T(8,128)(2,1)} %get-tuple-element.146), channel_id=1, source_target_pairs={{0,16},{8,24},{16,0},{24,8},{1,17},{9,25},{17,1},{25,9},{2,18},{10... | collective-permute-start | bytes 3145736 | tf_op jit(solution)/shard_map/ppermute | solution.py:60
  943.0 71.9 %collective-permute-start.36 = (bf16[256,2048]{1,0:T(8,128)(2,1)}, bf16[256,2048]{1,0:T(8,128)(2,1)}, u32[]{:S(2)}, u32[]{:S(2)}) collective-permute-start(bf16[256,2048]{1,0:T(8,128)(2,1)} %get-tuple-element.144), channel_id=1, source_target_pairs={{0,24},{8,0},{16,8},{24,16},{1,25},{9,1},{17,9},{25,17},{2,26},{10... | collective-permute-start | bytes 3145736 | tf_op jit(solution)/shard_map/ppermute | solution.py:60
  (91 other events, 2188.0 us)
Sparse Core Ops, SparseCore 0:
  31.1 91.8 all-gather.10
  125.0 125.0 all-gather.8
  252.0 64.1 all-gather.6
  317.9 89.8 all-gather.4
  536.9 115.8 reduce-scatter.4
  719.8 263.8 reduce-scatter.2

commit v3 on v2

--- a/solution.py
+++ b/solution.py
@@ -23,7 +23,7 @@
 KERNEL_PARAMS = pltpu.CompilerParams(vmem_limit_bytes=VMEM_BYTES)
 SMALL_COST = pl.CostEstimate(flops=1, bytes_accessed=1, transcendentals=0)
 DOWN_GRAD_COST = pl.CostEstimate(flops=10**11, bytes_accessed=1, transcendentals=0)
-ATTEND_BACK_COST = pl.CostEstimate(flops=345 * 10**9, bytes_accessed=1, transcendentals=0)
+ATTEND_BACK_COST = pl.CostEstimate(flops=250 * 10**9, bytes_accessed=1, transcendentals=0)
 
 
 def after(value, other):
@@ -96,7 +96,8 @@
 
 
 def sum_all(value, axis):
-    return add_up(gather_near(value, axis))
+    count = lax.axis_size(axis)
+    return jnp.sum(exchange(jnp.broadcast_to(value[None], (count,) + value.shape), axis), axis=0)
 
 
 def assemble_kernel(groups, parts, place_ref, *refs):
@@ -153,14 +154,14 @@
     return assemble(blocks, places, groups)
 
 
-def scatter_core(stacked, axis):
-    if lax.axis_size(axis) != 2:
-        return lax.psum_scatter(stacked, axis, scatter_dimension=0, tiled=False)
-    own = lax.axis_index(axis)
-    kept = lax.dynamic_index_in_dim(stacked, own, 0, keepdims=False)
-    given = lax.dynamic_index_in_dim(stacked, 1 - own, 0, keepdims=False)
+def scatter_core(terms, axis, earlier=()):
+    if len(terms) == 1:
+        return lax.psum_scatter(terms[0], axis, scatter_dimension=0, tiled=False)
+    kept, given = terms
+    for array in earlier:
+        given = after(given, array)
     received = lax.ppermute(given, axis, swap_pairs(2, 1))
-    return (kept.astype(f32) + received.astype(f32)).astype(stacked.dtype)
+    return (kept.astype(f32) + received.astype(f32)).astype(kept.dtype)
 
 
 def rms_inverse(values):
@@ -252,12 +253,14 @@
 
 
 def attend_back_kernel(
-    query_ref, key_ref, value_ref, grad_ref, turn_ref, row_seg_ref, col_seg_ref,
-    query_out_ref, key_out_ref, value_out_ref, key_sum_ref, value_sum_ref,
+    query_ref, key_ref, value_ref, grad_ref, query_pre_ref, key_pre_ref, gain_ref, turn_ref,
+    row_seg_ref, col_seg_ref, earlier_ref,
+    query_out_ref, key_out_ref, value_out_ref, inner_ref, key_sum_ref, value_sum_ref,
 ):
     length = query_ref.shape[0]
     scale = HEAD_DIM ** (-0.5)
     cosines, sines = turn_ref[0], -turn_ref[1]
+    first = pl.program_id(0) == 0
     for start in reversed(range(0, length, ATT_BLOCK)):
         stop = start + ATT_BLOCK
         query_rows, grad_rows, keys = query_ref[start:stop], grad_ref[start:stop], key_ref[:stop]
@@ -269,7 +272,11 @@
         inner = jnp.sum(probs * prob_grad, axis=1, keepdims=True)
         score_grad = (probs * (prob_grad - inner)).astype(bf16)
         query_grad = (dot(score_grad, keys, 1, 0) * scale).astype(bf16).astype(f32)
-        query_out_ref[start:stop] = turn(query_grad, cosines[start:stop], sines[start:stop])
+        query_grad = turn(query_grad, cosines[start:stop], sines[start:stop])
+        query_out_ref[start:stop] = query_grad
+        query_inner = query_grad * gain_ref[0:1, :] * query_pre_ref[start:stop]
+        query_inner = jnp.sum(query_inner, axis=1, keepdims=True)
+        inner_ref[start:stop, 0:1] = query_inner + jnp.where(first, 0.0, inner_ref[start:stop, 0:1])
         key_terms = dot(score_grad, query_rows, 0, 0)
         if stop == length:
             key_sum_ref[...] = key_terms
@@ -278,11 +285,16 @@
             key_sum_ref[:stop] += key_terms
             value_sum_ref[:stop] += value_terms
     key_grad = (key_sum_ref[...] * scale).astype(bf16).astype(f32)
-    key_out_ref[...] = turn(key_grad, cosines, sines)
+    key_grad = turn(key_grad, cosines, sines)
+    key_out_ref[...] = key_grad
+    key_inner = jnp.sum(key_grad * gain_ref[1:2, :] * key_pre_ref[...], axis=1, keepdims=True)
+    inner_ref[:, 1:2] = key_inner + jnp.where(first, 0.0, inner_ref[:, 1:2])
     value_out_ref[...] = value_sum_ref[...].astype(bf16)
 
 
-def attend_back(queries, keys, values, grads, turns, row_segment, col_segment, heads):
+def attend_back(
+    queries, keys, values, grads, projected, gains, turns, row_segment, col_segment, earlier, heads
+):
     length = queries.shape[0]
     column = pl.BlockSpec((length, HEAD_DIM), lambda h: (0, h))
     whole = lambda shape: pl.BlockSpec(shape, lambda h: (0,) * len(shape))
@@ -290,30 +302,104 @@
     return pl.pallas_call(
         attend_back_kernel,
         grid=(heads,),
-        in_specs=[column] * 4 + [whole(turns.shape), whole(row_segment.shape), whole(col_segment.shape)],
-        out_specs=[column] * 3,
+        in_specs=[column] * 4
+        + [column, pl.BlockSpec((length, HEAD_DIM), lambda h: (0, heads + h))]
+        + [pl.BlockSpec((2, HEAD_DIM), lambda h: (0, h))]
+        + [whole(turns.shape), whole(row_segment.shape), whole(col_segment.shape)]
+        + [pl.BlockSpec(memory_space=pl.ANY)],
+        out_specs=[column] * 3 + [whole((length, 2))],
         out_shape=[
             jax.ShapeDtypeStruct(shape, f32),
             jax.ShapeDtypeStruct(shape, f32),
             jax.ShapeDtypeStruct(shape, bf16),
+            jax.ShapeDtypeStruct((length, 2), f32),
         ],
         scratch_shapes=[pltpu.VMEM((length, HEAD_DIM), f32)] * 2,
         compiler_params=KERNEL_PARAMS,
         cost_estimate=ATTEND_BACK_COST,
         name="attend_back",
-    )(queries, keys, values, grads, turns, row_segment, col_segment)
+    )(
+        queries, keys, values, grads, projected, projected, gains, turns, row_segment, col_segment, earlier
+    )
+
+
+def interleave_kernel(*refs):
+    expert = 0
+    for ref in refs[:-1]:
+        for k in range(ref.shape[0]):
+            refs[-1][:, expert, :] = ref[k].astype(f32)
+            expert += 1
+
+
+def interleave(parts):
+    _, rows, width = parts[0].shape
+    experts = sum(part.shape[0] for part in parts)
+    block = min(rows, 64)
+    return pl.pallas_call(
+        interleave_kernel,
+        grid=(rows // block,),
+        in_specs=[
+            pl.BlockSpec((part.shape[0], block, width), lambda i: (0, i, 0)) for part in parts
+        ],
+        out_specs=pl.BlockSpec((block, experts, width), lambda i: (i, 0, 0)),
+        out_shape=jax.ShapeDtypeStruct((rows, experts, width), f32),
+        compiler_params=KERNEL_PARAMS,
+        cost_estimate=SMALL_COST,
+        name="interleave",
+    )(*parts)
+
+
+def norm_back_kernel(
+    query_grad_ref, key_grad_ref, value_grad_ref, query_pre_ref, key_pre_ref, scale_ref, mean_ref, gain_ref,
+    out_ref, gain_grad_ref,
+):
+    width = query_grad_ref.shape[1]
+
+    @pl.when(pl.program_id(0) == 0)
+    def _():
+        gain_grad_ref[...] = jnp.zeros_like(gain_grad_ref)
+
+    for part, (grad_ref, pre_ref) in enumerate(
+        ((query_grad_ref, query_pre_ref), (key_grad_ref, key_pre_ref))
+    ):
+        here = slice(part, part + 1)
+        grad, scale = grad_ref[...], scale_ref[:, here]
+        normal = pre_ref[...] * scale
+        gain_grad_ref[here, :] += jnp.sum(grad * normal, axis=0, keepdims=True)
+        back = scale * (grad * gain_ref[here, :]) - normal * (scale * scale * mean_ref[:, here])
+        out_ref[:, part * width : (part + 1) * width] = back.astype(bf16)
+    out_ref[:, 2 * width :] = value_grad_ref[...]
+
+
+def norm_back(query_grad, key_grad, value_grad, projected, scales, means, gains):
+    length, width = query_grad.shape
+    block = min(length, 256)
+    rows = lambda columns, part: pl.BlockSpec((block, columns), lambda i: (i, part))
+    whole = lambda shape: pl.BlockSpec(shape, lambda i: (0,) * len(shape))
+    return pl.pallas_call(
+        norm_back_kernel,
+        grid=(length // block,),
+        in_specs=[rows(width, 0)] * 3
+        + [rows(width, 0), rows(width, 1), rows(2, 0), rows(2, 0), whole(gains.shape)],
+        out_specs=[rows(3 * width, 0), whole(gains.shape)],
+        out_shape=[
+            jax.ShapeDtypeStruct((length, 3 * width), bf16),
+            jax.ShapeDtypeStruct(gains.shape, f32),
+        ],
+        compiler_params=KERNEL_PARAMS,
+        cost_estimate=SMALL_COST,
+        name="norm_back",
+    )(query_grad, key_grad, value_grad, projected, projected, scales, means, gains)
 
 
 def chunk_of(width, most):
     return most if width % most == 0 else width
 
 
-def forward_kernel(count, kept, pick_ref, gate_ref, in_ref, down_ref, *refs):
+def forward_kernel(count, kept, place_ref, pick_ref, gate_ref, in_ref, down_ref, *refs):
     near_refs, refs = refs[:count], refs[count:]
     earlier_refs, refs = refs[4:kept], refs[kept:]
-    rows_ref, gate_out_ref, up_out_ref, gated_ref = refs[:4]
-    mix_refs = refs[4 : count + 4]
-    result_ref, sums_ref = refs[count + 4 :]
+    rows_ref, gate_out_ref, up_out_ref, gated_ref, mix_ref, result_ref, sums_ref = refs
     step_number, steps = pl.program_id(0), pl.num_programs(0)
     capacity, width = pick_ref.shape[2], rows_ref.shape[2]
     hidden = gated_ref.shape[2]
@@ -355,37 +441,39 @@
         for k in range(count):
             mix = sums_ref[k]
             if earlier_refs:
-                mix = mix + earlier_refs[k][...].astype(f32)
-            mix_refs[k][...] = mix.astype(bf16)
-
-
-def experts_forward(first, kept, pick, gates, in_weight, down_weight, near):
+                mix = mix + earlier_refs[0][place_ref[k]].astype(f32)
+            mix_ref[place_ref[k]] = mix.astype(bf16)
+
+
+def experts_forward(first, kept, places, pick, gates, in_weight, down_weight, near):
     experts, count, capacity, tokens = pick.shape
     here, width, hidden = in_weight.shape[0], in_weight.shape[1], down_weight.shape[2]
     rows = count * capacity
     each = lambda shape: pl.BlockSpec((1,) + shape, lambda e: (first + e,) + (0,) * len(shape))
     near_each = lambda shape: pl.BlockSpec((1,) + shape, lambda e: (e,) + (0,) * len(shape))
     whole = pl.BlockSpec((tokens, width), lambda e: (0, 0), pipeline_mode=pl.Buffered(1))
+    sums = pl.BlockSpec((count, tokens, width), lambda e: (0, 0, 0), pipeline_mode=pl.Buffered(1))
     return pl.pallas_call(
         functools.partial(forward_kernel, count, len(kept)),
         grid=(here,),
         in_specs=[
+            pl.BlockSpec(memory_space=pltpu.SMEM),
             each((count, capacity, tokens)), each((rows, 1)),
             near_each((width, 2 * hidden)), near_each((width, hidden)),
-        ] + [whole] * count + [pl.BlockSpec(memory_space=pl.ANY)] * len(kept[:4]) + [whole] * len(kept[4:]),
-        out_specs=[each((rows, width))] + [each((rows, hidden))] * 3 + [whole] * count,
+        ] + [whole] * count + [pl.BlockSpec(memory_space=pl.ANY)] * len(kept[:4]) + [sums] * len(kept[4:]),
+        out_specs=[each((rows, width))] + [each((rows, hidden))] * 3 + [sums],
         out_shape=[jax.ShapeDtypeStruct((experts, rows, width), bf16)]
         + [jax.ShapeDtypeStruct((experts, rows, hidden), bf16)] * 3
-        + [jax.ShapeDtypeStruct((tokens, width), bf16)] * count,
+        + [jax.ShapeDtypeStruct((count, tokens, width), bf16)],
         scratch_shapes=[
             pltpu.VMEM((rows, chunk_of(width, 1024)), bf16),
             pltpu.VMEM((count, tokens, width), f32),
         ],
-        input_output_aliases={4 + count + i: i for i in range(len(kept[:4]))},
+        input_output_aliases={5 + count + i: i for i in range(len(kept[:4]))},
         compiler_params=KERNEL_PARAMS,
         cost_estimate=SMALL_COST,
         name="experts_forward",
-    )(pick, gates, in_weight, down_weight, *near, *kept)
+    )(places, pick, gates, in_weight, down_weight, *near, *kept)
 
 
 def down_grad_kernel(count, pick_ref, gated_ref, *refs):
@@ -535,7 +623,7 @@
 
 
 def experts_in_grad(rows, both, earlier):
-    experts, count, width = rows.shape
+    experts, _, width = rows.shape
     each = lambda shape: pl.BlockSpec((1,) + shape, lambda e: (e,) + (0,) * len(shape))
     return pl.pallas_call(
         in_grad_kernel,
@@ -549,35 +637,59 @@
     )(rows, both, earlier)
 
 
-def spread_kernel(split, left_ref, right_ref, *refs):
+def spread_kernel(split, outs, own_ref, left_ref, right_ref, *refs):
     groups, parts, cores = split
-    out_ref = refs[-1]
+    extra_refs, out_refs = refs[:-outs], refs[-outs:]
     width = right_ref.shape[1]
-    rows = out_ref.shape[2] // groups
+    rows = out_refs[0].shape[-2] // groups
     each = parts * cores * rows
+
+    def store(core, place, columns, values):
+        if outs == 1:
+            out_refs[0][(core,) + place + (columns,)] = values
+            return
+        for index, ref in enumerate(out_refs):
+
+            @pl.when(own_ref[0] == (core if index == 0 else 1 - core))
+            def _():
+                ref[place + (columns,)] = values
+
     for group in range(groups):
-        terms = dot(left_ref[:, group * each : (group + 1) * each], right_ref[...], 0, 0).astype(bf16)
+        here = slice(group * each, (group + 1) * each)
+        terms = dot(left_ref[:, here], right_ref[...], 0, 0)
+        low_terms = terms.astype(bf16)
+        if extra_refs:
+            beside_ref, weight_ref, gain_ref = extra_refs
+            sums = jnp.sum(terms * weight_ref[here, :width].astype(f32), axis=1, keepdims=True)
+            beside = beside_ref[here, :]
+            lane = lax.broadcasted_iota(jnp.int32, beside.shape, 1)
+            beside = jnp.where(lane == 0, sums / gain_ref[here, :], beside).astype(bf16)
         for part in range(parts):
             for core in range(cores):
                 start = (part * cores + core) * rows
-                place = pl.ds(group * rows, rows)
-                out_ref[core, part, place, :width] = terms[start : start + rows]
-                if len(refs) > 1:
-                    begin = group * each + start
-                    out_ref[core, part, place, width:] = refs[0][begin : begin + rows, :]
-
-
-def spread_product(left, right, beside, split):
+                place = (part, slice(group * rows, (group + 1) * rows))
+                store(core, place, slice(0, width), low_terms[start : start + rows])
+                if extra_refs:
+                    columns = slice(width, width + beside.shape[1])
+                    store(core, place, columns, beside[start : start + rows])
+
+
+def spread_product(left, right, beside, split, own_core):
     groups, parts, cores = split
     rows = left.shape[1] // (groups * parts * cores)
-    width = right.shape[1] + sum(array.shape[1] for array in beside)
+    width = right.shape[1] + (beside[0].shape[1] if beside else 0)
+    shape = (parts, groups * rows, width)
+    shapes = [shape] * 2 if cores == 2 else [(cores,) + shape]
+    arrays = [left, right] + beside
     return pl.pallas_call(
-        functools.partial(spread_kernel, split),
-        out_shape=jax.ShapeDtypeStruct((cores, parts, groups * rows, width), bf16),
+        functools.partial(spread_kernel, split, len(shapes)),
+        in_specs=[pl.BlockSpec(memory_space=pltpu.SMEM)]
+        + [pl.BlockSpec(memory_space=pltpu.VMEM)] * len(arrays),
+        out_shape=[jax.ShapeDtypeStruct(shape, bf16) for shape in shapes],
         compiler_params=KERNEL_PARAMS,
         cost_estimate=SMALL_COST,
         name="spread_product",
-    )(left, right, *beside)
+    )(jnp.reshape(own_core.astype(jnp.int32), (1,)), *arrays)
 
 
 def on_device(
@@ -630,18 +742,19 @@
     small = heads_all[:, 3 * head_cols : first_id].T
     gains = small[:4].astype(f32)
     router_rows = small[4:]
-    all_tokens = jnp.broadcast_to(own_low[None], (seq_count, tok_count, model_width))
-    all_tokens = exchange(all_tokens, "seq").reshape(length, model_width)
-
-    out_rows = after(w_out, all_tokens)[None]
+    out_rows = after(w_out, heads_seq)[None]
     out_rows = exchange(jnp.broadcast_to(out_rows, (seq_count,) + w_out.shape), "seq")
     out_rows = out_rows.reshape(seq_count * rows_dev, model_width)
+    all_tokens = after(own_low, out_rows)[None]
+    all_tokens = jnp.broadcast_to(all_tokens, (seq_count, tok_count, model_width))
+    all_tokens = exchange(all_tokens, "seq").reshape(length, model_width)
+
     out_near = gather_near(after(out_rows, heads_near[-1]), "exp")
 
     parts = 2 if exp_dev % 2 == 0 else 1
     part_experts = exp_dev // parts
-    in_blocks = jnp.transpose(after(expert_in, heads_seq), (1, 0, 2))
-    down_blocks = jnp.transpose(after(expert_out, heads_seq), (1, 0, 2))
+    in_blocks = jnp.transpose(after(expert_in, out_rows), (1, 0, 2))
+    down_blocks = jnp.transpose(after(expert_out, out_rows), (1, 0, 2))
     in_weights, down_weights = [], []
     for part in range(parts):
         chosen_experts = slice(part * part_experts, (part + 1) * part_experts)
@@ -659,11 +772,13 @@
     squares = jnp.stack([jnp.sum(query_pre * query_pre, axis=-1), jnp.sum(key_pre * key_pre, axis=-1)])
     squares = sum_all(squares, "seq")
     scales = lax.rsqrt(squares / model_width + epsilon).T
-    query_inverse, key_inverse = scales[:, 0:1], scales[:, 1:2]
     turns = rotary_tables(jnp.arange(length, dtype=jnp.int32), HEAD_DIM)
     row_segment, col_segment = segment[:, None], segment[None, :]
+    ready = scales
+    for near in out_near[1:]:
+        ready = after(ready, near)
     attended, queries, keys, values = attend(
-        projected, after(scales, out_near[-1]), own_gains[1:3], turns, row_segment, col_segment, heads_dev
+        projected, ready, own_gains[1:3], turns, row_segment, col_segment, heads_dev
     )
     out_weight = order_cores(out_near, seq_count, "exp", "fsdp")
     merged = lax.all_to_all(attended, "seq", split_axis=0, concat_axis=1, tiled=True)
@@ -699,14 +814,15 @@
     near_probs = jnp.transpose(near_probs, (2, 0, 1))
     gate_rows = jnp.sum(jnp.where(pick, near_probs[:, :, None, :], 0.0), axis=-1)
     gate_rows = gate_rows.reshape(exp_dev, exp_count * capacity, 1)
+    places = jnp.stack([ring_place(own_exp - k, exp_count) for k in range(exp_count)])
     kept = []
     for part in range(parts):
         kept = experts_forward(
-            part * part_experts, kept, pick_low, gate_rows, in_weights[part], down_weights[part], mlp_near
+            part * part_experts, kept, places.astype(jnp.int32), pick_low, gate_rows,
+            in_weights[part], down_weights[part], mlp_near,
         )
-    expert_rows, gate, up, gated = kept[:4]
-    mix_near = send_near(kept[4:], "exp")
-    output = (residual + add_up(mix_near)).astype(bf16)
+    expert_rows, gate, up, gated, mix = kept
+    output = (residual + jnp.sum(exchange(mix, "exp").astype(f32), axis=0)).astype(bf16)
 
     cot_rows, down_grad = experts_down_grad(pick_low, gated, cot_near)
     grad_expert_out = lax.psum_scatter(
@@ -719,10 +835,10 @@
             in_weights[part], down_weights[part],
         )
     copy_near = send_near(kept[1:], "exp")
-    earlier = jnp.stack([block[:8, :128] for block in kept[1:]] + [output[:8, :128]])
-    in_grad = experts_in_grad(expert_rows, kept[0], earlier)
+    before = jnp.stack([block[:16, :128] for block in kept[1:]])
+    in_grad = experts_in_grad(expert_rows, kept[0], before)
     grad_expert_in = lax.psum_scatter(in_grad, ("seq", "fsdp"), scatter_dimension=1, tiled=True)
-    copy_near[0] = after(copy_near[0], in_grad)
+    copy_near[0] = after(after(copy_near[0], in_grad), output)
     mlp_grad_experts = add_up([near[:, :model_width] for near in copy_near])
     prob_pairs = [
         near[:, model_width : model_width + 2 * exp_dev].astype(f32).reshape(tok_count, exp_dev, 2)
@@ -730,15 +846,19 @@
     ]
     prob_grad = order([jnp.sum(pair, axis=2) for pair in prob_pairs], "exp", 1, 1)
     prob_grad = prob_grad.reshape(tok_count, experts_total)
-    grad_expert_in = jnp.transpose(grad_expert_in, (1, 0, 2)).astype(f32)
-    grad_expert_out = jnp.transpose(grad_expert_out, (1, 0, 2)).astype(f32)
+    grad_expert_in = interleave([grad_expert_in])
+    grad_expert_out = interleave([grad_expert_out])
 
     logit_grad = router_probs * (
         prob_grad - jnp.sum(router_probs * prob_grad, axis=-1, keepdims=True)
     )
     router_grad = jnp.dot(logit_grad.T, mlp_low.astype(f32), precision=highest)
+    logit_high = logit_grad.astype(bf16)
+    logit_low = (logit_grad - logit_high.astype(f32)).astype(bf16)
     mlp_grad = mlp_grad_experts + jnp.dot(
-        logit_grad, router_rows.astype(f32), precision=highest
+        jnp.concatenate([logit_high, logit_low], axis=1),
+        jnp.concatenate([router_rows, router_rows], axis=0),
+        preferred_element_type=f32,
     )
     residual_norm_grad, mlp_gain_grad = rms_back(mlp_grad, residual, mlp_inverse, gains[3])
     residual_grad = cotangent[0].astype(f32) + residual_norm_grad
@@ -749,36 +869,28 @@
         merged_grad.astype(bf16), "seq", split_axis=1, concat_axis=0, tiled=True
     )
     split_sizes = (seq_count, exp_count, core_count)
-    out_terms = spread_product(after(branch_grad, merged_grad), merged, [], split_sizes)
-    out_terms = scatter_core(out_terms, "fsdp")
-    out_terms = scatter(out_terms, "exp").astype(bf16)
-    query_grad, key_grad, value_grad = attend_back(
-        queries, keys, values, heads_grad, turns, row_segment, col_segment, heads_dev
-    )
-    query_scaled, key_scaled = query_grad * own_gains[1], key_grad * own_gains[2]
-    means = jnp.stack(
-        [jnp.sum(query_scaled * query_pre, axis=-1), jnp.sum(key_scaled * key_pre, axis=-1)]
-    )
-    means = after(sum_all(means, "seq") / model_width, out_terms)
-    query_gain_grad = jnp.sum(query_grad * query_pre * query_inverse, axis=0)
-    key_gain_grad = jnp.sum(key_grad * key_pre * key_inverse, axis=0)
-    query_pre_grad = query_inverse * query_scaled - query_pre * query_inverse**3 * means[0][:, None]
-    key_pre_grad = key_inverse * key_scaled - key_pre * key_inverse**3 * means[1][:, None]
-    qkv_grad = jnp.concatenate(
-        [query_pre_grad.astype(bf16), key_pre_grad.astype(bf16), value_grad],
-        axis=1,
-    )
-    attn_in_part = jnp.einsum("tc,dc->td", qkv_grad, heads_weight, preferred_element_type=f32)
-    first_gain_grad = jnp.sum(attn_in_part * all_inputs * first_inverse, axis=0)
-    attn_in_grad = scatter(
-        attn_in_part.astype(bf16).reshape(seq_count, tok_count, model_width), "seq"
-    )
+    out_terms = spread_product(
+        branch_grad, merged, [], split_sizes, lax.axis_index("fsdp")
+    )
+    out_core = scatter_core(out_terms, "fsdp")
+    out_sent = send_near(split(out_core, "exp"), "exp")
+    out_terms = add_up(out_sent).astype(bf16)
+    query_grad, key_grad, value_grad, inner = attend_back(
+        queries, keys, values, heads_grad, projected, own_gains[1:3], turns, row_segment, col_segment,
+        out_core[0, :16, :128], heads_dev,
+    )
+    means = sum_all(inner.T, "seq").T / model_width
+    qkv_grad, head_gain_grads = norm_back(
+        query_grad, key_grad, value_grad, projected, scales, means, own_gains[1:3]
+    )
+    query_gain_grad, key_gain_grad = head_gain_grads[0], head_gain_grads[1]
+
     zero_row = jnp.zeros((model_width,), f32)
     small_terms = jnp.concatenate(
         [
             jnp.stack(
                 [
-                    first_gain_grad,
+                    zero_row,
                     lax.dynamic_update_slice_in_dim(zero_row, query_gain_grad, own_seq * head_cols, 0),
                     lax.dynamic_update_slice_in_dim(zero_row, key_gain_grad, own_seq * head_cols, 0),
                     mlp_gain_grad,
@@ -789,15 +901,28 @@
         axis=0,
     ).T
     small_terms = jnp.pad(small_terms, ((0, 0), (0, -small_cols % 128)))
-    heads_terms = spread_product(attn_low, qkv_grad, [small_terms.astype(bf16)], split_sizes)
-    heads_terms = scatter_core(heads_terms, "fsdp")
+    beside = [small_terms, heads_all, gains[0][:, None]]
+    heads_terms = spread_product(
+        attn_low, qkv_grad, beside, split_sizes, lax.axis_index("fsdp")
+    )
+    heads_terms = scatter_core(heads_terms, "fsdp", out_sent[1:])
+    attn_in_part = jnp.einsum(
+        "tc,dc->td", after(qkv_grad, heads_terms), heads_weight, preferred_element_type=f32
+    )
+    attn_in_grad = exchange(
+        attn_in_part.astype(bf16).reshape(seq_count, tok_count, model_width), "seq"
+    )
+    attn_in_grad = jnp.sum(attn_in_grad.astype(f32), axis=0)
     heads_terms = scatter(heads_terms, "exp").astype(bf16)
-    grad_w_out = scatter(
-        after(out_terms, heads_terms).reshape(seq_count, rows_dev, model_width), "seq"
-    )
-    heads_terms = heads_terms.reshape(seq_count, rows_dev, -1)
-    heads_terms = after(after(heads_terms, grad_expert_in), grad_expert_out)
-    heads_given, heads_terms = heads_terms, exchange(heads_terms, "seq")
+    terms_cols = heads_terms.shape[1]
+    last_terms = jnp.concatenate([heads_terms, out_terms], axis=1)
+    last_near = send_near(split(last_terms.reshape(seq_count, rows_dev, -1), "seq"), "seq")
+    grad_w_out = add_up([near[:, terms_cols:] for near in last_near])
+    small_grad = add_up(
+        [near[:, 3 * head_cols : 3 * head_cols + small_cols] for near in last_near]
+    )
+    heads_terms = order([near[:, : 3 * head_cols] for near in last_near], "seq", 0, 1)
+    heads_terms = after(heads_terms, attn_in_grad)
     grad_w_qkv = jnp.concatenate(
         [
             heads_terms[source, :, part * head_cols : (part + 1) * head_cols]
@@ -806,13 +931,11 @@
         ],
         axis=1,
     ).astype(f32)
+
     own_inverse = lax.dynamic_slice_in_dim(first_inverse, own_seq * tok_count, tok_count, 0)
-    input_norm_grad, _ = rms_back(after(attn_in_grad, heads_given), inputs, own_inverse, gains[0])
+    input_norm_grad, _ = rms_back(attn_in_grad, inputs, own_inverse, gains[0])
     input_grad = residual_grad + input_norm_grad
 
-    small_grad = jnp.sum(
-        heads_terms[:, :, 3 * head_cols : 3 * head_cols + small_cols].astype(f32), axis=0
-    )
     return (
         output[None],
         input_grad[None],

time: 1060 us -> 1010 us (0.953)
  waiting for transfers between devices: 436 us -> 398 us
  local copies, waits for them, and re-layouts: 92.2 us -> 63.4 us
  Pallas kernels: 273 us -> 301 us
  blocking collectives: 15.1 us -> 30.6 us
  other arithmetic: 79 us -> 66.4 us
  starting transfers between devices: 86.1 us -> 73.7 us
    reduce_scatter x1, waiting for transfers between devices: 40.3 us -> 0.01 us  [on_device(): lax.psum_scatter(in_grad, ('seq', 'fsdp'), scatter_dimension=1, tiled=True)]
    ppermute x18 -> x12, waiting for transfers between devices: 125 us -> 152 us  [send_near(): lax.ppermute(blocks[k], axis, shift_pairs(count, -k))]
    unnamed x155 -> x119, local copies, waits for them, and re-layouts: 35 us -> 9.41 us
    pallas_call x2 -> x5, Pallas kernels: 21.7 us -> 46.4 us  [the longest x2 28.7 us: spread_product(): pl.pallas_call(functools.partial(spread_kernel, split, len(shapes)), in_s...]
    all_to_all x1 -> x2, blocking collectives: 15.1 us -> 30.6 us  [exchange(): lax.all_to_all(stacked, axis, split_axis=split_axis, concat_axis=split_ax...]
    ppermute x18 -> x12, waiting for transfers between devices: 228 us -> 215 us  [gather_near(): lax.ppermute(block, axis, shift_pairs(count, k))]
    all_to_all x3 -> x5, waiting for transfers between devices: 15.1 us -> 1.98 us  [exchange(): lax.all_to_all(stacked, axis, split_axis=split_axis, concat_axis=split_ax...]
    all_to_all x1, waiting for transfers between devices: 0.01 us -> 12.2 us  [on_device(): lax.all_to_all(merged_grad.astype(bf16), 'seq', split_axis=1, concat_axis...]
  transfers between devices with their start and end apart: 57 -> 47, of which waited for: 22 -> 22; matrix products, arithmetic and copies ran while one was open for 18% -> 15% of each run, Pallas kernels for 24% -> 27%
where the time goes in v3:
time: 1010 us; the launch traced here: 996 us
  waiting for transfers between devices  398 us (39%)
  Pallas kernels  301 us (30%)
  starting transfers between devices  73.7 us (7%)
  other arithmetic  66.4 us (7%)
  local copies, waits for them, and re-layouts  63.4 us (6%)
  matrix products  35.9 us (4%)
  blocking collectives  30.6 us (3%)
  between operations  26.4 us (3%)
    ppermute x12, waiting for transfers between devices, gather_near(): lax.ppermute(block, axis, shift_pairs(count, k))  215 us
    ppermute x12, waiting for transfers between devices, send_near(): lax.ppermute(blocks[k], axis, shift_pairs(count, -k))  152 us
    pallas_call x2, Pallas kernels, experts_backward(): pl.pallas_call(functools.partial(backward_kernel, first, count, len(kept)...  77.6 us
    pallas_call x2, Pallas kernels, experts_forward(): pl.pallas_call(functools.partial(forward_kernel, count, len(kept)), grid=...  70.1 us
    pallas_call x1, Pallas kernels, experts_in_grad(): pl.pallas_call(in_grad_kernel, grid=(experts,), in_specs=[each(rows.shape...  35.3 us
    all_to_all x2, blocking collectives, exchange(): lax.all_to_all(stacked, axis, split_axis=split_axis, concat_axis=split_ax...  30.6 us
    pallas_call x2, Pallas kernels, spread_product(): pl.pallas_call(functools.partial(spread_kernel, split, len(shapes)), in_s...  28.7 us
    all_to_all x5, starting transfers between devices, exchange(): lax.all_to_all(stacked, axis, split_axis=split_axis, concat_axis=split_ax...  24.2 us
  transfers between devices with their start and end apart: 47, of which 22 were waited for; matrix products, arithmetic and copies ran while one was open for 15% of the time, Pallas kernels for 27%

profile of v3, /device:TPU:10, one launch (start us, length us, event | category | flops | bytes accessed | tf_op | source)
XLA Modules:
  0.0 995.7 jit_solution(390640359336579522)
XLA Ops:
  12.0 15.0 %all_to_all.73 = bf16[4,64,1664]{2,1,0:T(8,128)(2,1)S(1)} all-to-all(bf16[4,64,1664]{2,1,0:T(8,128)(2,1)S(1)} %pad_maximum_fusion.2), channel_id=1, replica_groups=mesh['seq'=4,'exp'=4,'fsdp'=2] {'seq'}, dimensions={0} | all-to-all | bytes 1703936 | tf_op jit(solution)/shard_map/all_to_all | solution.py:47
  28.7 15.7 %all_to_all.74 = bf16[4,64,2048]{2,1,0:T(8,128)(2,1)S(1)} all-to-all(bf16[4,64,2048]{2,1,0:T(8,128)(2,1)S(1)} %broadcast_in_dim.104), channel_id=1, replica_groups=mesh['seq'=4,'exp'=4,'fsdp'=2] {'seq'}, dimensions={0} | all-to-all | bytes 2097152 | tf_op jit(solution)/shard_map/all_to_all | solution.py:47
  48.4 6.8 fusion.7
  73.0 52.3 %collective-permute-done.refs_1_ = bf16[256,1664]{1,0:T(8,128)(2,1)} collective-permute-done((bf16[256,1664]{1,0:T(8,128)(2,1)S(1)}, bf16[256,1664]{1,0:T(8,128)(2,1)}, u32[]{:S(2)}, u32[]{:S(2)}) %collective-permute-start) | collective-permute-done | bytes 852000 | tf_op jit(solution)/shard_map/ppermute | solution.py:53
  125.3 13.9 %collective-permute-done.1.refs_2_ = bf16[256,1664]{1,0:T(8,128)(2,1)} collective-permute-done((bf16[256,1664]{1,0:T(8,128)(2,1)S(1)}, bf16[256,1664]{1,0:T(8,128)(2,1)}, u32[]{:S(2)}, u32[]{:S(2)}) %collective-permute-start.1) | collective-permute-done | bytes 852000 | tf_op jit(solution)/shard_map/ppermute | solution.py:53
  187.6 11.4 %collective-permute-done.9.refs_3_ = bf16[256,2048]{1,0:T(8,128)(2,1)} collective-permute-done((bf16[256,2048]{1,0:T(8,128)(2,1)}, bf16[256,2048]{1,0:T(8,128)(2,1)}, u32[]{:S(2)}, u32[]{:S(2)}) %collective-permute-start.9) | collective-permute-done | bytes 1048608 | tf_op jit(solution)/shard_map/ppermute | solution.py:53
  200.9 40.4 %collective-permute-done.8.refs_2_ = bf16[256,2048]{1,0:T(8,128)(2,1)} collective-permute-done((bf16[256,2048]{1,0:T(8,128)(2,1)}, bf16[256,2048]{1,0:T(8,128)(2,1)}, u32[]{:S(2)}, u32[]{:S(2)}) %collective-permute-start.8) | collective-permute-done | bytes 1048608 | tf_op jit(solution)/shard_map/ppermute | solution.py:53
  245.7 16.4 %attend.1 = (bf16[1024,512]{1,0:T(8,128)(2,1)}, bf16[1024,512]{1,0:T(8,128)(2,1)}, bf16[1024,512]{1,0:T(8,128)(2,1)}, bf16[1024,512]{1,0:T(8,128)(2,1)}) custom-call(f32[1024,1536]{1,0:T(8,128)} %copy-done, f32[1024,1536]{1,0:T(8,128)} %copy-done, f32[1024,1536]{1,0:T(8,128)} %copy-done, f32[1024,2]{1,0:T(8,128)} %add_add_fusion.3.scale_ref, ...), custom_call_target="tpu_custom_call" | custom-call | flops 1 | bytes 1 | tf_op jit(solution)/shard_map/attend/pallas_call | solution.py:239
  272.0 7.0 assemble.3
  278.9 13.3 %all-to-all-done.4 = bf16[4,256,512]{2,1,0:T(8,128)(2,1)} async-done(((bf16[4,256,512]{2,1,0:T(8,128)(2,1)}), bf16[4,256,512]{2,1,0:T(8,128)(2,1)}, u32[]{:S(2)}, u32[]{:S(2)}) %all-to-all-start.4) | async-done | bytes 1048608 | tf_op jit(solution)/shard_map/all_to_all | solution.py:784
  310.6 18.1 %collective-permute-done.16.refs_3_ = bf16[256,2048]{1,0:T(8,128)(2,1)S(1)} collective-permute-done((bf16[256,2048]{1,0:T(8,128)(2,1)S(1)}, bf16[256,2048]{1,0:T(8,128)(2,1)S(1)}, u32[]{:S(2)}, u32[]{:S(2)}) %collective-permute-start.16) | collective-permute-done | bytes 1048608 | tf_op jit(solution)/shard_map/ppermute | solution.py:53
  329.9 42.9 %collective-permute-done.15.refs_2_ = bf16[256,2048]{1,0:T(8,128)(2,1)S(1)} collective-permute-done((bf16[256,2048]{1,0:T(8,128)(2,1)S(1)}, bf16[256,2048]{1,0:T(8,128)(2,1)S(1)}, u32[]{:S(2)}, u32[]{:S(2)}) %collective-permute-start.15) | collective-permute-done | bytes 1048608 | tf_op jit(solution)/shard_map/ppermute | solution.py:53
  374.0 20.4 %collective-permute-done.14.refs_1_ = bf16[256,2048]{1,0:T(8,128)(2,1)} collective-permute-done((bf16[256,2048]{1,0:T(8,128)(2,1)S(1)}, bf16[256,2048]{1,0:T(8,128)(2,1)}, u32[]{:S(2)}, u32[]{:S(2)}) %collective-permute-start.14) | collective-permute-done | bytes 1048608 | tf_op jit(solution)/shard_map/ppermute | solution.py:53
  407.1 34.1 %experts_forward.2 = (bf16[4,576,2048]{2,1,0:T(8,128)(2,1)}, bf16[4,576,1024]{2,1,0:T(8,128)(2,1)}, bf16[4,576,1024]{2,1,0:T(8,128)(2,1)}, bf16[4,576,1024]{2,1,0:T(8,128)(2,1)}, bf16[4,256,2048]{2,1,0:T(8,128)(2,1)}) custom-call(s32[4]{0:T(128)} %pad_add_fusion.1.place_ref, bf16[4,4,144,256]{3,2,1,0:T(8,128)(2,1)} %fusion.12.pick_ref, ...), custom_call_target="tpu_custom_call" | custom-call | flops 1 | bytes 1 | tf_op jit(solution)/shard_map/experts_forward/pallas_call | solution.py:456
  441.3 36.0 %experts_forward.3 = (bf16[4,576,2048]{2,1,0:T(8,128)(2,1)}, bf16[4,576,1024]{2,1,0:T(8,128)(2,1)}, bf16[4,576,1024]{2,1,0:T(8,128)(2,1)}, bf16[4,576,1024]{2,1,0:T(8,128)(2,1)}, bf16[4,256,2048]{2,1,0:T(8,128)(2,1)}) custom-call(s32[4]{0:T(128)} %pad_add_fusion.1.place_ref, ...), custom_call_target="tpu_custom_call", output_to_operand_aliasing={{0}: (9, {}), {1}: (10, {}), {2}: (11, {}), {3}: (12, {})} | custom-call | flops 1 | bytes 1 | tf_op jit(solution)/shard_map/experts_forward/pallas_call | solution.py:456
  477.3 12.2 %collective-permute-done.18.refs_2_ = bf16[256,2048]{1,0:T(8,128)(2,1)} collective-permute-done((bf16[256,2048]{1,0:T(8,128)(2,1)}, bf16[256,2048]{1,0:T(8,128)(2,1)}, u32[]{:S(2)}, u32[]{:S(2)}) %collective-permute-start.18) | collective-permute-done | bytes 1048608 | tf_op jit(solution)/shard_map/ppermute | solution.py:53
  490.6 21.2 %experts_down_grad.1 = (bf16[4,576,2048]{2,1,0:T(8,128)(2,1)}, bf16[4,2048,1024]{2,1,0:T(8,128)(2,1)}) custom-call(bf16[4,4,144,256]{3,2,1,0:T(8,128)(2,1)} %fusion.12.pick_ref, bf16[4,576,1024]{2,1,0:T(8,128)(2,1)} %get-tuple-element.51.gated_ref, bf16[256,2048]{1,0:T(8,128)(2,1)} %add_bitcast_fusion.refs_0_, ...), custom_call_target="tpu_custom_call" | custom-call | flops 99999997952 | bytes 1 | tf_op jit(solution)/shard_map/experts_down_grad/pallas_call | solution.py:501
  516.8 37.7 %experts_backward.2 = (bf16[4,576,2048]{2,1,0:T(8,128)(2,1)}, bf16[256,2176]{1,0:T(8,128)(2,1)}, bf16[256,2176]{1,0:T(8,128)(2,1)}, bf16[256,2176]{1,0:T(8,128)(2,1)}, bf16[256,2176]{1,0:T(8,128)(2,1)}) custom-call(bf16[4,4,144,256]{3,2,1,0:T(8,128)(2,1)} %fusion.12.pick_ref, f32[4,576,1]{2,1,0:T(8,128)} %reshape.288.gate_ref.gate_rows_ref, ...), custom_call_target="tpu_custom_call" | custom-call | flops 1 | bytes 1 | tf_op jit(solution)/shard_map/experts_backward/pallas_call | solution.py:591
  554.5 39.9 %experts_backward.3 = (bf16[4,576,2048]{2,1,0:T(8,128)(2,1)}, bf16[256,2176]{1,0:T(8,128)(2,1)}, bf16[256,2176]{1,0:T(8,128)(2,1)}, bf16[256,2176]{1,0:T(8,128)(2,1)}, bf16[256,2176]{1,0:T(8,128)(2,1)}) custom-call(bf16[4,4,144,256]{3,2,1,0:T(8,128)(2,1)} %fusion.12.pick_ref, ...), custom_call_target="tpu_custom_call", output_to_operand_aliasing={{0}: (7, {})} | custom-call | flops 1 | bytes 1 | tf_op jit(solution)/shard_map/experts_backward/pallas_call | solution.py:591
  603.2 35.3 %experts_in_grad.1 = bf16[4,2048,2048]{2,1,0:T(8,128)(2,1)} custom-call(bf16[4,576,2048]{2,1,0:T(8,128)(2,1)} %get-tuple-element.61.rows_ref, bf16[4,576,2048]{2,1,0:T(8,128)(2,1)} %get-tuple-element.62.both_ref, bf16[4,16,128]{2,1,0:T(8,128)(2,1)} %pad_maximum_fusion.6.earlier_ref), custom_call_target="tpu_custom_call" | custom-call | flops 1 | bytes 1 | tf_op jit(solution)/shard_map/experts_in_grad/pallas_call | solution.py:628
  640.4 39.7 %collective-permute-done.20 = bf16[256,2176]{1,0:T(8,128)(2,1)} collective-permute-done((bf16[256,2176]{1,0:T(8,128)(2,1)}, bf16[256,2176]{1,0:T(8,128)(2,1)}, u32[]{:S(2)}, u32[]{:S(2)}) %collective-permute-start.20) | collective-permute-done | bytes 1114144 | tf_op jit(solution)/shard_map/ppermute | solution.py:60
  682.0 20.6 %collective-permute-done.22 = bf16[256,2176]{1,0:T(8,128)(2,1)} collective-permute-done((bf16[256,2176]{1,0:T(8,128)(2,1)}, bf16[256,2176]{1,0:T(8,128)(2,1)}, u32[]{:S(2)}, u32[]{:S(2)}) %collective-permute-start.22) | collective-permute-done | bytes 1114144 | tf_op jit(solution)/shard_map/ppermute | solution.py:60
  715.8 9.0 spread_product.2
  751.8 12.2 %all-to-all-done.6 = bf16[256,4,512]{2,0,1:T(8,128)(2,1)} async-done(((bf16[256,4,512]{2,0,1:T(8,128)(2,1)}), bf16[256,4,512]{2,0,1:T(8,128)(2,1)}, u32[]{:S(2)}, u32[]{:S(2)}) %all-to-all-start.6) | async-done | bytes 1048608 | tf_op jit(solution)/shard_map/all_to_all | solution.py:868
  764.0 21.5 %attend_back.1 = (f32[1024,512]{1,0:T(8,128)}, f32[1024,512]{1,0:T(8,128)}, bf16[1024,512]{1,0:T(8,128)(2,1)}, f32[1024,2]{1,0:T(8,128)}) custom-call(bf16[1024,512]{1,0:T(8,128)(2,1)} %get-tuple-element.66.query_ref, bf16[1024,512]{1,0:T(8,128)(2,1)} %get-tuple-element.67.key_ref, bf16[1024,512]{1,0:T(8,128)(2,1)} %get-tuple-element.68.value_ref, ...), custom_call_target="tpu_custom_call" | custom-call | flops 249999998976 | bytes 1 | tf_op jit(solution)/shard_map/attend_back/pallas_call | solution.py:302
  795.9 6.8 norm_back.1
  805.8 19.6 %spread_product.3 = (bf16[4,256,1664]{2,1,0:T(8,128)(2,1)}, bf16[4,256,1664]{2,1,0:T(8,128)(2,1)}) custom-call(s32[1]{0:T(128)} %bitcast.70.own_ref, bf16[1024,2048]{1,0:T(8,128)(2,1)} %copy-done.5, bf16[1024,1536]{1,0:T(8,128)(2,1)} %get-tuple-element.75.right_ref, f32[2048,128]{1,0:T(8,128)} %pad.14.refs_0_, bf16[2048,1664]{1,0:T(8,128)(2,1)} %assemble.2.refs_1_, ...), custom_call_target="tpu_custom_call" | custom-call | flops 1 | bytes 1 | tf_op jit(solution)/shard_map/spread_product/pallas_call | solution.py:684
  827.3 12.3 %collective-permute-done.25 = bf16[256,2048]{1,0:T(8,128)(2,1)} collective-permute-done((bf16[256,2048]{1,0:T(8,128)(2,1)}, bf16[256,2048]{1,0:T(8,128)(2,1)}, u32[]{:S(2)}, u32[]{:S(2)}) %collective-permute-start.25) | collective-permute-done | bytes 1048608 | tf_op jit(solution)/shard_map/ppermute | solution.py:60
  866.8 8.2 fusion.8
  883.4 51.8 %collective-permute-done.29 = bf16[256,1664]{1,0:T(8,128)(2,1)} collective-permute-done((bf16[256,1664]{1,0:T(8,128)(2,1)}, bf16[256,1664]{1,0:T(8,128)(2,1)}, u32[]{:S(2)}, u32[]{:S(2)}) %collective-permute-start.29) | collective-permute-done | bytes 852000 | tf_op jit(solution)/shard_map/ppermute | solution.py:60
  945.2 10.2 %collective-permute-done.33 = bf16[64,3712]{1,0:T(8,128)(2,1)S(1)} collective-permute-done((bf16[64,3712]{1,0:T(8,128)(2,1)S(1)}, bf16[64,3712]{1,0:T(8,128)(2,1)S(1)}, u32[]{:S(2)}, u32[]{:S(2)}) %collective-permute-start.33) | collective-permute-done | bytes 475168 | tf_op jit(solution)/shard_map/ppermute | solution.py:60
  955.4 10.4 %collective-permute-done.32 = bf16[64,3712]{1,0:T(8,128)(2,1)S(1)} collective-permute-done((bf16[64,3712]{1,0:T(8,128)(2,1)S(1)}, bf16[64,3712]{1,0:T(8,128)(2,1)S(1)}, u32[]{:S(2)}, u32[]{:S(2)}) %collective-permute-start.32) | collective-permute-done | bytes 475168 | tf_op jit(solution)/shard_map/ppermute | solution.py:60
  (370 shorter events, 257.1 us)
Async XLA Ops:
  7.2 399.9 %all-gather.11.cloned.1.call-start = ((), (), s32[]{:S(2)}) async-start(), calls=%async_computation.14 | async-start | bytes 9437184 | tf_op jit(solution)/shard_map/all_gather | solution.py:763
  48.3 358.8 %all-gather.9.cloned.1.call-start = ((), (), s32[]{:S(2)}) async-start(), calls=%async_computation.13 | async-start | bytes 18874368 | tf_op jit(solution)/shard_map/all_gather | solution.py:763
  57.5 383.7 %all-gather.7.cloned.1.call-start = ((), (), s32[]{:S(2)}) async-start(), calls=%async_computation.12 | async-start | bytes 9437184 | tf_op jit(solution)/shard_map/all_gather | solution.py:763
  58.3 383.0 %all-gather.5.cloned.1.call-start = ((), (), s32[]{:S(2)}) async-start(), calls=%async_computation.11 | async-start | bytes 18874368 | tf_op jit(solution)/shard_map/all_gather | solution.py:763
  61.6 100.7 %all-to-all-start.2 = ((bf16[4,256,2048]{2,1,0:T(8,128)(2,1)}), bf16[4,256,2048]{2,1,0:T(8,128)(2,1)}, u32[]{:S(2)}, u32[]{:S(2)}) async-start(bf16[4,256,2048]{2,1,0:T(8,128)(2,1)} %broadcast_in_dim.106), calls=%async_computation.2 | async-start | bytes 8388608 | tf_op jit(solution)/shard_map/all_to_all | solution.py:47
  67.8 57.5 %collective-permute-start = (bf16[256,1664]{1,0:T(8,128)(2,1)S(1)}, bf16[256,1664]{1,0:T(8,128)(2,1)}, u32[]{:S(2)}, u32[]{:S(2)}) collective-permute-start(bf16[256,1664]{1,0:T(8,128)(2,1)S(1)} %bitcast.280), channel_id=1, source_target_pairs={{0,2},{2,4},{4,6},{6,0},{1,3},{3,5},{5,7},{7,1},{8,10},{10,12},{12... | collective-permute-start | bytes 2555912 | tf_op jit(solution)/shard_map/ppermute | solution.py:53
  69.4 69.8 %collective-permute-start.1 = (bf16[256,1664]{1,0:T(8,128)(2,1)S(1)}, bf16[256,1664]{1,0:T(8,128)(2,1)}, u32[]{:S(2)}, u32[]{:S(2)}) collective-permute-start(bf16[256,1664]{1,0:T(8,128)(2,1)S(1)} %bitcast.281), channel_id=1, source_target_pairs={{0,4},{2,6},{4,0},{6,2},{1,5},{3,7},{5,1},{7,3},{8,12},{10,14},{12... | collective-permute-start | bytes 2555912 | tf_op jit(solution)/shard_map/ppermute | solution.py:53
  70.7 70.5 %collective-permute-start.2 = (bf16[256,1664]{1,0:T(8,128)(2,1)S(1)}, bf16[256,1664]{1,0:T(8,128)(2,1)}, u32[]{:S(2)}, u32[]{:S(2)}) collective-permute-start(bf16[256,1664]{1,0:T(8,128)(2,1)S(1)} %bitcast.282), channel_id=1, source_target_pairs={{0,6},{2,0},{4,2},{6,4},{1,7},{3,1},{5,3},{7,5},{8,14},{10,8},{12,... | collective-permute-start | bytes 2555912 | tf_op jit(solution)/shard_map/ppermute | solution.py:53
  72.9 77.2 %collective-permute-start.3 = (bf16[256,1664]{1,0:T(8,128)(2,1)S(1)}, bf16[256,1664]{1,0:T(8,128)(2,1)}, u32[]{:S(2)}, u32[]{:S(2)}) collective-permute-start(bf16[256,1664]{1,0:T(8,128)(2,1)S(1)} %bitcast.283), channel_id=1, source_target_pairs={{0,1},{1,0},{2,3},{3,2},{4,5},{5,4},{6,7},{7,6},{8,9},{9,8},{10,11... | collective-permute-start | bytes 2555912 | tf_op jit(solution)/shard_map/ppermute | solution.py:144
  150.1 35.6 %collective-permute-start.7 = (bf16[256,2048]{1,0:T(8,128)(2,1)}, bf16[256,2048]{1,0:T(8,128)(2,1)}, u32[]{:S(2)}, u32[]{:S(2)}) collective-permute-start(bf16[256,2048]{1,0:T(8,128)(2,1)} %broadcast_add_fusion.refs_0_), channel_id=1, source_target_pairs={{0,2},{2,4},{4,6},{6,0},{1,3},{3,5},{5,7},{7,1},{8,10},{10,12},{12... | collective-permute-start | bytes 3145736 | tf_op jit(solution)/shard_map/ppermute | solution.py:53
  150.1 48.9 %collective-permute-start.9 = (bf16[256,2048]{1,0:T(8,128)(2,1)}, bf16[256,2048]{1,0:T(8,128)(2,1)}, u32[]{:S(2)}, u32[]{:S(2)}) collective-permute-start(bf16[256,2048]{1,0:T(8,128)(2,1)} %broadcast_add_fusion.refs_0_), channel_id=1, source_target_pairs={{0,6},{2,0},{4,2},{6,4},{1,7},{3,1},{5,3},{7,5},{8,14},{10,8},{12,... | collective-permute-start | bytes 3145736 | tf_op jit(solution)/shard_map/ppermute | solution.py:53
  152.1 89.1 %collective-permute-start.8 = (bf16[256,2048]{1,0:T(8,128)(2,1)}, bf16[256,2048]{1,0:T(8,128)(2,1)}, u32[]{:S(2)}, u32[]{:S(2)}) collective-permute-start(bf16[256,2048]{1,0:T(8,128)(2,1)} %broadcast_add_fusion.refs_0_), channel_id=1, source_target_pairs={{0,4},{2,6},{4,0},{6,2},{1,5},{3,7},{5,1},{7,3},{8,12},{10,14},{12... | collective-permute-start | bytes 3145736 | tf_op jit(solution)/shard_map/ppermute | solution.py:53
  179.8 63.9 %all-to-all-start.3 = ((f32[4,2,1024]{2,1,0:T(2,128)}), f32[4,2,1024]{2,1,0:T(2,128)S(1)}, u32[]{:S(2)}, u32[]{:S(2)}) async-start(f32[4,2,1024]{2,1,0:T(2,128)} %broadcast_in_dim.107), calls=%async_computation.3 | async-start | bytes 65536 | tf_op jit(solution)/shard_map/all_to_all | solution.py:47
  185.1 86.9 %collective-permute-start.10 = (bf16[256,2048]{1,0:T(8,128)(2,1)}, bf16[256,2048]{1,0:T(8,128)(2,1)}, u32[]{:S(2)}, u32[]{:S(2)}) collective-permute-start(bf16[256,2048]{1,0:T(8,128)(2,1)} %broadcast_add_fusion.refs_0_), channel_id=1, source_target_pairs={{0,1},{1,0},{2,3},{3,2},{4,5},{5,4},{6,7},{7,6},{8,9},{9,8},{10,11... | collective-permute-start | bytes 3145736 | tf_op jit(solution)/shard_map/ppermute | solution.py:144
  266.6 711.1 %reduce-scatter.5.cloned.1.call-start = ((), (), s32[]{:S(2)}) async-start(), calls=%async_computation.16 | async-start | bytes 18874368 | tf_op jit(solution)/shard_map/reduce_scatter | solution.py:828
  304.7 68.0 %collective-permute-start.15 = (bf16[256,2048]{1,0:T(8,128)(2,1)S(1)}, bf16[256,2048]{1,0:T(8,128)(2,1)S(1)}, u32[]{:S(2)}, u32[]{:S(2)}) collective-permute-start(bf16[256,2048]{1,0:T(8,128)(2,1)S(1)} %multiply_convert_fusion.refs_0_), channel_id=1, source_target_pairs={{0,4},{2,6},{4,0},{6,2},{1,5},{3,7},{5,1},{7,3},{8,12},{10,14},{12... | collective-permute-start | bytes 3145736 | tf_op jit(solution)/shard_map/ppermute | solution.py:53
  304.7 89.6 %collective-permute-start.14 = (bf16[256,2048]{1,0:T(8,128)(2,1)S(1)}, bf16[256,2048]{1,0:T(8,128)(2,1)}, u32[]{:S(2)}, u32[]{:S(2)}) collective-permute-start(bf16[256,2048]{1,0:T(8,128)(2,1)S(1)} %multiply_convert_fusion.refs_0_), channel_id=1, source_target_pairs={{0,2},{2,4},{4,6},{6,0},{1,3},{3,5},{5,7},{7,1},{8,10},{10,12},{12... | collective-permute-start | bytes 3145736 | tf_op jit(solution)/shard_map/ppermute | solution.py:53
  397.3 79.9 %collective-permute-start.17 = (bf16[256,2048]{1,0:T(8,128)(2,1)}, bf16[256,2048]{1,0:T(8,128)(2,1)}, u32[]{:S(2)}, u32[]{:S(2)}) collective-permute-start(bf16[256,2048]{1,0:T(8,128)(2,1)} %add_bitcast_fusion.refs_0_), channel_id=1, source_target_pairs={{0,2},{2,4},{4,6},{6,0},{1,3},{3,5},{5,7},{7,1},{8,10},{10,12},{12... | collective-permute-start | bytes 3145736 | tf_op jit(solution)/shard_map/ppermute | solution.py:53
  399.9 89.5 %collective-permute-start.18 = (bf16[256,2048]{1,0:T(8,128)(2,1)}, bf16[256,2048]{1,0:T(8,128)(2,1)}, u32[]{:S(2)}, u32[]{:S(2)}) collective-permute-start(bf16[256,2048]{1,0:T(8,128)(2,1)} %add_bitcast_fusion.refs_0_), channel_id=1, source_target_pairs={{0,4},{2,6},{4,0},{6,2},{1,5},{3,7},{5,1},{7,3},{8,12},{10,14},{12... | collective-permute-start | bytes 3145736 | tf_op jit(solution)/shard_map/ppermute | solution.py:53
  401.3 89.3 %collective-permute-start.19 = (bf16[256,2048]{1,0:T(8,128)(2,1)}, bf16[256,2048]{1,0:T(8,128)(2,1)}, u32[]{:S(2)}, u32[]{:S(2)}) collective-permute-start(bf16[256,2048]{1,0:T(8,128)(2,1)} %add_bitcast_fusion.refs_0_), channel_id=1, source_target_pairs={{0,6},{2,0},{4,2},{6,4},{1,7},{3,1},{5,3},{7,5},{8,14},{10,8},{12,... | collective-permute-start | bytes 3145736 | tf_op jit(solution)/shard_map/ppermute | solution.py:53
  511.8 191.9 %all-to-all-start.5 = ((bf16[4,256,2048]{2,1,0:T(8,128)(2,1)}), bf16[4,256,2048]{2,1,0:T(8,128)(2,1)}, u32[]{:S(2)}, u32[]{:S(2)}) async-start(bf16[4,256,2048]{2,1,0:T(8,128)(2,1)} %get-tuple-element.50), calls=%async_computation.5 | async-start | bytes 8388608 | tf_op jit(solution)/shard_map/all_to_all | solution.py:47
  516.8 465.4 %reduce-scatter.3.cloned.1.call-start = ((), (), s32[]{:S(2)}) async-start(), calls=%async_computation.15 | async-start | bytes 37748736 | tf_op jit(solution)/shard_map/reduce_scatter | solution.py:840
  594.4 85.7 %collective-permute-start.20 = (bf16[256,2176]{1,0:T(8,128)(2,1)}, bf16[256,2176]{1,0:T(8,128)(2,1)}, u32[]{:S(2)}, u32[]{:S(2)}) collective-permute-start(bf16[256,2176]{1,0:T(8,128)(2,1)} %get-tuple-element.63), channel_id=1, source_target_pairs={{0,6},{2,0},{4,2},{6,4},{1,7},{3,1},{5,3},{7,5},{8,14},{10,8},{12,... | collective-permute-start | bytes 3342344 | tf_op jit(solution)/shard_map/ppermute | solution.py:60
  594.5 86.5 %collective-permute-start.21 = (bf16[256,2176]{1,0:T(8,128)(2,1)}, bf16[256,2176]{1,0:T(8,128)(2,1)}, u32[]{:S(2)}, u32[]{:S(2)}) collective-permute-start(bf16[256,2176]{1,0:T(8,128)(2,1)} %get-tuple-element.64), channel_id=1, source_target_pairs={{0,4},{2,6},{4,0},{6,2},{1,5},{3,7},{5,1},{7,3},{8,12},{10,14},{12... | collective-permute-start | bytes 3342344 | tf_op jit(solution)/shard_map/ppermute | solution.py:60
  598.2 104.4 %collective-permute-start.22 = (bf16[256,2176]{1,0:T(8,128)(2,1)}, bf16[256,2176]{1,0:T(8,128)(2,1)}, u32[]{:S(2)}, u32[]{:S(2)}) collective-permute-start(bf16[256,2176]{1,0:T(8,128)(2,1)} %get-tuple-element.65), channel_id=1, source_target_pairs={{0,2},{2,4},{4,6},{6,0},{1,3},{3,5},{5,7},{7,1},{8,10},{10,12},{12... | collective-permute-start | bytes 3342344 | tf_op jit(solution)/shard_map/ppermute | solution.py:60
  733.5 30.4 %all-to-all-start.6 = ((bf16[256,4,512]{2,0,1:T(8,128)(2,1)}), bf16[256,4,512]{2,0,1:T(8,128)(2,1)}, u32[]{:S(2)}, u32[]{:S(2)}) async-start(bf16[256,4,512]{2,0,1:T(8,128)(2,1)} %bitcast.265), calls=%async_computation.6 | async-start | bytes 2097152 | tf_op jit(solution)/shard_map/all_to_all | solution.py:868
  746.0 79.4 %collective-permute-start.26 = (bf16[256,2048]{1,0:T(8,128)(2,1)}, bf16[256,2048]{1,0:T(8,128)(2,1)}, u32[]{:S(2)}, u32[]{:S(2)}) collective-permute-start(bf16[256,2048]{1,0:T(8,128)(2,1)} %get-tuple-element.140), channel_id=1, source_target_pairs={{0,2},{2,4},{4,6},{6,0},{1,3},{3,5},{5,7},{7,1},{8,10},{10,12},{12... | collective-permute-start | bytes 3145736 | tf_op jit(solution)/shard_map/ppermute | solution.py:60
  749.0 90.6 %collective-permute-start.25 = (bf16[256,2048]{1,0:T(8,128)(2,1)}, bf16[256,2048]{1,0:T(8,128)(2,1)}, u32[]{:S(2)}, u32[]{:S(2)}) collective-permute-start(bf16[256,2048]{1,0:T(8,128)(2,1)} %get-tuple-element.141), channel_id=1, source_target_pairs={{0,4},{2,6},{4,0},{6,2},{1,5},{3,7},{5,1},{7,3},{8,12},{10,14},{12... | collective-permute-start | bytes 3145736 | tf_op jit(solution)/shard_map/ppermute | solution.py:60
  751.2 90.3 %collective-permute-start.24 = (bf16[256,2048]{1,0:T(8,128)(2,1)}, bf16[256,2048]{1,0:T(8,128)(2,1)}, u32[]{:S(2)}, u32[]{:S(2)}) collective-permute-start(bf16[256,2048]{1,0:T(8,128)(2,1)} %get-tuple-element.139), channel_id=1, source_target_pairs={{0,6},{2,0},{4,2},{6,4},{1,7},{3,1},{5,3},{7,5},{8,14},{10,8},{12,... | collective-permute-start | bytes 3145736 | tf_op jit(solution)/shard_map/ppermute | solution.py:60
  861.3 73.9 %collective-permute-start.29 = (bf16[256,1664]{1,0:T(8,128)(2,1)}, bf16[256,1664]{1,0:T(8,128)(2,1)}, u32[]{:S(2)}, u32[]{:S(2)}) collective-permute-start(bf16[256,1664]{1,0:T(8,128)(2,1)} %get-tuple-element.146), channel_id=1, source_target_pairs={{0,4},{2,6},{4,0},{6,2},{1,5},{3,7},{5,1},{7,3},{8,12},{10,14},{12... | collective-permute-start | bytes 2555912 | tf_op jit(solution)/shard_map/ppermute | solution.py:60
  864.8 74.4 %collective-permute-start.28 = (bf16[256,1664]{1,0:T(8,128)(2,1)}, bf16[256,1664]{1,0:T(8,128)(2,1)}, u32[]{:S(2)}, u32[]{:S(2)}) collective-permute-start(bf16[256,1664]{1,0:T(8,128)(2,1)} %get-tuple-element.144), channel_id=1, source_target_pairs={{0,6},{2,0},{4,2},{6,4},{1,7},{3,1},{5,3},{7,5},{8,14},{10,8},{12,... | collective-permute-start | bytes 2555912 | tf_op jit(solution)/shard_map/ppermute | solution.py:60
  875.1 93.1 %all-to-all-start.8 = ((bf16[4,256,2048]{2,1,0:T(8,128)(2,1)}), bf16[4,256,2048]{2,1,0:T(8,128)(2,1)}, u32[]{:S(2)}, u32[]{:S(2)}) async-start(bf16[4,256,2048]{2,1,0:T(8,128)(2,1)} %bitcast.279), calls=%async_computation.8 | async-start | bytes 8388608 | tf_op jit(solution)/shard_map/all_to_all | solution.py:47
  (66 other events, 1407.1 us)
Sparse Core Ops, SparseCore 0:
  48.4 91.9 all-gather.10
  142.3 90.1 all-gather.8
  234.4 65.6 all-gather.6
  301.8 89.8 all-gather.4
  511.9 115.7 reduce-scatter.4
  640.5 215.4 reduce-scatter.2

commit v4 on v3

--- a/solution.py
+++ b/solution.py
@@ -11,6 +11,7 @@
 HEAD_DIM = 128
 FF = 1024
 TOP = 8
+EARLY = (1,)
 ATT_BLOCK = 256
 
 
@@ -396,10 +397,55 @@
     return most if width % most == 0 else width
 
 
-def forward_kernel(count, kept, place_ref, pick_ref, gate_ref, in_ref, down_ref, *refs):
+def route_kernel(experts_total, count, first_ref, router_ref, pick_ref, *refs):
+    near_refs, (gate_ref, probs_ref) = refs[:count], refs[count:]
+    experts, _, capacity, tokens = pick_ref.shape
+    lane = lax.broadcasted_iota(jnp.int32, (tokens, router_ref.shape[0]), 1)
+    for k in range(count):
+        logits = dot(near_refs[k][...], router_ref[...], 1, 1)
+        logits = jnp.where(lane < experts_total, logits, -jnp.inf)
+        terms = jnp.exp(logits - jnp.max(logits, axis=1, keepdims=True))
+        probs = terms / jnp.sum(terms, axis=1, keepdims=True)
+        if k == 0:
+            probs_ref[...] = probs
+        pairs = jnp.zeros((tokens, router_ref.shape[0]), f32)
+        for j in range(experts):
+            prob = jnp.sum(jnp.where(lane == first_ref[0] + j, probs, 0.0), axis=1, keepdims=True)
+            high = prob.astype(bf16).astype(f32)
+            pairs = jnp.where(lane == 2 * j, high, pairs)
+            pairs = jnp.where(lane == 2 * j + 1, prob - high, pairs)
+        pairs = pairs.astype(bf16)
+        for j in range(experts):
+            gates = dot(pick_ref[j, k], pairs, 1, 0)
+            gate_ref[j, k * capacity : (k + 1) * capacity] = (
+                gates[:, 2 * j : 2 * j + 1] + gates[:, 2 * j + 1 : 2 * j + 2]
+            )
+
+
+def route(first, router_rows, pick, near):
+    experts, count, capacity, tokens = pick.shape
+    experts_total = router_rows.shape[0]
+    lanes = 128 * -(-max(experts_total, 2 * experts) // 128)
+    router_rows = jnp.pad(router_rows, ((0, lanes - experts_total), (0, 0)))
+    vmem = pl.BlockSpec(memory_space=pltpu.VMEM)
+    gates, probs = pl.pallas_call(
+        functools.partial(route_kernel, experts_total, count),
+        in_specs=[pl.BlockSpec(memory_space=pltpu.SMEM)] + [vmem] * (2 + count),
+        out_shape=[
+            jax.ShapeDtypeStruct((experts, count * capacity, 1), f32),
+            jax.ShapeDtypeStruct((tokens, lanes), f32),
+        ],
+        compiler_params=KERNEL_PARAMS,
+        cost_estimate=SMALL_COST,
+        name="route",
+    )(jnp.reshape(first.astype(jnp.int32), (1,)), router_rows, pick, *near)
+    return probs[:, :experts_total], gates
+
+
+def forward_kernel(count, kept, place_ref, pick_ref, turned_ref, gate_ref, in_ref, down_ref, *refs):
     near_refs, refs = refs[:count], refs[count:]
     earlier_refs, refs = refs[4:kept], refs[kept:]
-    rows_ref, gate_out_ref, up_out_ref, gated_ref, mix_ref, result_ref, sums_ref = refs
+    rows_ref, gate_out_ref, up_out_ref, gated_ref, mix_ref, result_ref = refs
     step_number, steps = pl.program_id(0), pl.num_programs(0)
     capacity, width = pick_ref.shape[2], rows_ref.shape[2]
     hidden = gated_ref.shape[2]
@@ -408,44 +454,33 @@
             pick_ref[0, k], near_refs[k][...], 1, 0
         ).astype(bf16)
     step = chunk_of(hidden, 512)
-
-    @pl.loop(0, hidden // step)
-    def _(j):
-        low = pl.ds(pl.multiple_of(j * step, step), step)
-        high = pl.ds(pl.multiple_of(hidden + j * step, step), step)
+    for start in range(0, hidden, step):
+        low, high = slice(start, start + step), slice(hidden + start, hidden + start + step)
         gate = dot(rows_ref[0], in_ref[0, :, low], 1, 0)
         up = dot(rows_ref[0], in_ref[0, :, high], 1, 0)
         gate_out_ref[0, :, low] = gate.astype(bf16)
         up_out_ref[0, :, low] = up.astype(bf16)
         gated_ref[0, :, low] = (gate * jax.nn.sigmoid(gate) * up * gate_ref[0]).astype(bf16)
-
     wide = chunk_of(width, 1024)
-
-    @pl.loop(0, width // wide)
-    def _(j):
-        cols = pl.ds(pl.multiple_of(j * wide, wide), wide)
-        result_ref[...] = dot(gated_ref[0], down_ref[0, cols, :], 1, 1).astype(bf16)
-        for k in range(count):
-            part = dot(pick_ref[0, k], result_ref[k * capacity : (k + 1) * capacity], 0, 0)
-
-            @pl.when(step_number == 0)
-            def _():
-                sums_ref[k, :, cols] = part
-
-            @pl.when(step_number > 0)
-            def _():
-                sums_ref[k, :, cols] += part
+    for start in range(0, width, wide):
+        cols = slice(start, start + wide)
+        result_ref[step_number, :, cols] = dot(gated_ref[0], down_ref[0, cols, :], 1, 1).astype(bf16)
 
     @pl.when(step_number == steps - 1)
     def _():
         for k in range(count):
-            mix = sums_ref[k]
-            if earlier_refs:
-                mix = mix + earlier_refs[0][place_ref[k]].astype(f32)
-            mix_ref[place_ref[k]] = mix.astype(bf16)
-
-
-def experts_forward(first, kept, places, pick, gates, in_weight, down_weight, near):
+            rows = slice(k * capacity, (k + 1) * capacity)
+            for start in range(0, width, wide):
+                cols = slice(start, start + wide)
+                mix = dot(turned_ref[0, k], result_ref[0, rows, cols], 1, 0)
+                for expert in range(1, result_ref.shape[0]):
+                    mix += dot(turned_ref[expert, k], result_ref[expert, rows, cols], 1, 0)
+                if earlier_refs:
+                    mix += earlier_refs[0][place_ref[k], :, cols].astype(f32)
+                mix_ref[place_ref[k], :, cols] = mix.astype(bf16)
+
+
+def experts_forward(first, kept, places, pick, turned, gates, in_weight, down_weight, near):
     experts, count, capacity, tokens = pick.shape
     here, width, hidden = in_weight.shape[0], in_weight.shape[1], down_weight.shape[2]
     rows = count * capacity
@@ -458,22 +493,23 @@
         grid=(here,),
         in_specs=[
             pl.BlockSpec(memory_space=pltpu.SMEM),
-            each((count, capacity, tokens)), each((rows, 1)),
+            each((count, capacity, tokens)),
+            pl.BlockSpec(
+                (here,) + turned.shape[1:], lambda e: (first // here, 0, 0, 0), pipeline_mode=pl.Buffered(1)
+            ),
+            each((rows, 1)),
             near_each((width, 2 * hidden)), near_each((width, hidden)),
         ] + [whole] * count + [pl.BlockSpec(memory_space=pl.ANY)] * len(kept[:4]) + [sums] * len(kept[4:]),
         out_specs=[each((rows, width))] + [each((rows, hidden))] * 3 + [sums],
         out_shape=[jax.ShapeDtypeStruct((experts, rows, width), bf16)]
         + [jax.ShapeDtypeStruct((experts, rows, hidden), bf16)] * 3
         + [jax.ShapeDtypeStruct((count, tokens, width), bf16)],
-        scratch_shapes=[
-            pltpu.VMEM((rows, chunk_of(width, 1024)), bf16),
-            pltpu.VMEM((count, tokens, width), f32),
-        ],
-        input_output_aliases={5 + count + i: i for i in range(len(kept[:4]))},
+        scratch_shapes=[pltpu.VMEM((here, rows, width), bf16)],
+        input_output_aliases={6 + count + i: i for i in range(len(kept[:4]))},
         compiler_params=KERNEL_PARAMS,
         cost_estimate=SMALL_COST,
         name="experts_forward",
-    )(places, pick, gates, in_weight, down_weight, *near, *kept)
+    )(places, pick, turned, gates, in_weight, down_weight, *near, *kept)
 
 
 def down_grad_kernel(count, pick_ref, gated_ref, *refs):
@@ -514,74 +550,56 @@
 
 
 def backward_kernel(
-    first, count, kept, pick_ref, gate_rows_ref, cot_ref, gate_ref, up_ref, in_ref, down_ref, *refs
+    first, count, kept, turned_ref, gate_rows_ref, cot_ref, gate_ref, up_ref, in_ref, down_ref, *refs
 ):
     earlier_refs, refs = refs[1:kept], refs[kept:]
     both_ref = refs[0]
     copy_refs = refs[1 : 1 + count]
-    result_ref, inner_ref, sums_ref, inner_sums_ref = refs[1 + count :]
+    result_ref, inner_ref = refs[1 + count :]
     step_number, steps = pl.program_id(0), pl.num_programs(0)
-    capacity, width = pick_ref.shape[2], cot_ref.shape[2]
+    capacity, width = turned_ref.shape[3], cot_ref.shape[2]
     hidden = gate_ref.shape[2]
-    lanes = inner_sums_ref.shape[2]
+    lanes = inner_ref.shape[2]
     step = chunk_of(hidden, 512)
-    inner_ref[...] = jnp.zeros_like(inner_ref)
-
-    @pl.when(step_number == 0)
-    def _():
-        inner_sums_ref[...] = jnp.zeros_like(inner_sums_ref)
-
-    @pl.loop(0, hidden // step)
-    def _(j):
-        low = pl.ds(pl.multiple_of(j * step, step), step)
-        high = pl.ds(pl.multiple_of(hidden + j * step, step), step)
+    inner = jnp.zeros((count * capacity, 1), f32)
+    for start in range(0, hidden, step):
+        low, high = slice(start, start + step), slice(hidden + start, hidden + start + step)
         result_grad = dot(cot_ref[0], down_ref[0, :, low], 1, 0)
         gate, up = gate_ref[0, :, low].astype(f32), up_ref[0, :, low].astype(f32)
         sigmoid = jax.nn.sigmoid(gate)
         silu = gate * sigmoid
-        inner_ref[...] += jnp.sum(result_grad * silu * up, axis=1, keepdims=True)
+        inner += jnp.sum(result_grad * silu * up, axis=1, keepdims=True)
         act_grad = result_grad * gate_rows_ref[0]
         both_ref[0, :, low] = (act_grad * up * (sigmoid + silu * (1.0 - sigmoid))).astype(bf16)
         both_ref[0, :, high] = (act_grad * silu).astype(bf16)
-
-    inner_high = inner_ref[...].astype(bf16).astype(f32)
+    inner_high = inner.astype(bf16).astype(f32)
     lane = lax.broadcasted_iota(jnp.int32, (count * capacity, lanes), 1)
     place = 2 * (first + step_number)
     inner_wide = jnp.where(lane == place, inner_high, 0.0)
-    inner_wide = jnp.where(lane == place + 1, inner_ref[...] - inner_high, inner_wide)
-    inner_wide = inner_wide.astype(bf16)
-    for k in range(count):
-        inner_sums_ref[k] += dot(pick_ref[0, k], inner_wide[k * capacity : (k + 1) * capacity], 0, 0)
+    inner_wide = jnp.where(lane == place + 1, inner - inner_high, inner_wide)
+    inner_ref[step_number] = inner_wide.astype(bf16)
     wide = chunk_of(width, 1024)
-
-    @pl.loop(0, width // wide)
-    def _(j):
-        cols = pl.ds(pl.multiple_of(j * wide, wide), wide)
-        result_ref[...] = dot(both_ref[0], in_ref[0, cols, :], 1, 1).astype(bf16)
-        for k in range(count):
-            part = dot(pick_ref[0, k], result_ref[k * capacity : (k + 1) * capacity], 0, 0)
-
-            @pl.when(step_number == 0)
-            def _():
-                sums_ref[k, :, cols] = part
-
-            @pl.when(step_number > 0)
-            def _():
-                sums_ref[k, :, cols] += part
+    for start in range(0, width, wide):
+        cols = slice(start, start + wide)
+        result_ref[step_number, :, cols] = dot(both_ref[0], in_ref[0, cols, :], 1, 1).astype(bf16)
 
     @pl.when(step_number == steps - 1)
     def _():
         for k in range(count):
-            copies, inner = sums_ref[k], inner_sums_ref[k]
-            if earlier_refs:
-                copies = copies + earlier_refs[k][:, :width].astype(f32)
-                inner = inner + earlier_refs[k][:, width:].astype(f32)
-            copy_refs[k][:, :width] = copies.astype(bf16)
-            copy_refs[k][:, width:] = inner.astype(bf16)
-
-
-def experts_backward(first, kept, pick, gate_rows, cot_rows, gate, up, in_weight, down_weight):
-    experts, count, capacity, tokens = pick.shape
+            rows = slice(k * capacity, (k + 1) * capacity)
+            pieces = [(result_ref, slice(start, start + wide), start) for start in range(0, width, wide)]
+            for ref, cols, start in pieces + [(inner_ref, slice(0, lanes), width)]:
+                copies = dot(turned_ref[0, k], ref[0, rows, cols], 1, 0)
+                for expert in range(1, result_ref.shape[0]):
+                    copies += dot(turned_ref[expert, k], ref[expert, rows, cols], 1, 0)
+                target = slice(start, start + cols.stop - cols.start)
+                if earlier_refs:
+                    copies += earlier_refs[k][:, target].astype(f32)
+                copy_refs[k][:, target] = copies.astype(bf16)
+
+
+def experts_backward(first, kept, turned, gate_rows, cot_rows, gate, up, in_weight, down_weight):
+    experts, count, tokens, capacity = turned.shape
     here, width, hidden = in_weight.shape[0], in_weight.shape[1], down_weight.shape[2]
     rows = count * capacity
     lanes = 128 * -(-2 * experts // 128)
@@ -592,7 +610,10 @@
         functools.partial(backward_kernel, first, count, len(kept)),
         grid=(here,),
         in_specs=[
-            each((count, capacity, tokens)), each((rows, 1)), each((rows, width)),
+            pl.BlockSpec(
+                (here,) + turned.shape[1:], lambda e: (first // here, 0, 0, 0), pipeline_mode=pl.Buffered(1)
+            ),
+            each((rows, 1)), each((rows, width)),
             each((rows, hidden)), each((rows, hidden)),
             near_each((width, 2 * hidden)), near_each((width, hidden)),
         ] + [pl.BlockSpec(memory_space=pl.ANY)] * len(kept[:1]) + [whole] * len(kept[1:]),
@@ -600,16 +621,14 @@
         out_shape=[jax.ShapeDtypeStruct((experts, rows, 2 * hidden), bf16)]
         + [jax.ShapeDtypeStruct((tokens, width + lanes), bf16)] * count,
         scratch_shapes=[
-            pltpu.VMEM((rows, chunk_of(width, 1024)), bf16),
-            pltpu.VMEM((rows, 1), f32),
-            pltpu.VMEM((count, tokens, width), f32),
-            pltpu.VMEM((count, tokens, lanes), f32),
+            pltpu.VMEM((here, rows, width), bf16),
+            pltpu.VMEM((here, rows, lanes), bf16),
         ],
         input_output_aliases={7 + i: i for i in range(len(kept[:1]))},
         compiler_params=KERNEL_PARAMS,
         cost_estimate=SMALL_COST,
         name="experts_backward",
-    )(pick, gate_rows, cot_rows, gate, up, in_weight, down_weight, *kept)
+    )(turned, gate_rows, cot_rows, gate, up, in_weight, down_weight, *kept)
 
 
 def in_grad_kernel(rows_ref, both_ref, earlier_ref, grad_ref):
@@ -733,6 +752,11 @@
     ids_cols = ids_low.shape[2]
     after_ids = heads_seq.shape[2] - first_id - ids_cols
     heads_rows = heads_seq + jnp.pad(ids_low, ((0, 0), (0, 0), (first_id, after_ids)))
+    cot_early = {
+        k: lax.ppermute(cotangent[0], "exp", shift_pairs(exp_count, k))
+        for k in range(1, exp_count)
+        if k in EARLY
+    }
     heads_near = gather_near(heads_rows.reshape(seq_count * rows_dev, -1), "exp")
     ids_group = jnp.stack(
         [near[:, first_id : first_id + ids_cols].reshape(tok_count, TOP) for near in heads_near]
@@ -751,10 +775,13 @@
 
     out_near = gather_near(after(out_rows, heads_near[-1]), "exp")
 
-    parts = 2 if exp_dev % 2 == 0 else 1
+    parts = 1
     part_experts = exp_dev // parts
-    in_blocks = jnp.transpose(after(expert_in, out_rows), (1, 0, 2))
-    down_blocks = jnp.transpose(after(expert_out, out_rows), (1, 0, 2))
+    sent = out_rows
+    for near in cot_early.values():
+        sent = after(sent[:16, :128], near)
+    in_blocks = jnp.transpose(after(expert_in, sent), (1, 0, 2))
+    down_blocks = jnp.transpose(after(expert_out, sent), (1, 0, 2))
     in_weights, down_weights = [], []
     for part in range(parts):
         chosen_experts = slice(part * part_experts, (part + 1) * part_experts)
@@ -799,30 +826,28 @@
     rank = jnp.where(jnp.transpose(chosen, (2, 0, 1)), rank, -1.0)
     pick = rank[:, :, None, :] == jnp.arange(capacity, dtype=f32)[None, None, :, None]
     pick_low = pick.astype(bf16)
+    turned = rank[:, :, :, None] == jnp.arange(capacity, dtype=f32)[None, None, None, :]
+    turned_low = turned.astype(bf16)
 
     mlp_near = gather_near(mlp_low, "exp")
-    cot_near = cotangent[0]
+    late = cotangent[0]
     for near in mlp_near[1:]:
-        cot_near = after(cot_near, near)
-    cot_near = gather_near(cot_near, "exp")
-    logits = jnp.stack(
-        [jnp.einsum("td,ed->te", near, router_rows, preferred_element_type=f32) for near in mlp_near]
-    )
-    group_probs = jax.nn.softmax(logits, axis=-1)
-    router_probs = group_probs[0]
-    near_probs = lax.dynamic_slice_in_dim(group_probs, own_exp * exp_dev, exp_dev, 2)
-    near_probs = jnp.transpose(near_probs, (2, 0, 1))
-    gate_rows = jnp.sum(jnp.where(pick, near_probs[:, :, None, :], 0.0), axis=-1)
-    gate_rows = gate_rows.reshape(exp_dev, exp_count * capacity, 1)
+        late = after(late, near)
+    cot_near = [cotangent[0]] + [
+        cot_early[k] if k in cot_early else lax.ppermute(late, "exp", shift_pairs(exp_count, k))
+        for k in range(1, exp_count)
+    ]
+    router_probs, gate_rows = route(own_exp * exp_dev, router_rows, pick_low, mlp_near)
     places = jnp.stack([ring_place(own_exp - k, exp_count) for k in range(exp_count)])
     kept = []
     for part in range(parts):
         kept = experts_forward(
-            part * part_experts, kept, places.astype(jnp.int32), pick_low, gate_rows,
+            part * part_experts, kept, places.astype(jnp.int32), pick_low, turned_low, gate_rows,
             in_weights[part], down_weights[part], mlp_near,
         )
     expert_rows, gate, up, gated, mix = kept
-    output = (residual + jnp.sum(exchange(mix, "exp").astype(f32), axis=0)).astype(bf16)
+    mix_near = exchange(mix, "exp")
+    output = (residual + jnp.sum(mix_near.astype(f32), axis=0)).astype(bf16)
 
     cot_rows, down_grad = experts_down_grad(pick_low, gated, cot_near)
     grad_expert_out = lax.psum_scatter(
@@ -831,14 +856,14 @@
     kept = []
     for part in range(parts):
         kept = experts_backward(
-            part * part_experts, kept, pick_low, gate_rows, cot_rows, gate, up,
+            part * part_experts, kept, turned_low, gate_rows, cot_rows, gate, up,
             in_weights[part], down_weights[part],
         )
     copy_near = send_near(kept[1:], "exp")
     before = jnp.stack([block[:16, :128] for block in kept[1:]])
     in_grad = experts_in_grad(expert_rows, kept[0], before)
     grad_expert_in = lax.psum_scatter(in_grad, ("seq", "fsdp"), scatter_dimension=1, tiled=True)
-    copy_near[0] = after(after(copy_near[0], in_grad), output)
+    copy_near[0] = after(after(copy_near[0], in_grad), mix_near)
     mlp_grad_experts = add_up([near[:, :model_width] for near in copy_near])
     prob_pairs = [
         near[:, model_width : model_width + 2 * exp_dev].astype(f32).reshape(tok_count, exp_dev, 2)

time: 1010 us -> 998 us (0.988)
  Pallas kernels: 301 us -> 267 us
  blocking collectives: 30.6 us -> 0 us
  waiting for transfers between devices: 398 us -> 425 us
  starting transfers between devices: 73.7 us -> 90.7 us
  other arithmetic: 66.4 us -> 76.8 us
    all_to_all x2 -> x0, blocking collectives: 30.6 us -> none  [exchange(): lax.all_to_all(stacked, axis, split_axis=split_axis, concat_axis=split_ax...]
    pallas_call x2 -> x1, Pallas kernels: 77.6 us -> 54.7 us  [experts_backward(): pl.pallas_call(functools.partial(backward_kernel, first, count, len(kept)...]
    pallas_call x2 -> x1, Pallas kernels: 70.1 us -> 48.6 us  [experts_forward(): pl.pallas_call(functools.partial(forward_kernel, count, len(kept)), grid=...]
    ppermute x12, waiting for transfers between devices: 152 us -> 169 us  [send_near(): lax.ppermute(blocks[k], axis, shift_pairs(count, -k))]
    ppermute x12 -> x9, waiting for transfers between devices: 215 us -> 199 us  [gather_near(): lax.ppermute(block, axis, shift_pairs(count, k))]
    all_to_all x5 -> x7, waiting for transfers between devices: 1.98 us -> 15.6 us  [exchange(): lax.all_to_all(stacked, axis, split_axis=split_axis, concat_axis=split_ax...]
    all_to_all x5 -> x7, starting transfers between devices: 24.2 us -> 35.4 us  [exchange(): lax.all_to_all(stacked, axis, split_axis=split_axis, concat_axis=split_ax...]
  transfers between devices with their start and end apart: 47 -> 47, of which waited for: 22 -> 23; matrix products, arithmetic and copies ran while one was open for 15% -> 16% of each run, Pallas kernels for 27% -> 24%
where the time goes in v4:
time: 998 us; the launch traced here: 985 us
  waiting for transfers between devices  425 us (43%)
  Pallas kernels  267 us (27%)
  starting transfers between devices  90.7 us (9%)
  other arithmetic  76.8 us (8%)
  local copies, waits for them, and re-layouts  65.9 us (7%)
  matrix products  33.1 us (3%)
  between operations  26.8 us (3%)
    ppermute x9, waiting for transfers between devices, gather_near(): lax.ppermute(block, axis, shift_pairs(count, k))  199 us
    ppermute x12, waiting for transfers between devices, send_near(): lax.ppermute(blocks[k], axis, shift_pairs(count, -k))  169 us
    pallas_call x1, Pallas kernels, experts_backward(): pl.pallas_call(functools.partial(backward_kernel, first, count, len(kept)...  54.7 us
    pallas_call x1, Pallas kernels, experts_forward(): pl.pallas_call(functools.partial(forward_kernel, count, len(kept)), grid=...  48.6 us
    all_to_all x7, starting transfers between devices, exchange(): lax.all_to_all(stacked, axis, split_axis=split_axis, concat_axis=split_ax...  35.4 us
    pallas_call x1, Pallas kernels, experts_in_grad(): pl.pallas_call(in_grad_kernel, grid=(experts,), in_specs=[each(rows.shape...  35.4 us
    pallas_call x2, Pallas kernels, spread_product(): pl.pallas_call(functools.partial(spread_kernel, split, len(shapes)), in_s...  28.5 us
    ppermute x12, starting transfers between devices, send_near(): lax.ppermute(blocks[k], axis, shift_pairs(count, -k))  23 us
  transfers between devices with their start and end apart: 47, of which 23 were waited for; matrix products, arithmetic and copies ran while one was open for 16% of the time, Pallas kernels for 24%

profile of v4, /device:TPU:10, one launch (start us, length us, event | category | flops | bytes accessed | tf_op | source)
XLA Modules:
  0.0 984.6 jit_solution(6572007153252117560)
XLA Ops:
  18.7 9.4 all-to-all-done
  34.5 7.0 collective-permute-done.17.refs_1_
  52.4 9.0 fusion.6
  78.0 51.7 %collective-permute-done.2.refs_3_ = bf16[256,1664]{1,0:T(8,128)(2,1)} collective-permute-done((bf16[256,1664]{1,0:T(8,128)(2,1)S(1)}, bf16[256,1664]{1,0:T(8,128)(2,1)}, u32[]{:S(2)}, u32[]{:S(2)}) %collective-permute-start.2) | collective-permute-done | bytes 852000 | tf_op jit(solution)/shard_map/ppermute | solution.py:54
  130.3 15.4 %collective-permute-done.refs_1_ = bf16[256,1664]{1,0:T(8,128)(2,1)S(1)} collective-permute-done((bf16[256,1664]{1,0:T(8,128)(2,1)S(1)}, bf16[256,1664]{1,0:T(8,128)(2,1)S(1)}, u32[]{:S(2)}, u32[]{:S(2)}) %collective-permute-start) | collective-permute-done | bytes 852000 | tf_op jit(solution)/shard_map/ppermute | solution.py:54
  191.7 29.6 %collective-permute-done.8.refs_2_ = bf16[256,2048]{1,0:T(8,128)(2,1)} collective-permute-done((bf16[256,2048]{1,0:T(8,128)(2,1)}, bf16[256,2048]{1,0:T(8,128)(2,1)}, u32[]{:S(2)}, u32[]{:S(2)}) %collective-permute-start.8) | collective-permute-done | bytes 1048608 | tf_op jit(solution)/shard_map/ppermute | solution.py:54
  223.2 20.6 %collective-permute-done.7.refs_1_ = bf16[256,2048]{1,0:T(8,128)(2,1)} collective-permute-done((bf16[256,2048]{1,0:T(8,128)(2,1)}, bf16[256,2048]{1,0:T(8,128)(2,1)}, u32[]{:S(2)}, u32[]{:S(2)}) %collective-permute-start.7) | collective-permute-done | bytes 1048608 | tf_op jit(solution)/shard_map/ppermute | solution.py:54
  248.2 17.7 %attend.1 = (bf16[1024,512]{1,0:T(8,128)(2,1)}, bf16[1024,512]{1,0:T(8,128)(2,1)}, bf16[1024,512]{1,0:T(8,128)(2,1)}, bf16[1024,512]{1,0:T(8,128)(2,1)}) custom-call(f32[1024,1536]{1,0:T(8,128)} %copy-done, f32[1024,1536]{1,0:T(8,128)} %copy-done, f32[1024,1536]{1,0:T(8,128)} %copy-done, f32[1024,2]{1,0:T(8,128)} %add_add_fusion.4.scale_ref, ...), custom_call_target="tpu_custom_call" | custom-call | flops 1 | bytes 1 | tf_op jit(solution)/shard_map/attend/pallas_call | solution.py:240
  270.5 7.5 assemble.3
  278.0 18.0 %all-to-all-done.4 = bf16[4,256,512]{2,1,0:T(8,128)(2,1)} async-done(((bf16[4,256,512]{2,1,0:T(8,128)(2,1)}), bf16[4,256,512]{2,1,0:T(8,128)(2,1)}, u32[]{:S(2)}, u32[]{:S(2)}) %all-to-all-start.4) | async-done | bytes 1048608 | tf_op jit(solution)/shard_map/all_to_all | solution.py:811
  314.2 19.7 %collective-permute-done.16.refs_3_ = bf16[256,2048]{1,0:T(8,128)(2,1)S(1)} collective-permute-done((bf16[256,2048]{1,0:T(8,128)(2,1)S(1)}, bf16[256,2048]{1,0:T(8,128)(2,1)S(1)}, u32[]{:S(2)}, u32[]{:S(2)}) %collective-permute-start.16) | collective-permute-done | bytes 1048608 | tf_op jit(solution)/shard_map/ppermute | solution.py:54
  335.1 41.1 %collective-permute-done.15.refs_2_ = bf16[256,2048]{1,0:T(8,128)(2,1)S(1)} collective-permute-done((bf16[256,2048]{1,0:T(8,128)(2,1)S(1)}, bf16[256,2048]{1,0:T(8,128)(2,1)S(1)}, u32[]{:S(2)}, u32[]{:S(2)}) %collective-permute-start.15) | collective-permute-done | bytes 1048608 | tf_op jit(solution)/shard_map/ppermute | solution.py:54
  377.5 21.2 %collective-permute-done.14.refs_1_ = bf16[256,2048]{1,0:T(8,128)(2,1)} collective-permute-done((bf16[256,2048]{1,0:T(8,128)(2,1)S(1)}, bf16[256,2048]{1,0:T(8,128)(2,1)}, u32[]{:S(2)}, u32[]{:S(2)}) %collective-permute-start.14) | collective-permute-done | bytes 1048608 | tf_op jit(solution)/shard_map/ppermute | solution.py:54
  412.7 8.0 route.1
  420.7 48.6 %experts_forward.1 = (bf16[4,576,2048]{2,1,0:T(8,128)(2,1)}, bf16[4,576,1024]{2,1,0:T(8,128)(2,1)}, bf16[4,576,1024]{2,1,0:T(8,128)(2,1)}, bf16[4,576,1024]{2,1,0:T(8,128)(2,1)}, bf16[4,256,2048]{2,1,0:T(8,128)(2,1)}) custom-call(s32[4]{0:T(128)} %pad_add_fusion.1.place_ref, bf16[4,4,144,256]{3,2,1,0:T(8,128)(2,1)} %fusion.12.pick_ref, ...), custom_call_target="tpu_custom_call" | custom-call | flops 1 | bytes 1 | tf_op jit(solution)/shard_map/experts_forward/pallas_call | solution.py:491
  472.2 21.2 %experts_down_grad.1 = (bf16[4,576,2048]{2,1,0:T(8,128)(2,1)}, bf16[4,2048,1024]{2,1,0:T(8,128)(2,1)}) custom-call(bf16[4,4,144,256]{3,2,1,0:T(8,128)(2,1)} %fusion.12.pick_ref, bf16[4,576,1024]{2,1,0:T(8,128)(2,1)} %get-tuple-element.39.gated_ref, bf16[256,2048]{1,0:T(8,128)(2,1)} %bitcast.257, bf16[256,2048]{1,0:T(8,128)(2,1)} %copy-done.44, ...), custom_call_target="tpu_custom_call" | custom-call | flops 99999997952 | bytes 1 | tf_op jit(solution)/shard_map/experts_down_grad/pallas_call | solution.py:537
  493.4 8.0 all-to-all-start.5
  501.4 54.7 %experts_backward.1 = (bf16[4,576,2048]{2,1,0:T(8,128)(2,1)}, bf16[256,2176]{1,0:T(8,128)(2,1)}, bf16[256,2176]{1,0:T(8,128)(2,1)}, bf16[256,2176]{1,0:T(8,128)(2,1)}, bf16[256,2176]{1,0:T(8,128)(2,1)}) custom-call(bf16[4,4,256,144]{3,2,1,0:T(8,128)(2,1)} %fusion.7.turned_ref, f32[4,576,1]{2,1,0:T(8,128)} %get-tuple-element.37.gate_ref.gate_rows_ref, ...), custom_call_target="tpu_custom_call" | custom-call | flops 1 | bytes 1 | tf_op jit(solution)/shard_map/experts_backward/pallas_call | solution.py:609
  564.9 35.4 %experts_in_grad.1 = bf16[4,2048,2048]{2,1,0:T(8,128)(2,1)} custom-call(bf16[4,576,2048]{2,1,0:T(8,128)(2,1)} %get-tuple-element.44.rows_ref, bf16[4,576,2048]{2,1,0:T(8,128)(2,1)} %get-tuple-element.45.both_ref, bf16[4,16,128]{2,1,0:T(8,128)(2,1)} %pad_maximum_fusion.4.earlier_ref), custom_call_target="tpu_custom_call" | custom-call | flops 1 | bytes 1 | tf_op jit(solution)/shard_map/experts_in_grad/pallas_call | solution.py:647
  602.1 63.8 %collective-permute-done.20 = bf16[256,2176]{1,0:T(8,128)(2,1)} collective-permute-done((bf16[256,2176]{1,0:T(8,128)(2,1)}, bf16[256,2176]{1,0:T(8,128)(2,1)}, u32[]{:S(2)}, u32[]{:S(2)}) %collective-permute-start.20) | collective-permute-done | bytes 1114144 | tf_op jit(solution)/shard_map/ppermute | solution.py:61
  667.8 19.0 %collective-permute-done.22 = bf16[256,2176]{1,0:T(8,128)(2,1)} collective-permute-done((bf16[256,2176]{1,0:T(8,128)(2,1)}, bf16[256,2176]{1,0:T(8,128)(2,1)}, u32[]{:S(2)}, u32[]{:S(2)}) %collective-permute-start.22) | collective-permute-done | bytes 1114144 | tf_op jit(solution)/shard_map/ppermute | solution.py:61
  709.4 9.1 spread_product.2
  747.0 10.7 %all-to-all-done.6 = bf16[256,4,512]{2,0,1:T(8,128)(2,1)} async-done(((bf16[256,4,512]{2,0,1:T(8,128)(2,1)}), bf16[256,4,512]{2,0,1:T(8,128)(2,1)}, u32[]{:S(2)}, u32[]{:S(2)}) %all-to-all-start.6) | async-done | bytes 1048608 | tf_op jit(solution)/shard_map/all_to_all | solution.py:893
  757.8 21.3 %attend_back.1 = (f32[1024,512]{1,0:T(8,128)}, f32[1024,512]{1,0:T(8,128)}, bf16[1024,512]{1,0:T(8,128)(2,1)}, f32[1024,2]{1,0:T(8,128)}) custom-call(bf16[1024,512]{1,0:T(8,128)(2,1)} %get-tuple-element.50.query_ref, bf16[1024,512]{1,0:T(8,128)(2,1)} %get-tuple-element.51.key_ref, bf16[1024,512]{1,0:T(8,128)(2,1)} %get-tuple-element.52.value_ref, ...), custom_call_target="tpu_custom_call" | custom-call | flops 249999998976 | bytes 1 | tf_op jit(solution)/shard_map/attend_back/pallas_call | solution.py:303
  789.5 6.8 norm_back.1
  799.5 19.4 %spread_product.3 = (bf16[4,256,1664]{2,1,0:T(8,128)(2,1)}, bf16[4,256,1664]{2,1,0:T(8,128)(2,1)}) custom-call(s32[1]{0:T(128)} %bitcast.66.own_ref, bf16[1024,2048]{1,0:T(8,128)(2,1)} %copy-done.3, bf16[1024,1536]{1,0:T(8,128)(2,1)} %get-tuple-element.59.right_ref, f32[2048,128]{1,0:T(8,128)} %pad.19.refs_0_, bf16[2048,1664]{1,0:T(8,128)(2,1)} %assemble.2.refs_1_, ...), custom_call_target="tpu_custom_call" | custom-call | flops 1 | bytes 1 | tf_op jit(solution)/shard_map/spread_product/pallas_call | solution.py:703
  822.6 11.7 %collective-permute-done.25 = bf16[256,2048]{1,0:T(8,128)(2,1)} collective-permute-done((bf16[256,2048]{1,0:T(8,128)(2,1)}, bf16[256,2048]{1,0:T(8,128)(2,1)}, u32[]{:S(2)}, u32[]{:S(2)}) %collective-permute-start.25) | collective-permute-done | bytes 1048608 | tf_op jit(solution)/shard_map/ppermute | solution.py:61
  861.3 8.2 fusion.8
  876.2 21.1 %collective-permute-done.30 = bf16[256,1664]{1,0:T(8,128)(2,1)} collective-permute-done((bf16[256,1664]{1,0:T(8,128)(2,1)}, bf16[256,1664]{1,0:T(8,128)(2,1)}, u32[]{:S(2)}, u32[]{:S(2)}) %collective-permute-start.30) | collective-permute-done | bytes 852000 | tf_op jit(solution)/shard_map/ppermute | solution.py:61
  897.3 32.1 %collective-permute-done.29 = bf16[256,1664]{1,0:T(8,128)(2,1)} collective-permute-done((bf16[256,1664]{1,0:T(8,128)(2,1)}, bf16[256,1664]{1,0:T(8,128)(2,1)}, u32[]{:S(2)}, u32[]{:S(2)}) %collective-permute-start.29) | collective-permute-done | bytes 852000 | tf_op jit(solution)/shard_map/ppermute | solution.py:61
  935.6 10.1 %collective-permute-done.33 = bf16[64,3712]{1,0:T(8,128)(2,1)S(1)} collective-permute-done((bf16[64,3712]{1,0:T(8,128)(2,1)S(1)}, bf16[64,3712]{1,0:T(8,128)(2,1)S(1)}, u32[]{:S(2)}, u32[]{:S(2)}) %collective-permute-start.33) | collective-permute-done | bytes 475168 | tf_op jit(solution)/shard_map/ppermute | solution.py:61
  945.7 9.3 collective-permute-done.32
  (354 shorter events, 271.2 us)
Async XLA Ops:
  34.5 386.2 %all-gather.5.cloned.1.call-start = ((), (), s32[]{:S(2)}) async-start(), calls=%async_computation.12 | async-start | bytes 18874368 | tf_op jit(solution)/shard_map/all_gather | solution.py:790
  52.3 368.3 %all-gather.3.cloned.1.call-start = ((), (), s32[]{:S(2)}) async-start(), calls=%async_computation.11 | async-start | bytes 37748736 | tf_op jit(solution)/shard_map/all_gather | solution.py:790
  65.6 99.2 %all-to-all-start.2 = ((bf16[4,256,2048]{2,1,0:T(8,128)(2,1)}), bf16[4,256,2048]{2,1,0:T(8,128)(2,1)}, u32[]{:S(2)}, u32[]{:S(2)}) async-start(bf16[4,256,2048]{2,1,0:T(8,128)(2,1)} %broadcast_in_dim.93), calls=%async_computation.2 | async-start | bytes 8388608 | tf_op jit(solution)/shard_map/all_to_all | solution.py:48
  71.2 58.6 %collective-permute-start.2 = (bf16[256,1664]{1,0:T(8,128)(2,1)S(1)}, bf16[256,1664]{1,0:T(8,128)(2,1)}, u32[]{:S(2)}, u32[]{:S(2)}) collective-permute-start(bf16[256,1664]{1,0:T(8,128)(2,1)S(1)} %bitcast.265), channel_id=1, source_target_pairs={{0,6},{2,0},{4,2},{6,4},{1,7},{3,1},{5,3},{7,5},{8,14},{10,8},{12,... | collective-permute-start | bytes 2555912 | tf_op jit(solution)/shard_map/ppermute | solution.py:54
  71.7 58.1 %collective-permute-start.1 = (bf16[256,1664]{1,0:T(8,128)(2,1)S(1)}, bf16[256,1664]{1,0:T(8,128)(2,1)}, u32[]{:S(2)}, u32[]{:S(2)}) collective-permute-start(bf16[256,1664]{1,0:T(8,128)(2,1)S(1)} %bitcast.266), channel_id=1, source_target_pairs={{0,4},{2,6},{4,0},{6,2},{1,5},{3,7},{5,1},{7,3},{8,12},{10,14},{12... | collective-permute-start | bytes 2555912 | tf_op jit(solution)/shard_map/ppermute | solution.py:54
  74.3 71.4 %collective-permute-start = (bf16[256,1664]{1,0:T(8,128)(2,1)S(1)}, bf16[256,1664]{1,0:T(8,128)(2,1)S(1)}, u32[]{:S(2)}, u32[]{:S(2)}) collective-permute-start(bf16[256,1664]{1,0:T(8,128)(2,1)S(1)} %bitcast.267), channel_id=1, source_target_pairs={{0,2},{2,4},{4,6},{6,0},{1,3},{3,5},{5,7},{7,1},{8,10},{10,12},{12... | collective-permute-start | bytes 2555912 | tf_op jit(solution)/shard_map/ppermute | solution.py:54
  78.0 75.6 %collective-permute-start.3 = (bf16[256,1664]{1,0:T(8,128)(2,1)S(1)}, bf16[256,1664]{1,0:T(8,128)(2,1)S(1)}, u32[]{:S(2)}, u32[]{:S(2)}) collective-permute-start(bf16[256,1664]{1,0:T(8,128)(2,1)S(1)} %bitcast.268), channel_id=1, source_target_pairs={{0,1},{1,0},{2,3},{3,2},{4,5},{5,4},{6,7},{7,6},{8,9},{9,8},{10,11... | collective-permute-start | bytes 2555912 | tf_op jit(solution)/shard_map/ppermute | solution.py:145
  129.8 27.0 %collective-permute-start.5 = (bf16[256,1664]{1,0:T(8,128)(2,1)}, bf16[256,1664]{1,0:T(8,128)(2,1)}, u32[]{:S(2)}, u32[]{:S(2)}) collective-permute-start(bf16[256,1664]{1,0:T(8,128)(2,1)} %collective-permute-done.1.refs_2_), channel_id=1, source_target_pairs={{0,1},{1,0},{2,3},{3,2},{4,5},{5,4},{6,7},{7,6},{8,9},{9,8},{10,11... | collective-permute-start | bytes 2555912 | tf_op jit(solution)/shard_map/ppermute | solution.py:145
  151.9 38.0 %collective-permute-start.9 = (bf16[256,2048]{1,0:T(8,128)(2,1)}, bf16[256,2048]{1,0:T(8,128)(2,1)}, u32[]{:S(2)}, u32[]{:S(2)}) collective-permute-start(bf16[256,2048]{1,0:T(8,128)(2,1)} %broadcast_add_fusion.refs_0_), channel_id=1, source_target_pairs={{0,6},{2,0},{4,2},{6,4},{1,7},{3,1},{5,3},{7,5},{8,14},{10,8},{12,... | collective-permute-start | bytes 3145736 | tf_op jit(solution)/shard_map/ppermute | solution.py:54
  154.5 66.8 %collective-permute-start.8 = (bf16[256,2048]{1,0:T(8,128)(2,1)}, bf16[256,2048]{1,0:T(8,128)(2,1)}, u32[]{:S(2)}, u32[]{:S(2)}) collective-permute-start(bf16[256,2048]{1,0:T(8,128)(2,1)} %broadcast_add_fusion.refs_0_), channel_id=1, source_target_pairs={{0,4},{2,6},{4,0},{6,2},{1,5},{3,7},{5,1},{7,3},{8,12},{10,14},{12... | collective-permute-start | bytes 3145736 | tf_op jit(solution)/shard_map/ppermute | solution.py:54
  156.7 87.0 %collective-permute-start.7 = (bf16[256,2048]{1,0:T(8,128)(2,1)}, bf16[256,2048]{1,0:T(8,128)(2,1)}, u32[]{:S(2)}, u32[]{:S(2)}) collective-permute-start(bf16[256,2048]{1,0:T(8,128)(2,1)} %broadcast_add_fusion.refs_0_), channel_id=1, source_target_pairs={{0,2},{2,4},{4,6},{6,0},{1,3},{3,5},{5,7},{7,1},{8,10},{10,12},{12... | collective-permute-start | bytes 3145736 | tf_op jit(solution)/shard_map/ppermute | solution.py:54
  182.4 63.9 %all-to-all-start.3 = ((f32[4,2,1024]{2,1,0:T(2,128)}), f32[4,2,1024]{2,1,0:T(2,128)S(1)}, u32[]{:S(2)}, u32[]{:S(2)}) async-start(f32[4,2,1024]{2,1,0:T(2,128)} %broadcast_in_dim.94), calls=%async_computation.3 | async-start | bytes 65536 | tf_op jit(solution)/shard_map/all_to_all | solution.py:48
  189.2 81.3 %collective-permute-start.10 = (bf16[256,2048]{1,0:T(8,128)(2,1)}, bf16[256,2048]{1,0:T(8,128)(2,1)}, u32[]{:S(2)}, u32[]{:S(2)}) collective-permute-start(bf16[256,2048]{1,0:T(8,128)(2,1)} %broadcast_add_fusion.refs_0_), channel_id=1, source_target_pairs={{0,1},{1,0},{2,3},{3,2},{4,5},{5,4},{6,7},{7,6},{8,9},{9,8},{10,11... | collective-permute-start | bytes 3145736 | tf_op jit(solution)/shard_map/ppermute | solution.py:145
  265.9 30.2 %all-to-all-start.4 = ((bf16[4,256,512]{2,1,0:T(8,128)(2,1)}), bf16[4,256,512]{2,1,0:T(8,128)(2,1)}, u32[]{:S(2)}, u32[]{:S(2)}) async-start(bf16[4,256,512]{2,1,0:T(8,128)(2,1)} %bitcast.272), calls=%async_computation.4 | async-start | bytes 2097152 | tf_op jit(solution)/shard_map/all_to_all | solution.py:811
  270.5 696.4 %reduce-scatter.5.cloned.1.call-start = ((), (), s32[]{:S(2)}) async-start(), calls=%async_computation.14 | async-start | bytes 18874368 | tf_op jit(solution)/shard_map/reduce_scatter | solution.py:853
  305.0 29.0 %collective-permute-start.16 = (bf16[256,2048]{1,0:T(8,128)(2,1)S(1)}, bf16[256,2048]{1,0:T(8,128)(2,1)S(1)}, u32[]{:S(2)}, u32[]{:S(2)}) collective-permute-start(bf16[256,2048]{1,0:T(8,128)(2,1)S(1)} %multiply_convert_fusion.refs_0_), channel_id=1, source_target_pairs={{0,6},{2,0},{4,2},{6,4},{1,7},{3,1},{5,3},{7,5},{8,14},{10,8},{12,... | collective-permute-start | bytes 3145736 | tf_op jit(solution)/shard_map/ppermute | solution.py:54
  309.3 67.0 %collective-permute-start.15 = (bf16[256,2048]{1,0:T(8,128)(2,1)S(1)}, bf16[256,2048]{1,0:T(8,128)(2,1)S(1)}, u32[]{:S(2)}, u32[]{:S(2)}) collective-permute-start(bf16[256,2048]{1,0:T(8,128)(2,1)S(1)} %multiply_convert_fusion.refs_0_), channel_id=1, source_target_pairs={{0,4},{2,6},{4,0},{6,2},{1,5},{3,7},{5,1},{7,3},{8,12},{10,14},{12... | collective-permute-start | bytes 3145736 | tf_op jit(solution)/shard_map/ppermute | solution.py:54
  310.0 88.6 %collective-permute-start.14 = (bf16[256,2048]{1,0:T(8,128)(2,1)S(1)}, bf16[256,2048]{1,0:T(8,128)(2,1)}, u32[]{:S(2)}, u32[]{:S(2)}) collective-permute-start(bf16[256,2048]{1,0:T(8,128)(2,1)S(1)} %multiply_convert_fusion.refs_0_), channel_id=1, source_target_pairs={{0,2},{2,4},{4,6},{6,0},{1,3},{3,5},{5,7},{7,1},{8,10},{10,12},{12... | collective-permute-start | bytes 3145736 | tf_op jit(solution)/shard_map/ppermute | solution.py:54
  402.8 66.6 %collective-permute-start.19 = (bf16[256,2048]{1,0:T(8,128)(2,1)}, bf16[256,2048]{1,0:T(8,128)(2,1)}, u32[]{:S(2)}, u32[]{:S(2)}) collective-permute-start(bf16[256,2048]{1,0:T(8,128)(2,1)} %add_add_fusion.3), channel_id=1, source_target_pairs={{0,6},{2,0},{4,2},{6,4},{1,7},{3,1},{5,3},{7,5},{8,14},{10,8},{12,... | collective-permute-start | bytes 3145736 | tf_op jit(solution)/shard_map/ppermute | solution.py:837
  405.7 66.6 %collective-permute-start.18 = (bf16[256,2048]{1,0:T(8,128)(2,1)}, bf16[256,2048]{1,0:T(8,128)(2,1)}, u32[]{:S(2)}, u32[]{:S(2)}) collective-permute-start(bf16[256,2048]{1,0:T(8,128)(2,1)} %add_add_fusion.3), channel_id=1, source_target_pairs={{0,4},{2,6},{4,0},{6,2},{1,5},{3,7},{5,1},{7,3},{8,12},{10,14},{12... | collective-permute-start | bytes 3145736 | tf_op jit(solution)/shard_map/ppermute | solution.py:837
  493.4 196.1 %all-to-all-start.5 = ((bf16[4,256,2048]{2,1,0:T(8,128)(2,1)}), bf16[4,256,2048]{2,1,0:T(8,128)(2,1)}, u32[]{:S(2)}, u32[]{:S(2)}) async-start(bf16[4,256,2048]{2,1,0:T(8,128)(2,1)} %get-tuple-element.38), calls=%async_computation.5 | async-start | bytes 8388608 | tf_op jit(solution)/shard_map/all_to_all | solution.py:48
  501.4 470.0 %reduce-scatter.3.cloned.1.call-start = ((), (), s32[]{:S(2)}) async-start(), calls=%async_computation.13 | async-start | bytes 37748736 | tf_op jit(solution)/shard_map/reduce_scatter | solution.py:865
  556.2 109.7 %collective-permute-start.20 = (bf16[256,2176]{1,0:T(8,128)(2,1)}, bf16[256,2176]{1,0:T(8,128)(2,1)}, u32[]{:S(2)}, u32[]{:S(2)}) collective-permute-start(bf16[256,2176]{1,0:T(8,128)(2,1)} %get-tuple-element.46), channel_id=1, source_target_pairs={{0,6},{2,0},{4,2},{6,4},{1,7},{3,1},{5,3},{7,5},{8,14},{10,8},{12,... | collective-permute-start | bytes 3342344 | tf_op jit(solution)/shard_map/ppermute | solution.py:61
  556.2 110.6 %collective-permute-start.21 = (bf16[256,2176]{1,0:T(8,128)(2,1)}, bf16[256,2176]{1,0:T(8,128)(2,1)}, u32[]{:S(2)}, u32[]{:S(2)}) collective-permute-start(bf16[256,2176]{1,0:T(8,128)(2,1)} %get-tuple-element.47), channel_id=1, source_target_pairs={{0,4},{2,6},{4,0},{6,2},{1,5},{3,7},{5,1},{7,3},{8,12},{10,14},{12... | collective-permute-start | bytes 3342344 | tf_op jit(solution)/shard_map/ppermute | solution.py:61
  559.8 126.9 %collective-permute-start.22 = (bf16[256,2176]{1,0:T(8,128)(2,1)}, bf16[256,2176]{1,0:T(8,128)(2,1)}, u32[]{:S(2)}, u32[]{:S(2)}) collective-permute-start(bf16[256,2176]{1,0:T(8,128)(2,1)} %get-tuple-element.48), channel_id=1, source_target_pairs={{0,2},{2,4},{4,6},{6,0},{1,3},{3,5},{5,7},{7,1},{8,10},{10,12},{12... | collective-permute-start | bytes 3342344 | tf_op jit(solution)/shard_map/ppermute | solution.py:61
  727.2 30.6 %all-to-all-start.6 = ((bf16[256,4,512]{2,0,1:T(8,128)(2,1)}), bf16[256,4,512]{2,0,1:T(8,128)(2,1)}, u32[]{:S(2)}, u32[]{:S(2)}) async-start(bf16[256,4,512]{2,0,1:T(8,128)(2,1)} %bitcast.248), calls=%async_computation.6 | async-start | bytes 2097152 | tf_op jit(solution)/shard_map/all_to_all | solution.py:893
  739.7 79.2 %collective-permute-start.24 = (bf16[256,2048]{1,0:T(8,128)(2,1)}, bf16[256,2048]{1,0:T(8,128)(2,1)}, u32[]{:S(2)}, u32[]{:S(2)}) collective-permute-start(bf16[256,2048]{1,0:T(8,128)(2,1)} %get-tuple-element.123), channel_id=1, source_target_pairs={{0,6},{2,0},{4,2},{6,4},{1,7},{3,1},{5,3},{7,5},{8,14},{10,8},{12,... | collective-permute-start | bytes 3145736 | tf_op jit(solution)/shard_map/ppermute | solution.py:61
  744.1 76.7 %collective-permute-start.26 = (bf16[256,2048]{1,0:T(8,128)(2,1)}, bf16[256,2048]{1,0:T(8,128)(2,1)}, u32[]{:S(2)}, u32[]{:S(2)}) collective-permute-start(bf16[256,2048]{1,0:T(8,128)(2,1)} %get-tuple-element.124), channel_id=1, source_target_pairs={{0,2},{2,4},{4,6},{6,0},{1,3},{3,5},{5,7},{7,1},{8,10},{10,12},{12... | collective-permute-start | bytes 3145736 | tf_op jit(solution)/shard_map/ppermute | solution.py:61
  744.1 90.2 %collective-permute-start.25 = (bf16[256,2048]{1,0:T(8,128)(2,1)}, bf16[256,2048]{1,0:T(8,128)(2,1)}, u32[]{:S(2)}, u32[]{:S(2)}) collective-permute-start(bf16[256,2048]{1,0:T(8,128)(2,1)} %get-tuple-element.125), channel_id=1, source_target_pairs={{0,4},{2,6},{4,0},{6,2},{1,5},{3,7},{5,1},{7,3},{8,12},{10,14},{12... | collective-permute-start | bytes 3145736 | tf_op jit(solution)/shard_map/ppermute | solution.py:61
  854.7 42.6 %collective-permute-start.30 = (bf16[256,1664]{1,0:T(8,128)(2,1)}, bf16[256,1664]{1,0:T(8,128)(2,1)}, u32[]{:S(2)}, u32[]{:S(2)}) collective-permute-start(bf16[256,1664]{1,0:T(8,128)(2,1)} %get-tuple-element.127), channel_id=1, source_target_pairs={{0,2},{2,4},{4,6},{6,0},{1,3},{3,5},{5,7},{7,1},{8,10},{10,12},{12... | collective-permute-start | bytes 2555912 | tf_op jit(solution)/shard_map/ppermute | solution.py:61
  856.1 73.3 %collective-permute-start.29 = (bf16[256,1664]{1,0:T(8,128)(2,1)}, bf16[256,1664]{1,0:T(8,128)(2,1)}, u32[]{:S(2)}, u32[]{:S(2)}) collective-permute-start(bf16[256,1664]{1,0:T(8,128)(2,1)} %get-tuple-element.128), channel_id=1, source_target_pairs={{0,4},{2,6},{4,0},{6,2},{1,5},{3,7},{5,1},{7,3},{8,12},{10,14},{12... | collective-permute-start | bytes 2555912 | tf_op jit(solution)/shard_map/ppermute | solution.py:61
  869.5 87.9 %all-to-all-start.8 = ((bf16[4,256,2048]{2,1,0:T(8,128)(2,1)}), bf16[4,256,2048]{2,1,0:T(8,128)(2,1)}, u32[]{:S(2)}, u32[]{:S(2)}) async-start(bf16[4,256,2048]{2,1,0:T(8,128)(2,1)} %bitcast.264), calls=%async_computation.8 | async-start | bytes 8388608 | tf_op jit(solution)/shard_map/all_to_all | solution.py:48
  (64 other events, 1197.9 us)
Sparse Core Ops, SparseCore 0:
  52.5 127.3 all-gather.4
  181.8 172.0 all-gather.2
  493.6 116.9 reduce-scatter.4
  614.0 216.9 reduce-scatter.2

commit v5 on v4

--- a/solution.py
+++ b/solution.py
@@ -24,7 +24,7 @@
 KERNEL_PARAMS = pltpu.CompilerParams(vmem_limit_bytes=VMEM_BYTES)
 SMALL_COST = pl.CostEstimate(flops=1, bytes_accessed=1, transcendentals=0)
 DOWN_GRAD_COST = pl.CostEstimate(flops=10**11, bytes_accessed=1, transcendentals=0)
-ATTEND_BACK_COST = pl.CostEstimate(flops=250 * 10**9, bytes_accessed=1, transcendentals=0)
+ATTEND_BACK_COST = pl.CostEstimate(flops=310 * 10**9, bytes_accessed=1, transcendentals=0)
 
 
 def after(value, other):
@@ -938,7 +938,9 @@
         attn_in_part.astype(bf16).reshape(seq_count, tok_count, model_width), "seq"
     )
     attn_in_grad = jnp.sum(attn_in_grad.astype(f32), axis=0)
-    heads_terms = scatter(heads_terms, "exp").astype(bf16)
+    heads_blocks = split(heads_terms, "exp")
+    heads_blocks[0] = after(after(heads_blocks[0], grad_expert_in), grad_expert_out)
+    heads_terms = add_up(send_near(heads_blocks, "exp")).astype(bf16)
     terms_cols = heads_terms.shape[1]
     last_terms = jnp.concatenate([heads_terms, out_terms], axis=1)
     last_near = send_near(split(last_terms.reshape(seq_count, rows_dev, -1), "seq"), "seq")

time: 998 us -> 989 us (level)
  waiting for transfers between devices: 425 us -> 415 us
    ppermute x12, waiting for transfers between devices: 169 us -> 120 us  [send_near(): lax.ppermute(blocks[k], axis, shift_pairs(count, -k))]
    all_to_all x7, waiting for transfers between devices: 15.6 us -> 50.3 us  [exchange(): lax.all_to_all(stacked, axis, split_axis=split_axis, concat_axis=split_ax...]
  transfers between devices with their start and end apart: 47 -> 47, of which waited for: 23 -> 22; matrix products, arithmetic and copies ran while one was open for 16% -> 15% of each run, Pallas kernels for 24% -> 25%
where the time goes in v5:
time: 989 us; the launch traced here: 975 us
  waiting for transfers between devices  415 us (42%)
  Pallas kernels  267 us (27%)
  starting transfers between devices  90.9 us (9%)
  other arithmetic  73.1 us (7%)
  local copies, waits for them, and re-layouts  67 us (7%)
  matrix products  33.1 us (3%)
  between operations  29.7 us (3%)
    ppermute x9, waiting for transfers between devices, gather_near(): lax.ppermute(block, axis, shift_pairs(count, k))  199 us
    ppermute x12, waiting for transfers between devices, send_near(): lax.ppermute(blocks[k], axis, shift_pairs(count, -k))  120 us
    pallas_call x1, Pallas kernels, experts_backward(): pl.pallas_call(functools.partial(backward_kernel, first, count, len(kept)...  54.7 us
    all_to_all x7, waiting for transfers between devices, exchange(): lax.all_to_all(stacked, axis, split_axis=split_axis, concat_axis=split_ax...  50.3 us
    pallas_call x1, Pallas kernels, experts_forward(): pl.pallas_call(functools.partial(forward_kernel, count, len(kept)), grid=...  48.6 us
    all_to_all x7, starting transfers between devices, exchange(): lax.all_to_all(stacked, axis, split_axis=split_axis, concat_axis=split_ax...  35.5 us
    pallas_call x1, Pallas kernels, experts_in_grad(): pl.pallas_call(in_grad_kernel, grid=(experts,), in_specs=[each(rows.shape...  35.4 us
    pallas_call x2, Pallas kernels, spread_product(): pl.pallas_call(functools.partial(spread_kernel, split, len(shapes)), in_s...  28.5 us
  transfers between devices with their start and end apart: 47, of which 22 were waited for; matrix products, arithmetic and copies ran while one was open for 15% of the time, Pallas kernels for 25%

profile of v5, /device:TPU:10, one launch (start us, length us, event | category | flops | bytes accessed | tf_op | source)
XLA Modules:
  0.0 975.3 jit_solution(2541786213895880878)
XLA Ops:
  18.7 9.4 all-to-all-done
  34.5 7.0 collective-permute-done.17.refs_1_
  52.4 9.0 fusion.6
  78.1 51.7 %collective-permute-done.2.refs_3_ = bf16[256,1664]{1,0:T(8,128)(2,1)} collective-permute-done((bf16[256,1664]{1,0:T(8,128)(2,1)S(1)}, bf16[256,1664]{1,0:T(8,128)(2,1)}, u32[]{:S(2)}, u32[]{:S(2)}) %collective-permute-start.2) | collective-permute-done | bytes 852000 | tf_op jit(solution)/shard_map/ppermute | solution.py:54
  130.3 15.4 %collective-permute-done.refs_1_ = bf16[256,1664]{1,0:T(8,128)(2,1)S(1)} collective-permute-done((bf16[256,1664]{1,0:T(8,128)(2,1)S(1)}, bf16[256,1664]{1,0:T(8,128)(2,1)S(1)}, u32[]{:S(2)}, u32[]{:S(2)}) %collective-permute-start) | collective-permute-done | bytes 852000 | tf_op jit(solution)/shard_map/ppermute | solution.py:54
  191.7 29.7 %collective-permute-done.8.refs_2_ = bf16[256,2048]{1,0:T(8,128)(2,1)} collective-permute-done((bf16[256,2048]{1,0:T(8,128)(2,1)}, bf16[256,2048]{1,0:T(8,128)(2,1)}, u32[]{:S(2)}, u32[]{:S(2)}) %collective-permute-start.8) | collective-permute-done | bytes 1048608 | tf_op jit(solution)/shard_map/ppermute | solution.py:54
  223.2 20.6 %collective-permute-done.7.refs_1_ = bf16[256,2048]{1,0:T(8,128)(2,1)} collective-permute-done((bf16[256,2048]{1,0:T(8,128)(2,1)}, bf16[256,2048]{1,0:T(8,128)(2,1)}, u32[]{:S(2)}, u32[]{:S(2)}) %collective-permute-start.7) | collective-permute-done | bytes 1048608 | tf_op jit(solution)/shard_map/ppermute | solution.py:54
  248.2 17.7 %attend.1 = (bf16[1024,512]{1,0:T(8,128)(2,1)}, bf16[1024,512]{1,0:T(8,128)(2,1)}, bf16[1024,512]{1,0:T(8,128)(2,1)}, bf16[1024,512]{1,0:T(8,128)(2,1)}) custom-call(f32[1024,1536]{1,0:T(8,128)} %copy-done, f32[1024,1536]{1,0:T(8,128)} %copy-done, f32[1024,1536]{1,0:T(8,128)} %copy-done, f32[1024,2]{1,0:T(8,128)} %add_add_fusion.4.scale_ref, ...), custom_call_target="tpu_custom_call" | custom-call | flops 1 | bytes 1 | tf_op jit(solution)/shard_map/attend/pallas_call | solution.py:240
  270.5 7.5 assemble.3
  278.0 18.0 %all-to-all-done.4 = bf16[4,256,512]{2,1,0:T(8,128)(2,1)} async-done(((bf16[4,256,512]{2,1,0:T(8,128)(2,1)}), bf16[4,256,512]{2,1,0:T(8,128)(2,1)}, u32[]{:S(2)}, u32[]{:S(2)}) %all-to-all-start.4) | async-done | bytes 1048608 | tf_op jit(solution)/shard_map/all_to_all | solution.py:811
  314.2 19.8 %collective-permute-done.16.refs_3_ = bf16[256,2048]{1,0:T(8,128)(2,1)S(1)} collective-permute-done((bf16[256,2048]{1,0:T(8,128)(2,1)S(1)}, bf16[256,2048]{1,0:T(8,128)(2,1)S(1)}, u32[]{:S(2)}, u32[]{:S(2)}) %collective-permute-start.16) | collective-permute-done | bytes 1048608 | tf_op jit(solution)/shard_map/ppermute | solution.py:54
  335.1 41.1 %collective-permute-done.15.refs_2_ = bf16[256,2048]{1,0:T(8,128)(2,1)S(1)} collective-permute-done((bf16[256,2048]{1,0:T(8,128)(2,1)S(1)}, bf16[256,2048]{1,0:T(8,128)(2,1)S(1)}, u32[]{:S(2)}, u32[]{:S(2)}) %collective-permute-start.15) | collective-permute-done | bytes 1048608 | tf_op jit(solution)/shard_map/ppermute | solution.py:54
  377.4 21.2 %collective-permute-done.14.refs_1_ = bf16[256,2048]{1,0:T(8,128)(2,1)} collective-permute-done((bf16[256,2048]{1,0:T(8,128)(2,1)S(1)}, bf16[256,2048]{1,0:T(8,128)(2,1)}, u32[]{:S(2)}, u32[]{:S(2)}) %collective-permute-start.14) | collective-permute-done | bytes 1048608 | tf_op jit(solution)/shard_map/ppermute | solution.py:54
  412.7 8.0 route.1
  420.7 48.6 %experts_forward.1 = (bf16[4,576,2048]{2,1,0:T(8,128)(2,1)}, bf16[4,576,1024]{2,1,0:T(8,128)(2,1)}, bf16[4,576,1024]{2,1,0:T(8,128)(2,1)}, bf16[4,576,1024]{2,1,0:T(8,128)(2,1)}, bf16[4,256,2048]{2,1,0:T(8,128)(2,1)}) custom-call(s32[4]{0:T(128)} %pad_add_fusion.1.place_ref, bf16[4,4,144,256]{3,2,1,0:T(8,128)(2,1)} %fusion.12.pick_ref, ...), custom_call_target="tpu_custom_call" | custom-call | flops 1 | bytes 1 | tf_op jit(solution)/shard_map/experts_forward/pallas_call | solution.py:491
  472.2 21.2 %experts_down_grad.1 = (bf16[4,576,2048]{2,1,0:T(8,128)(2,1)}, bf16[4,2048,1024]{2,1,0:T(8,128)(2,1)}) custom-call(bf16[4,4,144,256]{3,2,1,0:T(8,128)(2,1)} %fusion.12.pick_ref, bf16[4,576,1024]{2,1,0:T(8,128)(2,1)} %get-tuple-element.39.gated_ref, bf16[256,2048]{1,0:T(8,128)(2,1)} %bitcast.259, bf16[256,2048]{1,0:T(8,128)(2,1)} %copy-done.47, ...), custom_call_target="tpu_custom_call" | custom-call | flops 99999997952 | bytes 1 | tf_op jit(solution)/shard_map/experts_down_grad/pallas_call | solution.py:537
  493.4 8.0 all-to-all-start.5
  501.4 54.7 %experts_backward.1 = (bf16[4,576,2048]{2,1,0:T(8,128)(2,1)}, bf16[256,2176]{1,0:T(8,128)(2,1)}, bf16[256,2176]{1,0:T(8,128)(2,1)}, bf16[256,2176]{1,0:T(8,128)(2,1)}, bf16[256,2176]{1,0:T(8,128)(2,1)}) custom-call(bf16[4,4,256,144]{3,2,1,0:T(8,128)(2,1)} %fusion.7.turned_ref, f32[4,576,1]{2,1,0:T(8,128)} %get-tuple-element.37.gate_ref.gate_rows_ref, ...), custom_call_target="tpu_custom_call" | custom-call | flops 1 | bytes 1 | tf_op jit(solution)/shard_map/experts_backward/pallas_call | solution.py:609
  564.8 35.4 %experts_in_grad.1 = bf16[4,2048,2048]{2,1,0:T(8,128)(2,1)} custom-call(bf16[4,576,2048]{2,1,0:T(8,128)(2,1)} %get-tuple-element.44.rows_ref, bf16[4,576,2048]{2,1,0:T(8,128)(2,1)} %get-tuple-element.45.both_ref, bf16[4,16,128]{2,1,0:T(8,128)(2,1)} %pad_maximum_fusion.4.earlier_ref), custom_call_target="tpu_custom_call" | custom-call | flops 1 | bytes 1 | tf_op jit(solution)/shard_map/experts_in_grad/pallas_call | solution.py:647
  602.1 63.8 %collective-permute-done.20 = bf16[256,2176]{1,0:T(8,128)(2,1)} collective-permute-done((bf16[256,2176]{1,0:T(8,128)(2,1)}, bf16[256,2176]{1,0:T(8,128)(2,1)}, u32[]{:S(2)}, u32[]{:S(2)}) %collective-permute-start.20) | collective-permute-done | bytes 1114144 | tf_op jit(solution)/shard_map/ppermute | solution.py:61
  667.8 19.0 %collective-permute-done.22 = bf16[256,2176]{1,0:T(8,128)(2,1)} collective-permute-done((bf16[256,2176]{1,0:T(8,128)(2,1)}, bf16[256,2176]{1,0:T(8,128)(2,1)}, u32[]{:S(2)}, u32[]{:S(2)}) %collective-permute-start.22) | collective-permute-done | bytes 1114144 | tf_op jit(solution)/shard_map/ppermute | solution.py:61
  709.4 9.0 spread_product.2
  747.1 10.7 %all-to-all-done.6 = bf16[256,4,512]{2,0,1:T(8,128)(2,1)} async-done(((bf16[256,4,512]{2,0,1:T(8,128)(2,1)}), bf16[256,4,512]{2,0,1:T(8,128)(2,1)}, u32[]{:S(2)}, u32[]{:S(2)}) %all-to-all-start.6) | async-done | bytes 1048608 | tf_op jit(solution)/shard_map/all_to_all | solution.py:893
  757.8 21.3 %attend_back.1 = (f32[1024,512]{1,0:T(8,128)}, f32[1024,512]{1,0:T(8,128)}, bf16[1024,512]{1,0:T(8,128)(2,1)}, f32[1024,2]{1,0:T(8,128)}) custom-call(bf16[1024,512]{1,0:T(8,128)(2,1)} %get-tuple-element.50.query_ref, bf16[1024,512]{1,0:T(8,128)(2,1)} %get-tuple-element.51.key_ref, bf16[1024,512]{1,0:T(8,128)(2,1)} %get-tuple-element.52.value_ref, ...), custom_call_target="tpu_custom_call" | custom-call | flops 309999992832 | bytes 1 | tf_op jit(solution)/shard_map/attend_back/pallas_call | solution.py:303
  789.5 6.8 norm_back.1
  799.5 19.5 %spread_product.3 = (bf16[4,256,1664]{2,1,0:T(8,128)(2,1)}, bf16[4,256,1664]{2,1,0:T(8,128)(2,1)}) custom-call(s32[1]{0:T(128)} %bitcast.66.own_ref, bf16[1024,2048]{1,0:T(8,128)(2,1)} %copy-done.5, bf16[1024,1536]{1,0:T(8,128)(2,1)} %get-tuple-element.59.right_ref, f32[2048,128]{1,0:T(8,128)} %pad.19.refs_0_, bf16[2048,1664]{1,0:T(8,128)(2,1)} %assemble.2.refs_1_, ...), custom_call_target="tpu_custom_call" | custom-call | flops 1 | bytes 1 | tf_op jit(solution)/shard_map/spread_product/pallas_call | solution.py:703
  822.6 11.7 %collective-permute-done.25 = bf16[256,2048]{1,0:T(8,128)(2,1)} collective-permute-done((bf16[256,2048]{1,0:T(8,128)(2,1)}, bf16[256,2048]{1,0:T(8,128)(2,1)}, u32[]{:S(2)}, u32[]{:S(2)}) %collective-permute-start.25) | collective-permute-done | bytes 1048608 | tf_op jit(solution)/shard_map/ppermute | solution.py:61
  848.8 8.2 fusion.8
  875.2 34.6 %all-to-all-done.8 = bf16[4,256,2048]{2,1,0:T(8,128)(2,1)} async-done(((bf16[4,256,2048]{2,1,0:T(8,128)(2,1)}), bf16[4,256,2048]{2,1,0:T(8,128)(2,1)}, u32[]{:S(2)}, u32[]{:S(2)}) %all-to-all-start.8) | async-done | bytes 4194336 | tf_op jit(solution)/shard_map/all_to_all | solution.py:48
  929.6 9.5 collective-permute-done.29
  948.6 7.1 collective-permute-done.33
  955.6 9.1 collective-permute-done.32
  (362 shorter events, 271.3 us)
Async XLA Ops:
  34.5 386.2 %all-gather.5.cloned.1.call-start = ((), (), s32[]{:S(2)}) async-start(), calls=%async_computation.12 | async-start | bytes 18874368 | tf_op jit(solution)/shard_map/all_gather | solution.py:790
  52.4 368.3 %all-gather.3.cloned.1.call-start = ((), (), s32[]{:S(2)}) async-start(), calls=%async_computation.11 | async-start | bytes 37748736 | tf_op jit(solution)/shard_map/all_gather | solution.py:790
  65.6 99.3 %all-to-all-start.2 = ((bf16[4,256,2048]{2,1,0:T(8,128)(2,1)}), bf16[4,256,2048]{2,1,0:T(8,128)(2,1)}, u32[]{:S(2)}, u32[]{:S(2)}) async-start(bf16[4,256,2048]{2,1,0:T(8,128)(2,1)} %broadcast_in_dim.93), calls=%async_computation.2 | async-start | bytes 8388608 | tf_op jit(solution)/shard_map/all_to_all | solution.py:48
  71.2 58.6 %collective-permute-start.2 = (bf16[256,1664]{1,0:T(8,128)(2,1)S(1)}, bf16[256,1664]{1,0:T(8,128)(2,1)}, u32[]{:S(2)}, u32[]{:S(2)}) collective-permute-start(bf16[256,1664]{1,0:T(8,128)(2,1)S(1)} %bitcast.267), channel_id=1, source_target_pairs={{0,6},{2,0},{4,2},{6,4},{1,7},{3,1},{5,3},{7,5},{8,14},{10,8},{12,... | collective-permute-start | bytes 2555912 | tf_op jit(solution)/shard_map/ppermute | solution.py:54
  71.7 58.1 %collective-permute-start.1 = (bf16[256,1664]{1,0:T(8,128)(2,1)S(1)}, bf16[256,1664]{1,0:T(8,128)(2,1)}, u32[]{:S(2)}, u32[]{:S(2)}) collective-permute-start(bf16[256,1664]{1,0:T(8,128)(2,1)S(1)} %bitcast.268), channel_id=1, source_target_pairs={{0,4},{2,6},{4,0},{6,2},{1,5},{3,7},{5,1},{7,3},{8,12},{10,14},{12... | collective-permute-start | bytes 2555912 | tf_op jit(solution)/shard_map/ppermute | solution.py:54
  74.3 71.4 %collective-permute-start = (bf16[256,1664]{1,0:T(8,128)(2,1)S(1)}, bf16[256,1664]{1,0:T(8,128)(2,1)S(1)}, u32[]{:S(2)}, u32[]{:S(2)}) collective-permute-start(bf16[256,1664]{1,0:T(8,128)(2,1)S(1)} %bitcast.269), channel_id=1, source_target_pairs={{0,2},{2,4},{4,6},{6,0},{1,3},{3,5},{5,7},{7,1},{8,10},{10,12},{12... | collective-permute-start | bytes 2555912 | tf_op jit(solution)/shard_map/ppermute | solution.py:54
  78.0 75.6 %collective-permute-start.3 = (bf16[256,1664]{1,0:T(8,128)(2,1)S(1)}, bf16[256,1664]{1,0:T(8,128)(2,1)S(1)}, u32[]{:S(2)}, u32[]{:S(2)}) collective-permute-start(bf16[256,1664]{1,0:T(8,128)(2,1)S(1)} %bitcast.270), channel_id=1, source_target_pairs={{0,1},{1,0},{2,3},{3,2},{4,5},{5,4},{6,7},{7,6},{8,9},{9,8},{10,11... | collective-permute-start | bytes 2555912 | tf_op jit(solution)/shard_map/ppermute | solution.py:145
  151.9 37.9 %collective-permute-start.9 = (bf16[256,2048]{1,0:T(8,128)(2,1)}, bf16[256,2048]{1,0:T(8,128)(2,1)}, u32[]{:S(2)}, u32[]{:S(2)}) collective-permute-start(bf16[256,2048]{1,0:T(8,128)(2,1)} %broadcast_add_fusion.refs_0_), channel_id=1, source_target_pairs={{0,6},{2,0},{4,2},{6,4},{1,7},{3,1},{5,3},{7,5},{8,14},{10,8},{12,... | collective-permute-start | bytes 3145736 | tf_op jit(solution)/shard_map/ppermute | solution.py:54
  154.5 66.8 %collective-permute-start.8 = (bf16[256,2048]{1,0:T(8,128)(2,1)}, bf16[256,2048]{1,0:T(8,128)(2,1)}, u32[]{:S(2)}, u32[]{:S(2)}) collective-permute-start(bf16[256,2048]{1,0:T(8,128)(2,1)} %broadcast_add_fusion.refs_0_), channel_id=1, source_target_pairs={{0,4},{2,6},{4,0},{6,2},{1,5},{3,7},{5,1},{7,3},{8,12},{10,14},{12... | collective-permute-start | bytes 3145736 | tf_op jit(solution)/shard_map/ppermute | solution.py:54
  156.8 87.0 %collective-permute-start.7 = (bf16[256,2048]{1,0:T(8,128)(2,1)}, bf16[256,2048]{1,0:T(8,128)(2,1)}, u32[]{:S(2)}, u32[]{:S(2)}) collective-permute-start(bf16[256,2048]{1,0:T(8,128)(2,1)} %broadcast_add_fusion.refs_0_), channel_id=1, source_target_pairs={{0,2},{2,4},{4,6},{6,0},{1,3},{3,5},{5,7},{7,1},{8,10},{10,12},{12... | collective-permute-start | bytes 3145736 | tf_op jit(solution)/shard_map/ppermute | solution.py:54
  182.4 63.8 %all-to-all-start.3 = ((f32[4,2,1024]{2,1,0:T(2,128)}), f32[4,2,1024]{2,1,0:T(2,128)S(1)}, u32[]{:S(2)}, u32[]{:S(2)}) async-start(f32[4,2,1024]{2,1,0:T(2,128)} %broadcast_in_dim.94), calls=%async_computation.3 | async-start | bytes 65536 | tf_op jit(solution)/shard_map/all_to_all | solution.py:48
  189.2 81.3 %collective-permute-start.10 = (bf16[256,2048]{1,0:T(8,128)(2,1)}, bf16[256,2048]{1,0:T(8,128)(2,1)}, u32[]{:S(2)}, u32[]{:S(2)}) collective-permute-start(bf16[256,2048]{1,0:T(8,128)(2,1)} %broadcast_add_fusion.refs_0_), channel_id=1, source_target_pairs={{0,1},{1,0},{2,3},{3,2},{4,5},{5,4},{6,7},{7,6},{8,9},{9,8},{10,11... | collective-permute-start | bytes 3145736 | tf_op jit(solution)/shard_map/ppermute | solution.py:145
  265.9 30.1 %all-to-all-start.4 = ((bf16[4,256,512]{2,1,0:T(8,128)(2,1)}), bf16[4,256,512]{2,1,0:T(8,128)(2,1)}, u32[]{:S(2)}, u32[]{:S(2)}) async-start(bf16[4,256,512]{2,1,0:T(8,128)(2,1)} %bitcast.274), calls=%async_computation.4 | async-start | bytes 2097152 | tf_op jit(solution)/shard_map/all_to_all | solution.py:811
  270.4 644.4 %reduce-scatter.5.cloned.1.call-start = ((), (), s32[]{:S(2)}) async-start(), calls=%async_computation.14 | async-start | bytes 18874368 | tf_op jit(solution)/shard_map/reduce_scatter | solution.py:853
  305.0 29.0 %collective-permute-start.16 = (bf16[256,2048]{1,0:T(8,128)(2,1)S(1)}, bf16[256,2048]{1,0:T(8,128)(2,1)S(1)}, u32[]{:S(2)}, u32[]{:S(2)}) collective-permute-start(bf16[256,2048]{1,0:T(8,128)(2,1)S(1)} %multiply_convert_fusion.refs_0_), channel_id=1, source_target_pairs={{0,6},{2,0},{4,2},{6,4},{1,7},{3,1},{5,3},{7,5},{8,14},{10,8},{12,... | collective-permute-start | bytes 3145736 | tf_op jit(solution)/shard_map/ppermute | solution.py:54
  309.2 67.0 %collective-permute-start.15 = (bf16[256,2048]{1,0:T(8,128)(2,1)S(1)}, bf16[256,2048]{1,0:T(8,128)(2,1)S(1)}, u32[]{:S(2)}, u32[]{:S(2)}) collective-permute-start(bf16[256,2048]{1,0:T(8,128)(2,1)S(1)} %multiply_convert_fusion.refs_0_), channel_id=1, source_target_pairs={{0,4},{2,6},{4,0},{6,2},{1,5},{3,7},{5,1},{7,3},{8,12},{10,14},{12... | collective-permute-start | bytes 3145736 | tf_op jit(solution)/shard_map/ppermute | solution.py:54
  310.0 88.6 %collective-permute-start.14 = (bf16[256,2048]{1,0:T(8,128)(2,1)S(1)}, bf16[256,2048]{1,0:T(8,128)(2,1)}, u32[]{:S(2)}, u32[]{:S(2)}) collective-permute-start(bf16[256,2048]{1,0:T(8,128)(2,1)S(1)} %multiply_convert_fusion.refs_0_), channel_id=1, source_target_pairs={{0,2},{2,4},{4,6},{6,0},{1,3},{3,5},{5,7},{7,1},{8,10},{10,12},{12... | collective-permute-start | bytes 3145736 | tf_op jit(solution)/shard_map/ppermute | solution.py:54
  402.7 66.5 %collective-permute-start.19 = (bf16[256,2048]{1,0:T(8,128)(2,1)}, bf16[256,2048]{1,0:T(8,128)(2,1)}, u32[]{:S(2)}, u32[]{:S(2)}) collective-permute-start(bf16[256,2048]{1,0:T(8,128)(2,1)} %add_add_fusion.3), channel_id=1, source_target_pairs={{0,6},{2,0},{4,2},{6,4},{1,7},{3,1},{5,3},{7,5},{8,14},{10,8},{12,... | collective-permute-start | bytes 3145736 | tf_op jit(solution)/shard_map/ppermute | solution.py:837
  405.7 66.6 %collective-permute-start.18 = (bf16[256,2048]{1,0:T(8,128)(2,1)}, bf16[256,2048]{1,0:T(8,128)(2,1)}, u32[]{:S(2)}, u32[]{:S(2)}) collective-permute-start(bf16[256,2048]{1,0:T(8,128)(2,1)} %add_add_fusion.3), channel_id=1, source_target_pairs={{0,4},{2,6},{4,0},{6,2},{1,5},{3,7},{5,1},{7,3},{8,12},{10,14},{12... | collective-permute-start | bytes 3145736 | tf_op jit(solution)/shard_map/ppermute | solution.py:837
  493.4 196.1 %all-to-all-start.5 = ((bf16[4,256,2048]{2,1,0:T(8,128)(2,1)}), bf16[4,256,2048]{2,1,0:T(8,128)(2,1)}, u32[]{:S(2)}, u32[]{:S(2)}) async-start(bf16[4,256,2048]{2,1,0:T(8,128)(2,1)} %get-tuple-element.38), calls=%async_computation.5 | async-start | bytes 8388608 | tf_op jit(solution)/shard_map/all_to_all | solution.py:48
  501.4 419.9 %reduce-scatter.3.cloned.1.call-start = ((), (), s32[]{:S(2)}) async-start(), calls=%async_computation.13 | async-start | bytes 37748736 | tf_op jit(solution)/shard_map/reduce_scatter | solution.py:865
  556.2 109.7 %collective-permute-start.20 = (bf16[256,2176]{1,0:T(8,128)(2,1)}, bf16[256,2176]{1,0:T(8,128)(2,1)}, u32[]{:S(2)}, u32[]{:S(2)}) collective-permute-start(bf16[256,2176]{1,0:T(8,128)(2,1)} %get-tuple-element.46), channel_id=1, source_target_pairs={{0,6},{2,0},{4,2},{6,4},{1,7},{3,1},{5,3},{7,5},{8,14},{10,8},{12,... | collective-permute-start | bytes 3342344 | tf_op jit(solution)/shard_map/ppermute | solution.py:61
  556.2 110.6 %collective-permute-start.21 = (bf16[256,2176]{1,0:T(8,128)(2,1)}, bf16[256,2176]{1,0:T(8,128)(2,1)}, u32[]{:S(2)}, u32[]{:S(2)}) collective-permute-start(bf16[256,2176]{1,0:T(8,128)(2,1)} %get-tuple-element.47), channel_id=1, source_target_pairs={{0,4},{2,6},{4,0},{6,2},{1,5},{3,7},{5,1},{7,3},{8,12},{10,14},{12... | collective-permute-start | bytes 3342344 | tf_op jit(solution)/shard_map/ppermute | solution.py:61
  559.8 127.0 %collective-permute-start.22 = (bf16[256,2176]{1,0:T(8,128)(2,1)}, bf16[256,2176]{1,0:T(8,128)(2,1)}, u32[]{:S(2)}, u32[]{:S(2)}) collective-permute-start(bf16[256,2176]{1,0:T(8,128)(2,1)} %get-tuple-element.48), channel_id=1, source_target_pairs={{0,2},{2,4},{4,6},{6,0},{1,3},{3,5},{5,7},{7,1},{8,10},{10,12},{12... | collective-permute-start | bytes 3342344 | tf_op jit(solution)/shard_map/ppermute | solution.py:61
  727.3 30.5 %all-to-all-start.6 = ((bf16[256,4,512]{2,0,1:T(8,128)(2,1)}), bf16[256,4,512]{2,0,1:T(8,128)(2,1)}, u32[]{:S(2)}, u32[]{:S(2)}) async-start(bf16[256,4,512]{2,0,1:T(8,128)(2,1)} %bitcast.250), calls=%async_computation.6 | async-start | bytes 2097152 | tf_op jit(solution)/shard_map/all_to_all | solution.py:893
  739.7 79.2 %collective-permute-start.24 = (bf16[256,2048]{1,0:T(8,128)(2,1)}, bf16[256,2048]{1,0:T(8,128)(2,1)}, u32[]{:S(2)}, u32[]{:S(2)}) collective-permute-start(bf16[256,2048]{1,0:T(8,128)(2,1)} %get-tuple-element.123), channel_id=1, source_target_pairs={{0,6},{2,0},{4,2},{6,4},{1,7},{3,1},{5,3},{7,5},{8,14},{10,8},{12,... | collective-permute-start | bytes 3145736 | tf_op jit(solution)/shard_map/ppermute | solution.py:61
  744.1 76.7 %collective-permute-start.26 = (bf16[256,2048]{1,0:T(8,128)(2,1)}, bf16[256,2048]{1,0:T(8,128)(2,1)}, u32[]{:S(2)}, u32[]{:S(2)}) collective-permute-start(bf16[256,2048]{1,0:T(8,128)(2,1)} %get-tuple-element.124), channel_id=1, source_target_pairs={{0,2},{2,4},{4,6},{6,0},{1,3},{3,5},{5,7},{7,1},{8,10},{10,12},{12... | collective-permute-start | bytes 3145736 | tf_op jit(solution)/shard_map/ppermute | solution.py:61
  744.1 90.2 %collective-permute-start.25 = (bf16[256,2048]{1,0:T(8,128)(2,1)}, bf16[256,2048]{1,0:T(8,128)(2,1)}, u32[]{:S(2)}, u32[]{:S(2)}) collective-permute-start(bf16[256,2048]{1,0:T(8,128)(2,1)} %get-tuple-element.125), channel_id=1, source_target_pairs={{0,4},{2,6},{4,0},{6,2},{1,5},{3,7},{5,1},{7,3},{8,12},{10,14},{12... | collective-permute-start | bytes 3145736 | tf_op jit(solution)/shard_map/ppermute | solution.py:61
  857.1 52.7 %all-to-all-start.8 = ((bf16[4,256,2048]{2,1,0:T(8,128)(2,1)}), bf16[4,256,2048]{2,1,0:T(8,128)(2,1)}, u32[]{:S(2)}, u32[]{:S(2)}) async-start(bf16[4,256,2048]{2,1,0:T(8,128)(2,1)} %bitcast.266), calls=%async_computation.8 | async-start | bytes 8388608 | tf_op jit(solution)/shard_map/all_to_all | solution.py:48
  863.9 65.7 %collective-permute-start.28 = (bf16[256,1664]{1,0:T(8,128)(2,1)}, bf16[256,1664]{1,0:T(8,128)(2,1)S(1)}, u32[]{:S(2)}, u32[]{:S(2)}) collective-permute-start(bf16[256,1664]{1,0:T(8,128)(2,1)} %get-tuple-element.126), channel_id=1, source_target_pairs={{0,6},{2,0},{4,2},{6,4},{1,7},{3,1},{5,3},{7,5},{8,14},{10,8},{12,... | collective-permute-start | bytes 2555912 | tf_op jit(solution)/shard_map/ppermute | solution.py:61
  864.5 65.1 %collective-permute-start.30 = (bf16[256,1664]{1,0:T(8,128)(2,1)}, bf16[256,1664]{1,0:T(8,128)(2,1)}, u32[]{:S(2)}, u32[]{:S(2)}) collective-permute-start(bf16[256,1664]{1,0:T(8,128)(2,1)} %get-tuple-element.127), channel_id=1, source_target_pairs={{0,2},{2,4},{4,6},{6,0},{1,3},{3,5},{5,7},{7,1},{8,10},{10,12},{12... | collective-permute-start | bytes 2555912 | tf_op jit(solution)/shard_map/ppermute | solution.py:61
  866.1 73.0 %collective-permute-start.29 = (bf16[256,1664]{1,0:T(8,128)(2,1)}, bf16[256,1664]{1,0:T(8,128)(2,1)}, u32[]{:S(2)}, u32[]{:S(2)}) collective-permute-start(bf16[256,1664]{1,0:T(8,128)(2,1)} %get-tuple-element.128), channel_id=1, source_target_pairs={{0,4},{2,6},{4,0},{6,2},{1,5},{3,7},{5,1},{7,3},{8,12},{10,14},{12... | collective-permute-start | bytes 2555912 | tf_op jit(solution)/shard_map/ppermute | solution.py:61
  (67 other events, 1228.6 us)
Sparse Core Ops, SparseCore 0:
  52.5 127.3 all-gather.4
  181.8 172.0 all-gather.2
  493.6 116.9 reduce-scatter.4
  614.0 216.9 reduce-scatter.2
